TPU v7x, 256 devices: a whole 4x4x8 slice. The times are simulated.
256 devices in a mesh: box: 64 (over x, z, core), src: 4 (over y).
Axes of the slice: x: 4, y: 4, z: 8, core: 2. Of those that a mesh axis runs over, the one named last changes fastest.
Arguments:
- source_field: bfloat16 [512, 524288], P('src', 'box'), parts along dimension 0, may hold values from -6 to 6
- project_mats: bfloat16 [4096, 128], P('box'), may hold values from -0.5 to 0.5
- local_mats: bfloat16 [8, 2, 4096, 64], P(None, None, 'box'), may hold values from -0.75 to 0.75
- cross_mats: bfloat16 [6, 2, 4096, 64], P(None, None, 'box'), may hold values from -0.75 to 0.75
- angles: bfloat16 [14, 524288], P(None, 'box'), may hold values from -3.140625 to 3.140625
- evaluate_mats: bfloat16 [8192, 64], P('box'), may hold values from -0.75 to 0.75
Outputs:
- image_blocks: bfloat16 [512, 524288], P('src', 'box'), parts along dimension 0
There are 4 independent parts, one for each index of `src`. A program takes and returns all parts, laid end to end along the dimension named above; an argument that names none is the same for every part. Nothing has to cross between parts.
All inputs are finite; a program needn't handle non-finite values.
Results may differ from a plain program's by a relative error of at most 0.024.
Values may be sent and summed in bfloat16 or wider, within the bound.
No kernel may reach another device: no remote copies, remote signals or barrier semaphores. Data moves between devices by JAX's collectives and lax.ppermute only.
A program may use at most 128 MiB of HBM per device.

v0:
```python
import jax
import jax.numpy as jnp
from jax import lax
from jax.sharding import PartitionSpec as P


def swapped(x, axis, distance):
    return lax.ppermute(x, axis, [(i, i ^ 1 << distance) for i in range(lax.axis_size(axis))])


def flip_last(values, pair_span):
    full_shape = values.shape
    leading = full_shape[:-1]
    reshaped = values.reshape(leading + (full_shape[-1] // (2 * pair_span), 2, pair_span))
    return jnp.flip(reshaped, axis=-2).reshape(full_shape)


def mix_local(matrices, current, partner, phase_row):
    own_term = jnp.dot(matrices[0], current, preferred_element_type=jnp.float32)
    partner_term = jnp.dot(matrices[1], partner, preferred_element_type=jnp.float32)
    return (jnp.cos(phase_row)[None] * own_term + jnp.sin(phase_row)[None] * partner_term).astype(
        jnp.bfloat16
    )


def shards(source_field, project_mats, local_mats, cross_mats, angles, evaluate_mats):
    box_count = lax.axis_size("box")
    local_boxes = source_field.shape[1]
    rank_dim = project_mats.shape[0]
    pixel_rows = evaluate_mats.shape[0]
    local_levels = local_mats.shape[0]
    cross_levels = cross_mats.shape[0]
    group_size = local_boxes // box_count
    local_bits = (local_boxes & -local_boxes).bit_length() - 1
    box_bits = box_count.bit_length() - 1
    phases = angles.astype(jnp.float32)
    current = jnp.dot(project_mats, source_field, preferred_element_type=jnp.float32).astype(
        jnp.bfloat16
    )
    for level_idx in range(local_levels):
        partner = flip_last(current, 1 << level_idx % local_bits)
        current = mix_local(local_mats[level_idx], current, partner, phases[level_idx])
    for level_idx in range(cross_levels):
        level_bit = (box_bits - 1 - level_idx) % box_bits
        partner = swapped(current, "box", level_bit)
        current = mix_local(
            cross_mats[level_idx], current, partner, phases[local_levels + level_idx]
        )
    shaped = current.reshape(rank_dim, box_count, group_size)
    pixels_out = jnp.einsum(
        "qr,rdt->qdt",
        evaluate_mats,
        lax.all_to_all(shaped, "box", split_axis=1, concat_axis=1, tiled=True),
        preferred_element_type=jnp.float32,
    )
    return pixels_out.reshape(pixel_rows, local_boxes).astype(jnp.bfloat16)


def solution(mesh):
    in_specs = (
        P("src", "box"),
        P("box", None),
        P(None, None, "box", None),
        P(None, None, "box", None),
        P(None, "box"),
        P("box", None),
    )
    out_specs = P("src", "box")
    return jax.shard_map(shards, mesh=mesh, in_specs=in_specs, out_specs=out_specs, check_vma=False)
```

profile of v0, /device:TPU:1, one launch (start us, length us, event | category | flops | bytes accessed | tf_op | source)
XLA Modules:
  0.0 332.9 jit_solution(7540862742128506790)
XLA Ops:
  1.1 8.4 %slice_cosine_fusion.13 = (f32[1,8192]{1,0:T(1,128)}, f32[1,8192]{1,0:T(1,128)}, f32[1,8192]{1,0:T(1,128)}, f32[1,8192]{1,0:T(1,128)}, f32[1,8192]{1,0:T(1,128)}...) fusion(f32[14,8192]{1,0:T(8,128)S(1)} %convert_element_type.99), kind=kLoop, calls=%fused_computation.87 | loop fusion | bytes 589824 | tf_op jit(solution)/shard_map/cos | solution.py:21
  9.5 13.0 %slice_sine_fusion.13 = (f32[1,8192]{1,0:T(1,128)}, f32[1,8192]{1,0:T(1,128)}, f32[1,8192]{1,0:T(1,128)}, f32[1,8192]{1,0:T(1,128)}, f32[1,8192]{1,0:T(1,128)}, ...) fusion(f32[14,8192]{1,0:T(8,128)S(1)} %convert_element_type.99), kind=kLoop, calls=%fused_computation.86 | loop fusion | bytes 1081344 | tf_op jit(solution)/shard_map/sin | solution.py:21
  23.0 1.8 copy.9
  24.8 17.7 %rev.32 = bf16[64,4096,2,1]{0,2,1,3:T(2,128)(2,1)S(1)} reverse(bf16[64,4096,2,1]{0,2,1,3:T(2,128)(2,1)} %bitcast.194), dimensions={2} | reverse | bytes 2097152 | tf_op jit(solution)/shard_map/jit(_flip)/rev | solution.py:15
  45.2 1.8 copy.10
  47.0 3.2 rev.33
  50.3 1.7 convolution_multiply_fusion.26
  53.1 1.8 copy.11
  54.9 2.4 rev.34
  58.6 1.8 copy.12
  60.4 2.0 rev.35
  64.0 1.8 copy.13
  65.7 2.0 rev.36
  69.0 1.8 copy.14
  70.8 2.0 rev.37
  74.5 3.3 reshape.121
  77.8 18.3 %rev.38 = bf16[64,64,2,64]{3,2,1,0:T(2,128)(2,1)S(1)} reverse(bf16[64,64,2,64]{3,2,1,0:T(2,128)(2,1)} %reshape.121), dimensions={2} | reverse | bytes 2097152 | tf_op jit(solution)/shard_map/jit(_flip)/rev | solution.py:15
  96.1 2.5 reshape.122
  101.5 5.2 %rev.39 = bf16[64,32,2,128]{3,2,1,0:T(2,128)(2,1)S(1)} reverse(bf16[64,32,2,128]{3,2,1,0:T(2,128)(2,1)S(1)} %reshape.123), dimensions={2} | reverse | bytes 2097152 | tf_op jit(solution)/shard_map/jit(_flip)/rev | solution.py:15
  108.7 3.7 %collective-permute-start = (bf16[64,8192]{1,0:T(8,128)(2,1)S(1)}, bf16[64,8192]{1,0:T(8,128)(2,1)S(1)}, u32[]{:S(2)}, u32[]{:S(2)}) collective-permute-start(bf16[64,8192]{1,0:T(8,128)(2,1)S(1)} %bitcast.201), channel_id=1, source_target_pairs={{0,128},{4,132},{8,136},{12,140},{16,144},{20,148},{24,152},{28,15... | collective-permute-start | bytes 3145736 | tf_op jit(solution)/shard_map/ppermute | solution.py:8
  112.8 21.4 %collective-permute-done = bf16[64,8192]{1,0:T(8,128)(2,1)S(1)} collective-permute-done((bf16[64,8192]{1,0:T(8,128)(2,1)S(1)}, bf16[64,8192]{1,0:T(8,128)(2,1)S(1)}, u32[]{:S(2)}, u32[]{:S(2)}) %collective-permute-start) | collective-permute-done | bytes 1048608 | tf_op jit(solution)/shard_map/ppermute | solution.py:8
  134.6 2.3 collective-permute-start.1
  137.3 21.2 %collective-permute-done.1 = bf16[64,8192]{1,0:T(8,128)(2,1)S(1)} collective-permute-done((bf16[64,8192]{1,0:T(8,128)(2,1)S(1)}, bf16[64,8192]{1,0:T(8,128)(2,1)S(1)}, u32[]{:S(2)}, u32[]{:S(2)}) %collective-permute-start.1) | collective-permute-done | bytes 1048608 | tf_op jit(solution)/shard_map/ppermute | solution.py:8
  159.0 7.2 %collective-permute-start.2 = (bf16[64,8192]{1,0:T(8,128)(2,1)S(1)}, bf16[64,8192]{1,0:T(8,128)(2,1)S(1)}, u32[]{:S(2)}, u32[]{:S(2)}) collective-permute-start(bf16[64,8192]{1,0:T(8,128)(2,1)S(1)} %bitcast.203), channel_id=1, source_target_pairs={{0,32},{4,36},{8,40},{12,44},{16,48},{20,52},{24,56},{28,60},{32,0... | collective-permute-start | bytes 3145736 | tf_op jit(solution)/shard_map/ppermute | solution.py:8
  166.6 25.2 %collective-permute-done.2 = bf16[64,8192]{1,0:T(8,128)(2,1)S(1)} collective-permute-done((bf16[64,8192]{1,0:T(8,128)(2,1)S(1)}, bf16[64,8192]{1,0:T(8,128)(2,1)S(1)}, u32[]{:S(2)}, u32[]{:S(2)}) %collective-permute-start.2) | collective-permute-done | bytes 1048608 | tf_op jit(solution)/shard_map/ppermute | solution.py:8
  192.2 21.4 %collective-permute-start.3 = (bf16[64,8192]{1,0:T(8,128)(2,1)S(1)}, bf16[64,8192]{1,0:T(8,128)(2,1)S(1)}, u32[]{:S(2)}, u32[]{:S(2)}) collective-permute-start(bf16[64,8192]{1,0:T(8,128)(2,1)S(1)} %bitcast.204), channel_id=1, source_target_pairs={{0,16},{4,20},{8,24},{12,28},{16,0},{20,4},{24,8},{28,12},{32,48},... | collective-permute-start | bytes 3145736 | tf_op jit(solution)/shard_map/ppermute | solution.py:8
  214.0 45.7 %collective-permute-done.3 = bf16[64,8192]{1,0:T(8,128)(2,1)S(1)} collective-permute-done((bf16[64,8192]{1,0:T(8,128)(2,1)S(1)}, bf16[64,8192]{1,0:T(8,128)(2,1)S(1)}, u32[]{:S(2)}, u32[]{:S(2)}) %collective-permute-start.3) | collective-permute-done | bytes 1048608 | tf_op jit(solution)/shard_map/ppermute | solution.py:8
  260.9 23.8 %collective-permute-done.4 = bf16[64,8192]{1,0:T(8,128)(2,1)S(1)} collective-permute-done((bf16[64,8192]{1,0:T(8,128)(2,1)S(1)}, bf16[64,8192]{1,0:T(8,128)(2,1)S(1)}, u32[]{:S(2)}, u32[]{:S(2)}) %collective-permute-start.4) | collective-permute-done | bytes 1048608 | tf_op jit(solution)/shard_map/ppermute | solution.py:8
  287.0 1.9 collective-permute-done.5
  289.6 37.0 %all_to_all.5 = bf16[64,64,128]{2,0,1:T(8,128)(2,1)S(1)} all-to-all(bf16[64,64,128]{2,0,1:T(8,128)(2,1)S(1)} %bitcast.206), channel_id=1, replica_groups=mesh['box'=64,'src'=4] {'box'}, dimensions={1} | all-to-all | bytes 2097152 | tf_op jit(solution)/shard_map/all_to_all | solution.py:53
  326.6 2.1 convolution_convert_fusion.1
  328.7 4.2 %copy.16 = bf16[128,8192]{1,0:T(8,128)(2,1)} copy(bf16[128,8192]{0,1:T(8,128)(2,1)} %bitcast.193) | data formatting | bytes 4194304 | tf_op jit(solution)/shard_map/convert_element_type | solution.py:56
  (98 shorter events, 23.3 us)
Async XLA Ops:
  0.0 22.6 %copy-start = (bf16[128,8192]{1,0:T(8,128)(2,1)S(1)}, bf16[128,8192]{1,0:T(8,128)(2,1)}, u32[]{:S(2)}) copy-start(bf16[128,8192]{1,0:T(8,128)(2,1)} %param.6) | copy-start | bytes 6291460
  0.0 22.6 %copy-start.30 = (bf16[64,128]{1,0:T(8,128)(2,1)S(1)}, bf16[64,128]{1,0:T(8,128)(2,1)}, u32[]{:S(2)}) copy-start(bf16[64,128]{1,0:T(8,128)(2,1)} %param.7) | copy-start | bytes 49156
  45.2 1.8 copy-start.2
  50.3 1.7 copy-start.3
  54.9 2.4 copy-start.8
  58.5 1.8 copy-start.4
  62.3 1.2 copy-start.5
  69.0 1.8 copy-start.6
  72.8 1.2 copy-start.7
  96.1 2.5 copy-start.26
  98.5 1.7 copy-start.23
  101.4 6.1 %copy-start.25 = (f32[1,8192]{1,0:T(1,128)S(1)}, f32[1,8192]{1,0:T(1,128)}, u32[]{:S(2)}) copy-start(f32[1,8192]{1,0:T(1,128)} %get-tuple-element.11) | copy-start | bytes 98308
  108.2 4.1 %copy-start.9 = (bf16[6,2,64,64]{3,2,1,0:T(8,128)(2,1)S(1)}, bf16[6,2,64,64]{3,2,1,0:T(8,128)(2,1)}, u32[]{:S(2)}) copy-start(bf16[6,2,64,64]{3,2,1,0:T(8,128)(2,1)} %param.9) | copy-start | bytes 294916
  108.2 4.1 %copy-start.19 = (f32[1,8192]{1,0:T(1,128)S(1)}, f32[1,8192]{1,0:T(1,128)}, u32[]{:S(2)}) copy-start(f32[1,8192]{1,0:T(1,128)} %get-tuple-element.28) | copy-start | bytes 98308
  108.7 25.5 %copy-start.22 = (f32[1,8192]{1,0:T(1,128)S(1)}, f32[1,8192]{1,0:T(1,128)}, u32[]{:S(2)}) copy-start(f32[1,8192]{1,0:T(1,128)} %get-tuple-element.10) | copy-start | bytes 98308
  108.7 25.5 %collective-permute-start = (bf16[64,8192]{1,0:T(8,128)(2,1)S(1)}, bf16[64,8192]{1,0:T(8,128)(2,1)S(1)}, u32[]{:S(2)}, u32[]{:S(2)}) collective-permute-start(bf16[64,8192]{1,0:T(8,128)(2,1)S(1)} %bitcast.201), channel_id=1, source_target_pairs={{0,128},{4,132},{8,136},{12,140},{16,144},{20,148},{24,152},{28,15... | collective-permute-start | bytes 3145736 | tf_op jit(solution)/shard_map/ppermute | solution.py:8
  134.2 2.7 copy-start.17
  134.6 23.9 %copy-start.20 = (f32[1,8192]{1,0:T(1,128)S(1)}, f32[1,8192]{1,0:T(1,128)}, u32[]{:S(2)}) copy-start(f32[1,8192]{1,0:T(1,128)} %get-tuple-element.9) | copy-start | bytes 98308
  134.6 23.9 %collective-permute-start.1 = (bf16[64,8192]{1,0:T(8,128)(2,1)S(1)}, bf16[64,8192]{1,0:T(8,128)(2,1)S(1)}, u32[]{:S(2)}, u32[]{:S(2)}) collective-permute-start(bf16[64,8192]{1,0:T(8,128)(2,1)S(1)} %bitcast.202), channel_id=1, source_target_pairs={{0,64},{4,68},{8,72},{12,76},{16,80},{20,84},{24,88},{28,92},{32,9... | collective-permute-start | bytes 3145736 | tf_op jit(solution)/shard_map/ppermute | solution.py:8
  158.5 7.7 %copy-start.15 = (f32[1,8192]{1,0:T(1,128)S(1)}, f32[1,8192]{1,0:T(1,128)}, u32[]{:S(2)}) copy-start(f32[1,8192]{1,0:T(1,128)} %get-tuple-element.30) | copy-start | bytes 98308
  159.0 32.8 %copy-start.18 = (f32[1,8192]{1,0:T(1,128)S(1)}, f32[1,8192]{1,0:T(1,128)}, u32[]{:S(2)}) copy-start(f32[1,8192]{1,0:T(1,128)} %get-tuple-element.8) | copy-start | bytes 98308
  159.0 32.8 %collective-permute-start.2 = (bf16[64,8192]{1,0:T(8,128)(2,1)S(1)}, bf16[64,8192]{1,0:T(8,128)(2,1)S(1)}, u32[]{:S(2)}, u32[]{:S(2)}) collective-permute-start(bf16[64,8192]{1,0:T(8,128)(2,1)S(1)} %bitcast.203), channel_id=1, source_target_pairs={{0,32},{4,36},{8,40},{12,44},{16,48},{20,52},{24,56},{28,60},{32,0... | collective-permute-start | bytes 3145736 | tf_op jit(solution)/shard_map/ppermute | solution.py:8
  191.8 21.8 %copy-start.13 = (f32[1,8192]{1,0:T(1,128)S(1)}, f32[1,8192]{1,0:T(1,128)}, u32[]{:S(2)}) copy-start(f32[1,8192]{1,0:T(1,128)} %get-tuple-element.31) | copy-start | bytes 98308
  192.2 67.5 %copy-start.16 = (f32[1,8192]{1,0:T(1,128)S(1)}, f32[1,8192]{1,0:T(1,128)}, u32[]{:S(2)}) copy-start(f32[1,8192]{1,0:T(1,128)} %get-tuple-element.7) | copy-start | bytes 98308
  192.2 67.4 %collective-permute-start.3 = (bf16[64,8192]{1,0:T(8,128)(2,1)S(1)}, bf16[64,8192]{1,0:T(8,128)(2,1)S(1)}, u32[]{:S(2)}, u32[]{:S(2)}) collective-permute-start(bf16[64,8192]{1,0:T(8,128)(2,1)S(1)} %bitcast.204), channel_id=1, source_target_pairs={{0,16},{4,20},{8,24},{12,28},{16,0},{20,4},{24,8},{28,12},{32,48},... | collective-permute-start | bytes 3145736 | tf_op jit(solution)/shard_map/ppermute | solution.py:8
  260.1 24.6 %copy-start.14 = (f32[1,8192]{1,0:T(1,128)S(1)}, f32[1,8192]{1,0:T(1,128)}, u32[]{:S(2)}) copy-start(f32[1,8192]{1,0:T(1,128)} %get-tuple-element.6) | copy-start | bytes 98308
  260.1 24.5 %collective-permute-start.4 = (bf16[64,8192]{1,0:T(8,128)(2,1)S(1)}, bf16[64,8192]{1,0:T(8,128)(2,1)S(1)}, u32[]{:S(2)}, u32[]{:S(2)}) collective-permute-start(bf16[64,8192]{1,0:T(8,128)(2,1)S(1)} %bitcast.205), channel_id=1, source_target_pairs={{0,8},{4,12},{8,0},{12,4},{16,24},{20,28},{24,16},{28,20},{32,40},... | collective-permute-start | bytes 3145736 | tf_op jit(solution)/shard_map/ppermute | solution.py:8
  284.7 1.9 copy-start.10
  285.1 3.7 %copy-start.12 = (f32[1,8192]{1,0:T(1,128)S(1)}, f32[1,8192]{1,0:T(1,128)}, u32[]{:S(2)}) copy-start(f32[1,8192]{1,0:T(1,128)} %get-tuple-element.5) | copy-start | bytes 98308
  285.1 3.7 %collective-permute-start.5 = (bf16[64,8192]{1,0:T(8,128)(2,1)S(1)}, bf16[64,8192]{1,0:T(8,128)(2,1)S(1)}, u32[]{:S(2)}, u32[]{:S(2)}) collective-permute-start(bf16[64,8192]{1,0:T(8,128)(2,1)S(1)} %bitcast.200), channel_id=1, source_target_pairs={{0,4},{4,0},{8,12},{12,8},{16,20},{20,16},{24,28},{28,24},{32,36},... | collective-permute-start | bytes 3145736 | tf_op jit(solution)/shard_map/ppermute | solution.py:8
  289.3 37.3 %copy-start.31 = (bf16[128,64]{0,1:T(8,128)(2,1)S(1)}, bf16[128,64]{0,1:T(8,128)(2,1)}, u32[]{:S(2)}) copy-start(bf16[128,64]{0,1:T(8,128)(2,1)} %param.11) | copy-start | bytes 49156
  328.7 4.2 %copy-start.1 = (bf16[128,8192]{1,0:T(8,128)(2,1)S(1)}, bf16[128,8192]{1,0:T(8,128)(2,1)}, u32[]{:S(2)}) copy-start(bf16[128,8192]{1,0:T(8,128)(2,1)} %param.6) | copy-start | bytes 6291460
  (6 other events, 5.7 us)
where the time goes:
time: 336 us; the launch traced here: 333 us
  waiting for transfers between devices  139 us (41%)
  local copies, waits for them, and re-layouts  97.8 us (29%)
  blocking collectives  37 us (11%)
  starting transfers between devices  36.3 us (11%)
  matrix products  21.1 us (6%)
    ppermute x6, waiting for transfers between devices, swapped(): lax.ppermute(x, axis, [(i, i ^ 1 << distance) for i in range(lax.axis_siz...  139 us
    rev x8, local copies, waits for them, and re-layouts, flip_last(): return jnp.flip(reshaped, axis=-2).reshape(full_shape)  52.7 us
    all_to_all x1, blocking collectives, shards(): lax.all_to_all(shaped, 'box', split_axis=1, concat_axis=1, tiled=True)  37 us
    ppermute x6, starting transfers between devices, swapped(): lax.ppermute(x, axis, [(i, i ^ 1 << distance) for i in range(lax.axis_siz...  36.3 us
    sin x1, local copies, waits for them, and re-layouts, mix_local(): jnp.sin(phase_row)[None] * partner_term  13 us
    dot_general x14, matrix products, mix_local(): jnp.dot(matrices[1], partner, preferred_element_type=jnp.float32)  11.2 us
    convert_element_type x5, local copies, waits for them, and re-layouts, mix_local(): (jnp.cos(phase_row)[None] * own_term + jnp.sin(phase_row)[None] * partner...  8.91 us
    cos x1, local copies, waits for them, and re-layouts, mix_local(): jnp.cos(phase_row)[None] * own_term  8.39 us
  transfers between devices with their start and end apart: 6, of which 6 were waited for; matrix products, arithmetic and copies ran while one was open for 1% of the time, Pallas kernels for 0%

commit v1 on v0

v1 whole, which is shorter than its diff:
```python
import jax
import jax.numpy as jnp
from jax import lax
from jax.experimental import pallas as pl
from jax.experimental.pallas import tpu as pltpu
from jax.sharding import PartitionSpec as P

R = 64
TILE = 256
BF = jnp.bfloat16
F32 = jnp.float32

NX, NZ, NC = 4, 8, 2


def dot(a, b):
    return jnp.dot(a, b, preferred_element_type=F32)


def cos_sin(t):
    h = 0.5 * t
    q = h * h
    s = 1.0 + q * (
        -1.0 / 6 + q * (1.0 / 120 + q * (-1.0 / 5040 + q * (1.0 / 362880 + q * (-1.0 / 39916800 + q * (1.0 / 6227020800)))))
    )
    s = s * h
    c = 1.0 + q * (
        -0.5 + q * (1.0 / 24 + q * (-1.0 / 720 + q * (1.0 / 40320 + q * (-1.0 / 3628800 + q * (1.0 / 479001600)))))
    )
    return 1.0 - 2.0 * s * s, 2.0 * s * c


def mix(mat, own, partner, c, s):
    return dot(mat, jnp.concatenate([own * c, partner * s], axis=0)).astype(BF)


def row(values, i):
    return values[i : i + 1].astype(BF)


def local_kernel(block_ref, src_ref, ang_ref, proj_ref, mats_ref, out_ref):
    tiles = src_ref.shape[1] // TILE
    levels = mats_ref.shape[0]
    ang = ang_ref[...].astype(F32)
    cos, sin = cos_sin(ang[:levels])
    proj = proj_ref[...]
    x = [dot(proj, src_ref[:, i * TILE : (i + 1) * TILE]).astype(BF) for i in range(tiles)]
    to = lax.broadcasted_iota(jnp.int32, (TILE, TILE), 1)
    frm = lax.broadcasted_iota(jnp.int32, (TILE, TILE), 0)
    for level in range(levels):
        span = 1 << level
        if span == 128:
            xp = [jnp.concatenate([v[:, 128:], v[:, :128]], axis=1) for v in x]
        else:
            perm = jnp.where(frm == (to ^ span), 1.0, 0.0).astype(BF)
            every = dot(jnp.concatenate(x, axis=0), perm).astype(BF)
            xp = [every[i * R : (i + 1) * R] for i in range(tiles)]
        mat = jnp.concatenate([mats_ref[level, 0], mats_ref[level, 1]], axis=1)
        c, s = row(cos, level), row(sin, level)
        x = [
            mix(mat, x[i], xp[i], c[:, i * TILE : (i + 1) * TILE], s[:, i * TILE : (i + 1) * TILE])
            for i in range(tiles)
        ]
    for i in range(tiles):
        out_ref[0, i * R : (i + 1) * R] = x[i]
    a = jnp.concatenate(
        [ang[levels + 2 : levels + 6], ang[levels : levels + 2], jnp.zeros((2, ang.shape[1]), F32)], axis=0
    )
    a = jnp.concatenate([a[:, i * TILE : (i + 1) * TILE] for i in range(tiles)], axis=0)
    out_ref[0, tiles * R : tiles * R + tiles * 8] = a.astype(BF)


def local_levels(blocks, source_field, angles, project_mats, local_mats):
    n = blocks.shape[0]
    q, columns = source_field.shape
    width = columns // NX
    rows = NZ * R + NZ * 8
    return pl.pallas_call(
        local_kernel,
        grid_spec=pltpu.PrefetchScalarGridSpec(
            num_scalar_prefetch=1,
            grid=(n,),
            in_specs=[
                pl.BlockSpec((q, width), lambda i, b: (0, b[i])),
                pl.BlockSpec((angles.shape[0], width), lambda i, b: (0, b[i])),
                pl.BlockSpec(project_mats.shape, lambda i, b: (0, 0)),
                pl.BlockSpec(local_mats.shape, lambda i, b: (0, 0, 0, 0)),
            ],
            out_specs=pl.BlockSpec((1, rows, TILE), lambda i, b: (i, 0, 0)),
        ),
        out_shape=jax.ShapeDtypeStruct((n, rows, TILE), BF),
        compiler_params=pltpu.CompilerParams(vmem_limit_bytes=48 * 2**20),
    )(blocks, source_field, angles, project_mats, local_mats)


def x_kernel(*refs):
    data, angs, mats, out_ref = refs[:4], refs[4:8], refs[8:12], refs[12]
    tiles = data[0].shape[1] // R
    phases = [a[0].astype(F32) for a in angs]
    for i in range(tiles):
        x = [d[0, i * R : (i + 1) * R] for d in data]
        t = [angs_rows(p, i) for p in phases]
        cs = [cos_sin(v) for v in t]
        for level, bit in ((0, 2), (1, 1)):
            x = [
                mix(mats[j][level], x[j], x[j ^ bit], row(cs[j][0], 4 + level), row(cs[j][1], 4 + level))
                for j in range(4)
            ]
        for j in range(4):
            out_ref[i, j * R : (j + 1) * R] = x[j]
        out_ref[i, 4 * R :] = jnp.concatenate([v[:4] for v in t], axis=0).astype(BF)


def angs_rows(phases, i):
    return phases[i * 8 : (i + 1) * 8]


def x_levels(messages, mats):
    rows = 4 * R + 16
    specs = [pl.BlockSpec((1, NZ * R, TILE), lambda i: (0, 0, 0)) for _ in messages]
    ang_specs = [pl.BlockSpec((1, NZ * 8, TILE), lambda i: (0, 8, 0)) for _ in messages]
    mat_specs = [pl.BlockSpec((2, R, 2 * R), lambda i: (0, 0, 0)) for _ in mats]
    return pl.pallas_call(
        x_kernel,
        grid=(1,),
        in_specs=specs + ang_specs + mat_specs,
        out_specs=pl.BlockSpec((NZ, rows, TILE), lambda i: (0, 0, 0)),
        out_shape=jax.ShapeDtypeStruct((NZ, rows, TILE), BF),
        compiler_params=pltpu.CompilerParams(vmem_limit_bytes=48 * 2**20),
    )(*messages, *messages, *mats)


def z_kernel(core_ref, data_ref, ang_ref, mats_ref, keep_ref, send_ref):
    j = pl.program_id(0)
    low = core_ref[0] == 0
    x = [data_ref[k] for k in range(NZ)]
    cs = []
    for k in range(NZ):
        cs.append(cos_sin(ang_ref[k, pl.ds(0, 16)].astype(F32)))
    def pick(v):
        out = v[0:4]
        for n in range(1, 4):
            out = jnp.where(j == n, v[4 * n : 4 * n + 4], out)
        return out

    cs = [(pick(c), pick(s)) for c, s in cs]
    for level, bit in ((0, 4), (1, 2), (2, 1)):
        x = [
            mix(mats_ref[k, 0, level], x[k], x[k ^ bit], row(cs[k][0], level), row(cs[k][1], level))
            for k in range(NZ)
        ]
    for k in range(NZ):
        at = pl.ds(pl.multiple_of(j * (NZ * R) + k * R, R), R)
        lo, hi = x[k][:, :128], x[k][:, 128:]
        keep_ref[at] = jnp.where(low, lo, hi)
        send_ref[at] = jnp.where(low, hi, lo)

    @pl.when(j == 0)
    def _():
        for k in range(NZ):
            at = pl.ds(4 * NZ * R + k * 16, 16)
            a = ang_ref[k]
            lo, hi = a[:, :128], a[:, 128:]
            keep_ref[at] = jnp.where(low, lo, hi)
            send_ref[at] = jnp.where(low, hi, lo)


def z_levels(core, moved, mats):
    rows = 4 * NZ * R + NZ * 16
    out = jax.ShapeDtypeStruct((rows, 128), BF)
    return pl.pallas_call(
        z_kernel,
        grid_spec=pltpu.PrefetchScalarGridSpec(
            num_scalar_prefetch=1,
            grid=(4,),
            in_specs=[
                pl.BlockSpec((NZ, R, TILE), lambda j, c: (0, j, 0)),
                pl.BlockSpec((NZ, 16, TILE), lambda j, c: (0, 16, 0)),
                pl.BlockSpec((NZ, 1, 4, R, 2 * R), lambda j, c: (0, j, 0, 0, 0)),
            ],
            out_specs=[pl.BlockSpec((rows, 128), lambda j, c: (0, 0))] * 2,
        ),
        out_shape=[out, out],
        compiler_params=pltpu.CompilerParams(vmem_limit_bytes=48 * 2**20),
    )(core, moved, moved, mats)


def last_kernel(where_ref, own_ref, oth_ref, own_ang_ref, oth_ang_ref, own_mats_ref, oth_mats_ref, eval_ref, out_ref):
    j = pl.program_id(0)
    low = where_ref[4] == 0
    ev = eval_ref[...]

    def phases(ref, k):
        v = ref[pl.ds(k * 16, 16)].astype(F32)
        out = v[3:4]
        for n in range(1, 4):
            out = jnp.where(j == n, v[4 * n + 3 : 4 * n + 4], out)
        return out

    own_c, own_s = cos_sin(jnp.concatenate([phases(own_ang_ref, k) for k in range(NZ)], axis=0))
    oth_c, oth_s = cos_sin(jnp.concatenate([phases(oth_ang_ref, k) for k in range(NZ)], axis=0))
    for k in range(NZ):
        own = own_ref[k * R : (k + 1) * R]
        oth = oth_ref[k * R : (k + 1) * R]
        y_own = mix(own_mats_ref[k, 0, 0], own, oth, row(own_c, k), row(own_s, k))
        y_oth = mix(oth_mats_ref[k, 0], oth, own, row(oth_c, k), row(oth_s, k))
        y = jnp.concatenate([jnp.where(low, y_own, y_oth), jnp.where(low, y_oth, y_own)], axis=1)
        out_ref[:, k * TILE : (k + 1) * TILE] = dot(ev, y).astype(BF)


def last_level(where, keep, received, mats, other_mats, evaluate_mats):
    q = evaluate_mats.shape[0]
    columns = 64 * 128
    return pl.pallas_call(
        last_kernel,
        grid_spec=pltpu.PrefetchScalarGridSpec(
            num_scalar_prefetch=1,
            grid=(4,),
            in_specs=[
                pl.BlockSpec((NZ * R, 128), lambda j, w: (j, 0)),
                pl.BlockSpec((NZ * R, 128), lambda j, w: (j, 0)),
                pl.BlockSpec((NZ * 16, 128), lambda j, w: (16, 0)),
                pl.BlockSpec((NZ * 16, 128), lambda j, w: (16, 0)),
                pl.BlockSpec((NZ, 1, 1, R, 2 * R), lambda j, w: (0, j, 3, 0, 0)),
                pl.BlockSpec((NZ, 1, R, 2 * R), lambda j, w: (0, j, 0, 0)),
                pl.BlockSpec(evaluate_mats.shape, lambda j, w: (0, 0)),
            ],
            out_specs=pl.BlockSpec((q, columns // 4), lambda j, w: (0, w[j])),
        ),
        out_shape=jax.ShapeDtypeStruct((q, columns), BF),
        compiler_params=pltpu.CompilerParams(vmem_limit_bytes=48 * 2**20),
    )(where, keep, received, keep, received, mats, other_mats, evaluate_mats)


def shards(source_field, project_mats, local_mats, cross_mats, angles, evaluate_mats):
    box = lax.axis_index("box")
    x, core = box // (NZ * NC), box % NC
    count = NX * NZ * NC

    def along_x(values, j):
        return lax.ppermute(values, "box", [(i, i ^ (j * NZ * NC)) for i in range(count)])

    def across(values):
        return lax.ppermute(values, "box", [(i, i ^ 1) for i in range(count)])

    z_groups = [[xx * NZ * NC + z * NC + c for z in range(NZ)] for xx in range(NX) for c in range(NC)]

    own_mats = jnp.concatenate([cross_mats[:, 0], cross_mats[:, 1]], axis=-1)
    slot_mats = [own_mats] + [along_x(own_mats, j) for j in (1, 2, 3)]
    gathered = lax.all_gather(jnp.stack([m[2:] for m in slot_mats]), "box", axis=0, axis_index_groups=z_groups)

    def local(*slots):
        blocks = jnp.stack([x ^ j for j in slots]).astype(jnp.int32)
        return local_levels(blocks, source_field, angles, project_mats, local_mats)

    m2 = along_x(local(2), 2)
    m1 = along_x(local(1), 1)
    m3 = along_x(local(3), 3)
    m0 = local(0)
    sent = x_levels([m0, m1, m2, m3], slot_mats)
    moved = lax.all_to_all(sent, "box", 0, 0, tiled=True, axis_index_groups=z_groups)
    keep, send = z_levels(core[None].astype(jnp.int32), moved, gathered)
    other_mats = across(gathered[:, :, 3])
    received = across(send)
    where = jnp.stack([x, x ^ 1, x ^ 2, x ^ 3, core]).astype(jnp.int32)
    return last_level(where, keep, received, gathered, other_mats, evaluate_mats)


def solution(mesh):
    in_specs = (
        P("src", "box"),
        P("box", None),
        P(None, None, "box", None),
        P(None, None, "box", None),
        P(None, "box"),
        P("box", None),
    )
    out_specs = P("src", "box")
    return jax.shard_map(shards, mesh=mesh, in_specs=in_specs, out_specs=out_specs, check_vma=False)
```

time: 336 us -> 107 us (0.32)
  waiting for transfers between devices: 139 us -> 45.7 us
  local copies, waits for them, and re-layouts: 97.8 us -> 5.89 us
  blocking collectives: 37 us -> 0 us
  Pallas kernels: 0 us -> 22.5 us
  matrix products: 21.1 us -> 0 us
  starting transfers between devices: 36.3 us -> 17.9 us
  between operations: 0.53 us -> 13.5 us
    ppermute x6 -> x8, waiting for transfers between devices: 139 us -> 17.4 us  [the longest x6 15.4 us: along_x(): lax.ppermute(values, 'box', [(i, i ^ j * NZ * NC) for i in range(count)])]
    rev x8 -> x0, local copies, waits for them, and re-layouts: 52.7 us -> none  [flip_last(): return jnp.flip(reshaped, axis=-2).reshape(full_shape)]
    all_to_all x1 -> x0, blocking collectives: 37 us -> none  [shards(): lax.all_to_all(shaped, 'box', split_axis=1, concat_axis=1, tiled=True)]
    all_to_all x0 -> x1, waiting for transfers between devices: none -> 28.3 us  [shards(): lax.all_to_all(sent, 'box', 0, 0, tiled=True, axis_index_groups=z_groups)]
    ppermute x6 -> x8, starting transfers between devices: 36.3 us -> 9.47 us  [the longest x6 8.2 us: along_x(): lax.ppermute(values, 'box', [(i, i ^ j * NZ * NC) for i in range(count)])]
    pallas_call x0 -> x7, Pallas kernels: none -> 22.5 us  [the longest x4 10.1 us: local_levels(): pl.pallas_call(local_kernel, grid_spec=pltpu.PrefetchScalarGridSpec(num_s...]
    dot_general x30 -> x0, matrix products: 21.1 us -> none  [the longest x14 11.2 us: mix_local(): jnp.dot(matrices[1], partner, preferred_element_type=jnp.float32)]
    convert_element_type x7 -> x0, local copies, waits for them, and re-layouts: 14.9 us -> none  [the longest x5 8.91 us: mix_local(): (jnp.cos(phase_row)[None] * own_term + jnp.sin(phase_row)[None] * partner...]
  transfers between devices with their start and end apart: 6 -> 10, of which waited for: 6 -> 6; matrix products, arithmetic and copies ran while one was open for 1% -> 1% of each run, Pallas kernels for 0% -> 12%
where the time goes in v1:
time: 107 us; the launch traced here: 106 us
  waiting for transfers between devices  45.7 us (43%)
  Pallas kernels  22.5 us (21%)
  starting transfers between devices  17.9 us (17%)
  between operations  13.5 us (13%)
  local copies, waits for them, and re-layouts  5.89 us (6%)
    all_to_all x1, waiting for transfers between devices, shards(): lax.all_to_all(sent, 'box', 0, 0, tiled=True, axis_index_groups=z_groups)  28.3 us
    ppermute x6, waiting for transfers between devices, along_x(): lax.ppermute(values, 'box', [(i, i ^ j * NZ * NC) for i in range(count)])  15.4 us
    pallas_call x4, Pallas kernels, local_levels(): pl.pallas_call(local_kernel, grid_spec=pltpu.PrefetchScalarGridSpec(num_s...  10.1 us
    all_to_all x1, starting transfers between devices, shards(): lax.all_to_all(sent, 'box', 0, 0, tiled=True, axis_index_groups=z_groups)  8.4 us
    ppermute x6, starting transfers between devices, along_x(): lax.ppermute(values, 'box', [(i, i ^ j * NZ * NC) for i in range(count)])  8.2 us
    pallas_call x1, Pallas kernels, last_level(): pl.pallas_call(last_kernel, grid_spec=pltpu.PrefetchScalarGridSpec(num_sc...  5.57 us
    pallas_call x1, Pallas kernels, z_levels(): pl.pallas_call(z_kernel, grid_spec=pltpu.PrefetchScalarGridSpec(num_scala...  4.08 us
    unnamed x23, local copies, waits for them, and re-layouts  3.63 us
  transfers between devices with their start and end apart: 10, of which 6 were waited for; matrix products, arithmetic and copies ran while one was open for 1% of the time, Pallas kernels for 12%

profile of v1, /device:TPU:1, one launch (start us, length us, event | category | flops | bytes accessed | tf_op | source)
XLA Modules:
  0.0 106.4 jit_solution(17137104820614418462)
XLA Ops:
  6.5 1.1 %slice_bitcast_fusion.2 = (bf16[6,64,64]{2,1,0:T(8,128)(2,1)S(1)}, bf16[6,64,64]{2,1,0:T(8,128)(2,1)S(1)}) fusion(bf16[6,2,64,64]{3,2,1,0:T(8,128)(2,1)} %param.9), kind=kLoop, calls=%fused_computation.3 | loop fusion | bytes 196608 | tf_op jit(solution)/shard_map/squeeze | solution.py:248
  7.6 0.1 pad_maximum_fusion.1.refs_8_
  7.8 3.4 %collective-permute-start.5 = (bf16[6,64,128]{2,1,0:T(8,128)(2,1)S(1)}, bf16[6,64,128]{2,1,0:T(8,128)(2,1)S(1)}, u32[]{:S(2)}, u32[]{:S(2)}) collective-permute-start(bf16[6,64,128]{2,1,0:T(8,128)(2,1)S(1)} %pad_maximum_fusion.1.refs_8_), channel_id=1, source_target_pairs={{0,192},{4,196},{8,200},{12,204},{16,208},{20,212},{24,216},{28,22... | collective-permute-start | bytes 294920 | tf_op jit(solution)/shard_map/ppermute | solution.py:241
  11.2 0.5 collective-permute-start.4
  11.7 0.2 collective-permute-start.3
  11.8 0.1 fusion.1
  11.9 2.2 %collective-permute-done.5.refs_11_ = bf16[6,64,128]{2,1,0:T(8,128)(2,1)S(1)} collective-permute-done((bf16[6,64,128]{2,1,0:T(8,128)(2,1)S(1)}, bf16[6,64,128]{2,1,0:T(8,128)(2,1)S(1)}, u32[]{:S(2)}, u32[]{:S(2)}) %collective-permute-start.5) | collective-permute-done | bytes 98336 | tf_op jit(solution)/shard_map/ppermute | solution.py:241
  14.2 2.1 %collective-permute-done.4.refs_10_ = bf16[6,64,128]{2,1,0:T(8,128)(2,1)S(1)} collective-permute-done((bf16[6,64,128]{2,1,0:T(8,128)(2,1)S(1)}, bf16[6,64,128]{2,1,0:T(8,128)(2,1)S(1)}, u32[]{:S(2)}, u32[]{:S(2)}) %collective-permute-start.4) | collective-permute-done | bytes 98336 | tf_op jit(solution)/shard_map/ppermute | solution.py:241
  16.3 0.7 pad_maximum_fusion
  17.1 0.9 copy-done.3
  18.0 0.9 copy-done.5
  19.0 2.9 %shard_map.65 = bf16[1,576,256]{2,1,0:T(8,128)(2,1)} custom-call(s32[1]{0:T(128)} %bitcast.1.block_ref, bf16[128,8192]{1,0:T(8,128)(2,1)S(1)} %copy-done, bf16[14,8192]{1,0:T(8,128)(2,1)S(1)} %copy-done.3, bf16[64,128]{1,0:T(8,128)(2,1)S(1)} %copy-done.9, bf16[8,2,64,64]{3,2,1,0:T(8,128)(2,1)S(1)} %copy-done.5), custom_call_target="tpu_custom_call" | custom-call | tf_op jit(solution)/shard_map/pallas_call | solution.py:78
  21.9 1.0 collective-permute-start
  22.8 2.9 %shard_map.66 = bf16[1,576,256]{2,1,0:T(8,128)(2,1)} custom-call(s32[1]{0:T(128)} %bitcast.2.block_ref, bf16[128,8192]{1,0:T(8,128)(2,1)S(1)} %copy-done, bf16[14,8192]{1,0:T(8,128)(2,1)S(1)} %copy-done.4, bf16[64,128]{1,0:T(8,128)(2,1)S(1)} %copy-done.9, bf16[8,2,64,64]{3,2,1,0:T(8,128)(2,1)S(1)} %copy-done.6), custom_call_target="tpu_custom_call" | custom-call | tf_op jit(solution)/shard_map/pallas_call | solution.py:78
  25.7 2.2 %collective-permute-start.1 = (bf16[1,576,256]{2,1,0:T(8,128)(2,1)}, bf16[1,576,256]{2,1,0:T(8,128)(2,1)S(1)}, u32[]{:S(2)}, u32[]{:S(2)}) collective-permute-start(bf16[1,576,256]{2,1,0:T(8,128)(2,1)} %shard_map.66), channel_id=1, source_target_pairs={{0,128},{4,132},{8,136},{12,140},{16,144},{20,148},{24,152},{28,15... | collective-permute-start | bytes 884744 | tf_op jit(solution)/shard_map/ppermute | solution.py:241
  27.9 2.2 %shard_map.67 = bf16[1,576,256]{2,1,0:T(8,128)(2,1)S(1)} custom-call(s32[1]{0:T(128)} %bitcast.3.block_ref, bf16[128,8192]{1,0:T(8,128)(2,1)S(1)} %copy-done, bf16[14,8192]{1,0:T(8,128)(2,1)S(1)} %copy-done.4, bf16[64,128]{1,0:T(8,128)(2,1)S(1)} %copy-done.9, bf16[8,2,64,64]{3,2,1,0:T(8,128)(2,1)S(1)} %copy-done.6), custom_call_target="tpu_custom_call" | custom-call | tf_op jit(solution)/shard_map/pallas_call | solution.py:78
  30.1 1.0 collective-permute-start.2
  31.1 2.2 %shard_map.64.refs_0_.refs_4_ = bf16[1,576,256]{2,1,0:T(8,128)(2,1)S(1)} custom-call(s32[1]{0:T(128)} %bitcast.block_ref, bf16[128,8192]{1,0:T(8,128)(2,1)S(1)} %copy-done, bf16[14,8192]{1,0:T(8,128)(2,1)S(1)} %copy-done.4, bf16[64,128]{1,0:T(8,128)(2,1)S(1)} %copy-done.9, bf16[8,2,64,64]{3,2,1,0:T(8,128)(2,1)S(1)} %copy-done.6), custom_call_target="tpu_custom_call" | custom-call | tf_op jit(solution)/shard_map/pallas_call | solution.py:78
  33.3 3.4 %collective-permute-done.1.refs_2_.refs_6_ = bf16[1,576,256]{2,1,0:T(8,128)(2,1)S(1)} collective-permute-done((bf16[1,576,256]{2,1,0:T(8,128)(2,1)}, bf16[1,576,256]{2,1,0:T(8,128)(2,1)S(1)}, u32[]{:S(2)}, u32[]{:S(2)}) %collective-permute-start.1) | collective-permute-done | bytes 294944 | tf_op jit(solution)/shard_map/ppermute | solution.py:241
  36.6 7.7 %collective-permute-done.2.refs_3_.refs_7_ = bf16[1,576,256]{2,1,0:T(8,128)(2,1)S(1)} collective-permute-done((bf16[1,576,256]{2,1,0:T(8,128)(2,1)S(1)}, bf16[1,576,256]{2,1,0:T(8,128)(2,1)S(1)}, u32[]{:S(2)}, u32[]{:S(2)}) %collective-permute-start.2) | collective-permute-done | bytes 294944 | tf_op jit(solution)/shard_map/ppermute | solution.py:241
  44.3 2.8 %shard_map.68 = bf16[8,272,256]{2,1,0:T(8,128)(2,1)} custom-call(bf16[1,576,256]{2,1,0:T(8,128)(2,1)S(1)} %shard_map.64.refs_0_.refs_4_, bf16[1,576,256]{2,1,0:T(8,128)(2,1)S(1)} %collective-permute-done.refs_1_.refs_5_, bf16[1,576,256]{2,1,0:T(8,128)(2,1)S(1)} %collective-permute-done.1.refs_2_.refs_6_, ...), custom_call_target="tpu_custom_call" | custom-call | tf_op jit(solution)/shard_map/pallas_call | solution.py:123
  47.1 8.4 %all-to-all-start = ((bf16[8,272,256]{2,1,0:T(8,128)(2,1)}), bf16[8,272,256]{2,1,0:T(8,128)(2,1)S(1)}, u32[]{:S(2)}, u32[]{:S(2)}) async-start(bf16[8,272,256]{2,1,0:T(8,128)(2,1)} %shard_map.68), calls=%async_computation | async-start | bytes 2228224 | tf_op jit(solution)/shard_map/all_to_all | solution.py:261
  55.5 28.3 %all-to-all-done.data_ref.ang_ref = bf16[8,272,256]{2,1,0:T(8,128)(2,1)S(1)} async-done(((bf16[8,272,256]{2,1,0:T(8,128)(2,1)}), bf16[8,272,256]{2,1,0:T(8,128)(2,1)S(1)}, u32[]{:S(2)}, u32[]{:S(2)}) %all-to-all-start) | async-done | bytes 1114144 | tf_op jit(solution)/shard_map/all_to_all | solution.py:261
  83.8 1.6 %copy-done.1 = bf16[32,4,64,128]{3,2,1,0:T(8,128)(2,1)S(1)} copy-done((bf16[32,4,64,128]{3,2,1,0:T(8,128)(2,1)S(1)}, bf16[32,4,64,128]{3,2,1,0:T(8,128)(2,1)}, u32[]{:S(2)}) %copy-start.1) | copy-done | bytes 2097176
  85.4 4.1 %shard_map.69 = (bf16[2176,128]{1,0:T(8,128)(2,1)S(1)}, bf16[2176,128]{1,0:T(8,128)(2,1)}) custom-call(s32[1]{0:T(128)} %bitcast.4.core_ref, bf16[8,272,256]{2,1,0:T(8,128)(2,1)S(1)} %all-to-all-done.data_ref.ang_ref, bf16[8,272,256]{2,1,0:T(8,128)(2,1)S(1)} %all-to-all-done.data_ref.ang_ref, bf16[8,4,4,64,128]{4,3,2,1,0:T(8,128)(2,1)S(1)} %bitcast.25), custom_call_target="tpu_custom_call" | custom-call | tf_op jit(solution)/shard_map/pallas_call | solution.py:171
  89.4 1.3 %collective-permute-start.6 = (bf16[2176,128]{1,0:T(8,128)(2,1)}, bf16[2176,128]{1,0:T(8,128)(2,1)S(1)}, u32[]{:S(2)}, u32[]{:S(2)}) collective-permute-start(bf16[2176,128]{1,0:T(8,128)(2,1)} %get-tuple-element.8), channel_id=1, source_target_pairs={{0,4},{4,0},{8,12},{12,8},{16,20},{20,16},{24,28},{28,24},{32,36},... | collective-permute-start | bytes 1671176 | tf_op jit(solution)/shard_map/ppermute | solution.py:244
  90.7 0.2 copy.15
  90.9 0.8 slice_bitcast_fusion
  91.8 0.1 stack.42.where_ref
  91.9 0.1 copy.18.eval_ref
  92.0 2.0 %collective-permute-done.7.oth_mats_ref = bf16[8,4,64,128]{3,2,1,0:T(8,128)(2,1)} collective-permute-done((bf16[8,4,64,128]{3,2,1,0:T(8,128)(2,1)}, bf16[8,4,64,128]{3,2,1,0:T(8,128)(2,1)}, u32[]{:S(2)}, u32[]{:S(2)}) %collective-permute-start.7) | collective-permute-done | bytes 524320 | tf_op jit(solution)/shard_map/ppermute | solution.py:244
  94.0 5.6 %shard_map.70 = bf16[128,8192]{1,0:T(8,128)(2,1)} custom-call(s32[5]{0:T(128)S(1)} %stack.42.where_ref, bf16[2176,128]{1,0:T(8,128)(2,1)S(1)} %get-tuple-element.7.own_ref.own_ang_ref, bf16[2176,128]{1,0:T(8,128)(2,1)S(1)} %collective-permute-done.6.oth_ref.oth_ang_ref, bf16[2176,128]{1,0:T(8,128)(2,1)S(1)} %get-tuple-element.7.own_ref.own_ang_ref, ...), custom_call_target="tpu_custom_call" | custom-call | tf_op jit(solution)/shard_map/pallas_call | solution.py:214
  (29 shorter events, 0.1 us)
Async XLA Ops:
  6.5 10.5 %copy-start.9 = (bf16[64,128]{1,0:T(8,128)(2,1)S(1)}, bf16[64,128]{1,0:T(8,128)(2,1)}, u32[]{:S(2)}) copy-start(bf16[64,128]{1,0:T(8,128)(2,1)} %proj_ref.7) | copy-start | bytes 49156
  6.5 10.5 %copy-start = (bf16[128,8192]{1,0:T(8,128)(2,1)S(1)}, bf16[128,8192]{1,0:T(8,128)(2,1)}, u32[]{:S(2)}) copy-start(bf16[128,8192]{1,0:T(8,128)(2,1)} %src_ref.7) | copy-start | bytes 6291460
  6.5 77.2 %all-gather.3.cloned.1.call-start = ((), (), s32[]{:S(2)}) async-start(), calls=%async_computation.1 | async-start | bytes 2359296 | tf_op jit(solution)/shard_map/all_gather | solution.py:250
  7.8 6.4 %collective-permute-start.5 = (bf16[6,64,128]{2,1,0:T(8,128)(2,1)S(1)}, bf16[6,64,128]{2,1,0:T(8,128)(2,1)S(1)}, u32[]{:S(2)}, u32[]{:S(2)}) collective-permute-start(bf16[6,64,128]{2,1,0:T(8,128)(2,1)S(1)} %pad_maximum_fusion.1.refs_8_), channel_id=1, source_target_pairs={{0,192},{4,196},{8,200},{12,204},{16,208},{20,212},{24,216},{28,22... | collective-permute-start | bytes 294920 | tf_op jit(solution)/shard_map/ppermute | solution.py:241
  11.2 5.1 %collective-permute-start.4 = (bf16[6,64,128]{2,1,0:T(8,128)(2,1)S(1)}, bf16[6,64,128]{2,1,0:T(8,128)(2,1)S(1)}, u32[]{:S(2)}, u32[]{:S(2)}) collective-permute-start(bf16[6,64,128]{2,1,0:T(8,128)(2,1)S(1)} %pad_maximum_fusion.1.refs_8_), channel_id=1, source_target_pairs={{0,128},{4,132},{8,136},{12,140},{16,144},{20,148},{24,152},{28,15... | collective-permute-start | bytes 294920 | tf_op jit(solution)/shard_map/ppermute | solution.py:241
  11.7 4.6 %collective-permute-start.3 = (bf16[6,64,128]{2,1,0:T(8,128)(2,1)S(1)}, bf16[6,64,128]{2,1,0:T(8,128)(2,1)S(1)}, u32[]{:S(2)}, u32[]{:S(2)}) collective-permute-start(bf16[6,64,128]{2,1,0:T(8,128)(2,1)S(1)} %pad_maximum_fusion.1.refs_8_), channel_id=1, source_target_pairs={{0,64},{4,68},{8,72},{12,76},{16,80},{20,84},{24,88},{28,92},{32,9... | collective-permute-start | bytes 294920 | tf_op jit(solution)/shard_map/ppermute | solution.py:241
  16.2 0.8 copy-start.7
  17.1 1.0 copy-start.3
  18.0 0.9 copy-start.5
  19.0 3.8 %copy-start.4 = (bf16[14,8192]{1,0:T(8,128)(2,1)S(1)}, bf16[14,8192]{1,0:T(8,128)(2,1)}, u32[]{:S(2)}) copy-start(bf16[14,8192]{1,0:T(8,128)(2,1)} %ang_ref.7) | copy-start | bytes 688132
  19.0 3.9 %copy-start.6 = (bf16[8,2,64,64]{3,2,1,0:T(8,128)(2,1)S(1)}, bf16[8,2,64,64]{3,2,1,0:T(8,128)(2,1)}, u32[]{:S(2)}) copy-start(bf16[8,2,64,64]{3,2,1,0:T(8,128)(2,1)} %mats_ref.7) | copy-start | bytes 393220
  21.9 11.4 %collective-permute-start = (bf16[1,576,256]{2,1,0:T(8,128)(2,1)}, bf16[1,576,256]{2,1,0:T(8,128)(2,1)S(1)}, u32[]{:S(2)}, u32[]{:S(2)}) collective-permute-start(bf16[1,576,256]{2,1,0:T(8,128)(2,1)} %shard_map.65), channel_id=1, source_target_pairs={{0,64},{4,68},{8,72},{12,76},{16,80},{20,84},{24,88},{28,92},{32,9... | collective-permute-start | bytes 884744 | tf_op jit(solution)/shard_map/ppermute | solution.py:241
  25.7 10.9 %collective-permute-start.1 = (bf16[1,576,256]{2,1,0:T(8,128)(2,1)}, bf16[1,576,256]{2,1,0:T(8,128)(2,1)S(1)}, u32[]{:S(2)}, u32[]{:S(2)}) collective-permute-start(bf16[1,576,256]{2,1,0:T(8,128)(2,1)} %shard_map.66), channel_id=1, source_target_pairs={{0,128},{4,132},{8,136},{12,140},{16,144},{20,148},{24,152},{28,15... | collective-permute-start | bytes 884744 | tf_op jit(solution)/shard_map/ppermute | solution.py:241
  30.1 14.2 %copy-start.8 = (bf16[6,64,128]{2,1,0:T(8,128)(2,1)S(1)}, bf16[6,64,128]{2,1,0:T(8,128)(2,1)}, u32[]{:S(2)}) copy-start(bf16[6,64,128]{2,1,0:T(8,128)(2,1)} %copy-done.7) | copy-start | bytes 294916
  30.1 14.2 %collective-permute-start.2 = (bf16[1,576,256]{2,1,0:T(8,128)(2,1)S(1)}, bf16[1,576,256]{2,1,0:T(8,128)(2,1)S(1)}, u32[]{:S(2)}, u32[]{:S(2)}) collective-permute-start(bf16[1,576,256]{2,1,0:T(8,128)(2,1)S(1)} %shard_map.67), channel_id=1, source_target_pairs={{0,192},{4,196},{8,200},{12,204},{16,208},{20,212},{24,216},{28,22... | collective-permute-start | bytes 884744 | tf_op jit(solution)/shard_map/ppermute | solution.py:241
  47.1 36.7 %all-to-all-start = ((bf16[8,272,256]{2,1,0:T(8,128)(2,1)}), bf16[8,272,256]{2,1,0:T(8,128)(2,1)S(1)}, u32[]{:S(2)}, u32[]{:S(2)}) async-start(bf16[8,272,256]{2,1,0:T(8,128)(2,1)} %shard_map.68), calls=%async_computation | async-start | bytes 2228224 | tf_op jit(solution)/shard_map/all_to_all | solution.py:261
  83.8 1.6 %copy-start.1 = (bf16[32,4,64,128]{3,2,1,0:T(8,128)(2,1)S(1)}, bf16[32,4,64,128]{3,2,1,0:T(8,128)(2,1)}, u32[]{:S(2)}) copy-start(bf16[32,4,64,128]{3,2,1,0:T(8,128)(2,1)} %all-gather.3.cloned.1.call-done) | copy-start | bytes 6291460
  89.4 2.4 %copy-start.10 = (bf16[128,64]{0,1:T(8,128)(2,1)S(1)}, bf16[128,64]{0,1:T(8,128)(2,1)}, u32[]{:S(2)}) copy-start(bf16[128,64]{0,1:T(8,128)(2,1)} %param.11) | copy-start | bytes 49156
  89.4 4.6 %copy-start.2 = (bf16[32,4,64,128]{3,2,1,0:T(8,128)(2,1)S(1)}, bf16[32,4,64,128]{3,2,1,0:T(8,128)(2,1)}, u32[]{:S(2)}) copy-start(bf16[32,4,64,128]{3,2,1,0:T(8,128)(2,1)} %all-gather.3.cloned.1.call-done) | copy-start | bytes 6291460
  89.4 4.6 %collective-permute-start.6 = (bf16[2176,128]{1,0:T(8,128)(2,1)}, bf16[2176,128]{1,0:T(8,128)(2,1)S(1)}, u32[]{:S(2)}, u32[]{:S(2)}) collective-permute-start(bf16[2176,128]{1,0:T(8,128)(2,1)} %get-tuple-element.8), channel_id=1, source_target_pairs={{0,4},{4,0},{8,12},{12,8},{16,20},{20,16},{24,28},{28,24},{32,36},... | collective-permute-start | bytes 1671176 | tf_op jit(solution)/shard_map/ppermute | solution.py:244
  91.8 2.3 %collective-permute-start.7 = (bf16[8,4,64,128]{3,2,1,0:T(8,128)(2,1)}, bf16[8,4,64,128]{3,2,1,0:T(8,128)(2,1)}, u32[]{:S(2)}, u32[]{:S(2)}) collective-permute-start(bf16[8,4,64,128]{3,2,1,0:T(8,128)(2,1)} %slice_bitcast_fusion), channel_id=1, source_target_pairs={{0,4},{4,0},{8,12},{12,8},{16,20},{20,16},{24,28},{28,24},{32,36},... | collective-permute-start | bytes 1572872 | tf_op jit(solution)/shard_map/ppermute | solution.py:244
Sparse Core Ops, SparseCore 0:
  17.2 41.2 all-gather.2

commit v2 on v0

v2 whole, which is shorter than its diff:
```python
import functools

import jax
import jax.numpy as jnp
from jax import lax
from jax.experimental import pallas as pl
from jax.experimental.pallas import tpu as pltpu
from jax.sharding import PartitionSpec as P

R = 64
TILE = 256
BF = jnp.bfloat16
F32 = jnp.float32

NX, NZ, NC, PLANES = 4, 8, 2, 4
BLOCKS = NX * NZ
ROWS = 2 * R + 16
PARAMS = pltpu.CompilerParams(vmem_limit_bytes=60 * 2**20)
SLOTS = [(j, t, i) for j in range(NX) for t in range(PLANES) for i in range(2)]


def dot(a, b):
    return jnp.dot(a, b, preferred_element_type=F32)


def cos_sin(t):
    h = 0.5 * t
    q = h * h
    s = 1.0 + q * (
        -1.0 / 6 + q * (1.0 / 120 + q * (-1.0 / 5040 + q * (1.0 / 362880 + q * (-1.0 / 39916800 + q * (1.0 / 6227020800)))))
    )
    s = s * h
    c = 1.0 + q * (
        -0.5 + q * (1.0 / 24 + q * (-1.0 / 720 + q * (1.0 / 40320 + q * (-1.0 / 3628800 + q * (1.0 / 479001600)))))
    )
    return 1.0 - 2.0 * s * s, 2.0 * s * c


def mix(mat, own, partner, c, s):
    return dot(mat, jnp.concatenate([own * c, partner * s], axis=0)).astype(BF)


def row(values, i):
    return values[i : i + 1].astype(BF)


def local_kernel(start, src_any, ang_any, proj_any, mats_any, *refs):
    out_ref, src_all, ang_all, proj_ref, mats_ref, sems = refs[-6:]
    step, steps, width = pl.program_id(0), src_all.shape[0], src_all.shape[2]

    def loads(n):
        columns = pl.ds((start + n) * width, width)
        return (
            pltpu.make_async_copy(src_any.at[:, columns], src_all.at[n], sems.at[n, 0]),
            pltpu.make_async_copy(ang_any.at[:, columns], ang_all.at[n], sems.at[n, 1]),
        )

    shared = (
        pltpu.make_async_copy(proj_any, proj_ref, sems.at[steps, 0]),
        pltpu.make_async_copy(mats_any, mats_ref, sems.at[steps, 1]),
    )

    @pl.when(step == 0)
    def _():
        for copy in (shared[0], *loads(0), shared[1]):
            copy.start()
        for n in range(1, steps):
            for copy in loads(n):
                copy.start()
        for copy in shared:
            copy.wait()

    for n in range(steps):

        @pl.when(step == n)
        def _():
            for copy in loads(n):
                copy.wait()

    src_ref = src_all.at[step]
    tiles = width // TILE
    levels = mats_ref.shape[0]
    ang = ang_all[step].astype(F32)
    cos, sin = cos_sin(ang[:levels])
    proj = proj_ref[...]
    x = [dot(proj, src_ref[:, i * TILE : (i + 1) * TILE]).astype(BF) for i in range(tiles)]
    to = lax.broadcasted_iota(jnp.int32, (TILE, TILE), 1)
    frm = lax.broadcasted_iota(jnp.int32, (TILE, TILE), 0)
    for level in range(levels):
        span = 1 << level
        if span == 128:
            xp = [jnp.concatenate([v[:, 128:], v[:, :128]], axis=1) for v in x]
        else:
            perm = jnp.where(frm == (to ^ span), 1.0, 0.0).astype(BF)
            every = dot(jnp.concatenate(x, axis=0), perm).astype(BF)
            xp = [every[i * R : (i + 1) * R] for i in range(tiles)]
        mat = jnp.concatenate([mats_ref[level, 0], mats_ref[level, 1]], axis=1)
        c, s = row(cos, level), row(sin, level)
        x = [
            mix(mat, x[i], xp[i], c[:, i * TILE : (i + 1) * TILE], s[:, i * TILE : (i + 1) * TILE])
            for i in range(tiles)
        ]
    a = jnp.concatenate([ang[levels : levels + 6], jnp.zeros((2, ang.shape[1]), F32)], axis=0)
    for i in range(tiles):
        lo, mid, hi = i * TILE, i * TILE + 128, (i + 1) * TILE
        out_ref[i, :R] = x[i][:, :128]
        out_ref[i, R : 2 * R] = x[i][:, 128:]
        out_ref[i, 2 * R :] = jnp.concatenate([a[:, lo:mid], a[:, mid:hi]], axis=0).astype(BF)


def local_levels(steps, start, before, source_field, angles, project_mats, local_mats):
    q, columns = source_field.shape
    width = columns // 4
    tiles = width // TILE
    args = [source_field, angles, project_mats, local_mats]
    if before is not None:
        args.append(before)
    return pl.pallas_call(
        functools.partial(local_kernel, start),
        grid=(steps,),
        in_specs=[pl.BlockSpec(memory_space=pltpu.HBM)] * len(args),
        out_specs=pl.BlockSpec((tiles, ROWS, 128), lambda i: (start + i, 0, 0)),
        out_shape=jax.ShapeDtypeStruct((BLOCKS, ROWS, 128), BF),
        scratch_shapes=[
            pltpu.VMEM((steps, q, width), BF),
            pltpu.VMEM((steps, angles.shape[0], width), BF),
            pltpu.VMEM(project_mats.shape, BF),
            pltpu.VMEM(local_mats.shape, BF),
            pltpu.SemaphoreType.DMA((steps + 1, 2)),
        ],
        input_output_aliases={4: 0} if before is not None else {},
        compiler_params=PARAMS,
    )(*args)


def chip_kernel(at_ref, data_ref, q0_ref, q1_ref, q2lo_ref, q2hi_ref, q3_ref, keep_ref, send_ref, mats_ref, sems):
    early, late = pl.ds(0, 3), pl.ds(3, 3)
    pieces = [(t, part, ref.at[part]) for part in (early, late) for t, ref in ((0, q0_ref), (1, q1_ref), (3, q3_ref))]
    pieces += [(2, early, q2lo_ref), (2, late, q2hi_ref)]
    copies = [
        pltpu.make_async_copy(ref, mats_ref.at[t, part], sems.at[n]) for n, (t, part, ref) in enumerate(pieces)
    ]
    for copy in copies:
        copy.start()
    low = at_ref[0] == 0
    x, cs, last = {}, {}, {}
    for n, slot in enumerate(SLOTS):
        block = at_ref[1 + n]
        x[slot] = jnp.concatenate([data_ref[block, :R], data_ref[block, R : 2 * R]], axis=1)
        a = data_ref[block, 2 * R :].astype(F32)
        cs[slot] = cos_sin(jnp.concatenate([a[:8], a[8:]], axis=1))
        last[slot] = (a[:8], a[8:])
    for copy in copies:
        copy.wait()
    flips = ((2, 0, 0), (1, 0, 0), (0, 2, 0), (0, 1, 0), (0, 0, 1))
    for level, flip in enumerate(flips):
        x = {
            (j, t, i): mix(
                mats_ref[t, level, j, i],
                x[j, t, i],
                x[j ^ flip[0], t ^ flip[1], i ^ flip[2]],
                row(cs[j, t, i][0], level),
                row(cs[j, t, i][1], level),
            )
            for j, t, i in SLOTS
        }
    for n, slot in enumerate(SLOTS):
        at = n * R
        lo, hi = x[slot][:, :128], x[slot][:, 128:]
        keep_ref[at : at + R] = jnp.where(low, lo, hi)
        send_ref[at : at + R] = jnp.where(low, hi, lo)
    for n in range(0, BLOCKS, 2):
        at = BLOCKS * R + n * 8
        (lo0, hi0), (lo1, hi1) = last[SLOTS[n]], last[SLOTS[n + 1]]
        lo, hi = jnp.concatenate([lo0, lo1], axis=0), jnp.concatenate([hi0, hi1], axis=0)
        keep_ref[at : at + 16] = jnp.where(low, lo, hi).astype(BF)
        send_ref[at : at + 16] = jnp.where(low, hi, lo).astype(BF)
    for n, (j, t, i) in enumerate(SLOTS):
        at = BLOCKS * (R + 8) + n * R
        keep_ref[at : at + R] = mats_ref[t, 5, j, i]
        send_ref[at : at + R] = mats_ref[t, 5, j, i]


def chip_levels(at, moved, mats):
    out = jax.ShapeDtypeStruct((BLOCKS * (2 * R + 8), 128), BF)
    vmem = pl.BlockSpec(memory_space=pltpu.VMEM)
    return pl.pallas_call(
        chip_kernel,
        in_specs=[pl.BlockSpec(memory_space=pltpu.SMEM), vmem] + [pl.BlockSpec(memory_space=pltpu.HBM)] * 5,
        out_specs=[vmem, vmem],
        out_shape=[out, out],
        scratch_shapes=[pltpu.VMEM((PLANES, 6, NX, 2, R, 2 * R), BF), pltpu.SemaphoreType.DMA((8,))],
        compiler_params=PARAMS,
    )(at, moved, *mats)


def last_kernel(at_ref, own_ref, oth_ref, eval_ref, out_ref):
    low = at_ref[0] == 0
    ev = eval_ref[...]
    for n in range(BLOCKS):
        if n % 2 == 0:
            a = BLOCKS * R + n * 8
            own_c, own_s = cos_sin(own_ref[a : a + 16].astype(F32))
            oth_c, oth_s = cos_sin(oth_ref[a : a + 16].astype(F32))
        at, r, m = n * R, 5 + 8 * (n % 2), BLOCKS * (R + 8) + n * R
        own, oth = own_ref[at : at + R], oth_ref[at : at + R]
        y_own = mix(own_ref[m : m + R], own, oth, row(own_c, r), row(own_s, r))
        y_oth = mix(oth_ref[m : m + R], oth, own, row(oth_c, r), row(oth_s, r))
        y = jnp.concatenate([jnp.where(low, y_own, y_oth), jnp.where(low, y_oth, y_own)], axis=1)
        column = pl.multiple_of(at_ref[1 + n] * TILE, TILE)
        out_ref[:, pl.ds(column, TILE)] = dot(ev, y).astype(BF)


def last_level(at, keep, received, evaluate_mats):
    vmem = pl.BlockSpec(memory_space=pltpu.VMEM)
    return pl.pallas_call(
        last_kernel,
        in_specs=[pl.BlockSpec(memory_space=pltpu.SMEM)] + [vmem] * 3,
        out_specs=vmem,
        out_shape=jax.ShapeDtypeStruct((evaluate_mats.shape[0], 64 * 128), BF),
        compiler_params=PARAMS,
    )(at, keep, received, evaluate_mats)


def shards(source_field, project_mats, local_mats, cross_mats, angles, evaluate_mats):
    box, plane = lax.axis_index("box"), lax.axis_index("src")
    x, z, core = box // (NZ * NC), box // NC % NZ, box % NC
    count = NX * NZ * NC

    def swap(values, distance):
        return lax.ppermute(values, "box", [(i, i ^ distance) for i in range(count)])

    def along_z(values, n):
        pairs = [
            (i * PLANES + p, (i ^ ((2 * p + n) * NC)) * PLANES + p) for i in range(count) for p in range(PLANES)
        ]
        return lax.ppermute(values, ("box", "src"), pairs)

    def along_src(values, t):
        return lax.ppermute(values, "src", [(p, p ^ t) for p in range(PLANES)])

    def after(value, *first):
        return lax.optimization_barrier((value, *first))[0]

    chips = [[xx * NZ * NC + zz * NC + c for xx in range(NX) for zz in range(NZ)] for c in range(NC)]

    own = jnp.concatenate([cross_mats[:, 0], cross_mats[:, 1]], axis=-1)
    pair = [along_z(own, n) for n in (0, 1)]
    first = local_levels(1, 0, None, source_field, angles, project_mats, local_mats)
    pair = jnp.stack([after(pair[0], first), pair[1]], axis=1)
    quarter = [pair] + [swap(pair, j * NZ * NC) for j in (1, 2, 3)]
    sent = local_levels(3, 1, after(first, pair), source_field, angles, project_mats, local_mats)
    sent, *quarter = lax.optimization_barrier((sent, *quarter))
    moved = lax.all_to_all(sent, "box", 0, 0, tiled=True, axis_index_groups=chips)
    quarter = jnp.stack(quarter, axis=1)
    q1, q3 = along_src(quarter, 1), along_src(quarter, 3)
    mats = [quarter, q1, along_src(q3[:3], 1), along_src(q1[3:], 3), q3]

    blocks = [(x ^ j) * NZ + (z ^ (((plane ^ t) << 1) | i)) for j, t, i in SLOTS]
    at = jnp.stack([core] + blocks).astype(jnp.int32)
    keep, send = chip_levels(at, moved, mats)
    received = swap(send, 1)
    return last_level(at, keep, received, evaluate_mats)


def solution(mesh):
    in_specs = (
        P("src", "box"),
        P("box", None),
        P(None, None, "box", None),
        P(None, None, "box", None),
        P(None, "box"),
        P("box", None),
    )
    out_specs = P("src", "box")
    return jax.shard_map(shards, mesh=mesh, in_specs=in_specs, out_specs=out_specs, check_vma=False)
```

time: 336 us -> 89.9 us (0.27)
  waiting for transfers between devices: 139 us -> 26.5 us
  local copies, waits for them, and re-layouts: 97.8 us -> 5.95 us
  blocking collectives: 37 us -> 0 us
  Pallas kernels: 0 us -> 23.1 us
  matrix products: 21.1 us -> 0 us
    ppermute x6 -> x10, waiting for transfers between devices: 139 us -> 26.5 us  [the longest x4 22.1 us: along_src(): return lax.ppermute(values, 'src', [(p, p ^ t) for p in range(PLANES)])]
    rev x8 -> x0, local copies, waits for them, and re-layouts: 52.7 us -> none  [flip_last(): return jnp.flip(reshaped, axis=-2).reshape(full_shape)]
    all_to_all x1 -> x0, blocking collectives: 37 us -> none  [shards(): lax.all_to_all(shaped, 'box', split_axis=1, concat_axis=1, tiled=True)]
    pallas_call x0 -> x4, Pallas kernels: none -> 23.1 us  [the longest x2 12.6 us: local_levels(): pl.pallas_call(functools.partial(local_kernel, start), grid=(steps,), in_...]
    dot_general x30 -> x0, matrix products: 21.1 us -> none  [the longest x14 11.2 us: mix_local(): jnp.dot(matrices[1], partner, preferred_element_type=jnp.float32)]
    convert_element_type x7 -> x0, local copies, waits for them, and re-layouts: 14.9 us -> none  [the longest x5 8.91 us: mix_local(): (jnp.cos(phase_row)[None] * own_term + jnp.sin(phase_row)[None] * partner...]
    sin x1 -> x0, local copies, waits for them, and re-layouts: 13 us -> none  [mix_local(): jnp.sin(phase_row)[None] * partner_term]
    ppermute x6 -> x10, starting transfers between devices: 36.3 us -> 25.9 us  [the longest x4 15.1 us: along_src(): return lax.ppermute(values, 'src', [(p, p ^ t) for p in range(PLANES)])]
  transfers between devices with their start and end apart: 6 -> 11, of which waited for: 6 -> 5; matrix products, arithmetic and copies ran while one was open for 1% -> 3% of each run, Pallas kernels for 0% -> 14%
where the time goes in v2:
time: 89.9 us; the launch traced here: 89.6 us
  starting transfers between devices  33.6 us (37%)
  waiting for transfers between devices  26.5 us (29%)
  Pallas kernels  23.1 us (26%)
  local copies, waits for them, and re-layouts  5.95 us (7%)
    ppermute x4, waiting for transfers between devices, along_src(): return lax.ppermute(values, 'src', [(p, p ^ t) for p in range(PLANES)])  22.1 us
    ppermute x4, starting transfers between devices, along_src(): return lax.ppermute(values, 'src', [(p, p ^ t) for p in range(PLANES)])  15.1 us
    pallas_call x2, Pallas kernels, local_levels(): pl.pallas_call(functools.partial(local_kernel, start), grid=(steps,), in_...  12.6 us
    all_to_all x1, starting transfers between devices, shards(): lax.all_to_all(sent, 'box', 0, 0, tiled=True, axis_index_groups=chips)  7.69 us
    ppermute x4, starting transfers between devices, swap(): lax.ppermute(values, 'box', [(i, i ^ distance) for i in range(count)])  7.64 us
    pallas_call x1, Pallas kernels, chip_levels(): pl.pallas_call(chip_kernel, in_specs=[pl.BlockSpec(memory_space=pltpu.SME...  6.12 us
    pallas_call x1, Pallas kernels, last_level(): pl.pallas_call(last_kernel, in_specs=[pl.BlockSpec(memory_space=pltpu.SME...  4.42 us
    ppermute x4, waiting for transfers between devices, swap(): lax.ppermute(values, 'box', [(i, i ^ distance) for i in range(count)])  4.41 us
  transfers between devices with their start and end apart: 11, of which 5 were waited for; matrix products, arithmetic and copies ran while one was open for 3% of the time, Pallas kernels for 14%

profile of v2, /device:TPU:1, one launch (start us, length us, event | category | flops | bytes accessed | tf_op | source)
XLA Modules:
  0.0 89.6 jit_solution(13359524424958193035)
XLA Ops:
  0.0 1.0 %slice_bitcast_fusion.1 = (bf16[6,64,64]{2,1,0:T(8,128)(2,1)S(1)}, bf16[6,64,64]{2,1,0:T(8,128)(2,1)S(1)}) fusion(bf16[6,2,64,64]{3,2,1,0:T(8,128)(2,1)} %param.9), kind=kLoop, calls=%fused_computation.4 | loop fusion | bytes 196608 | tf_op jit(solution)/shard_map/squeeze | solution.py:247
  1.0 0.1 pad_maximum_fusion.2
  1.1 0.7 collective-permute-start
  1.7 2.6 %collective-permute-start.1 = (bf16[6,64,128]{2,1,0:T(8,128)(2,1)S(1)}, bf16[6,64,128]{2,1,0:T(8,128)(2,1)S(1)}, u32[]{:S(2)}, u32[]{:S(2)}) collective-permute-start(bf16[6,64,128]{2,1,0:T(8,128)(2,1)S(1)} %pad_maximum_fusion.2), channel_id=1, source_target_pairs={{0,8},{1,25},{2,42},{3,59},{4,12},{5,29},{6,46},{7,63},{8,0},{9,17... | collective-permute-start | bytes 294920 | tf_op jit(solution)/shard_map/ppermute | solution.py:237
  4.3 4.1 %shard_map.64.refs_0_ = bf16[32,144,128]{2,1,0:T(8,128)(2,1)} custom-call(bf16[128,8192]{1,0:T(8,128)(2,1)} %src_any.3, bf16[14,8192]{1,0:T(8,128)(2,1)} %ang_any.3, bf16[64,128]{1,0:T(8,128)(2,1)} %proj_any.3, bf16[8,2,64,64]{3,2,1,0:T(8,128)(2,1)} %mats_any.3), custom_call_target="tpu_custom_call" | custom-call | tf_op jit(solution)/shard_map/pallas_call | solution.py:118
  8.4 0.0 collective-permute-done
  8.4 1.3 %collective-permute-start.2 = (bf16[6,2,64,128]{3,2,1,0:T(8,128)(2,1)S(1)}, bf16[6,2,64,128]{3,2,1,0:T(8,128)(2,1)S(1)}, u32[]{:S(2)}, u32[]{:S(2)}) collective-permute-start(bf16[6,2,64,128]{3,2,1,0:T(8,128)(2,1)S(1)} %pad_maximum_fusion.1), channel_id=1, source_target_pairs={{0,64},{4,68},{8,72},{12,76},{16,80},{20,84},{24,88},{28,92},{32,9... | collective-permute-start | bytes 589832 | tf_op jit(solution)/shard_map/ppermute | solution.py:231
  9.7 2.4 %collective-permute-start.3 = (bf16[6,2,64,128]{3,2,1,0:T(8,128)(2,1)S(1)}, bf16[6,2,64,128]{3,2,1,0:T(8,128)(2,1)S(1)}, u32[]{:S(2)}, u32[]{:S(2)}) collective-permute-start(bf16[6,2,64,128]{3,2,1,0:T(8,128)(2,1)S(1)} %pad_maximum_fusion.1), channel_id=1, source_target_pairs={{0,128},{4,132},{8,136},{12,140},{16,144},{20,148},{24,152},{28,15... | collective-permute-start | bytes 589832 | tf_op jit(solution)/shard_map/ppermute | solution.py:231
  12.2 0.2 collective-permute-start.4
  12.4 8.5 %shard_map.65 = bf16[32,144,128]{2,1,0:T(8,128)(2,1)} custom-call(bf16[128,8192]{1,0:T(8,128)(2,1)} %src_any.3, bf16[14,8192]{1,0:T(8,128)(2,1)} %ang_any.3, bf16[64,128]{1,0:T(8,128)(2,1)} %proj_any.3, bf16[8,2,64,64]{3,2,1,0:T(8,128)(2,1)} %mats_any.3, bf16[32,144,128]{2,1,0:T(8,128)(2,1)} %shard_map.64.refs_0_), custom_call_target="tpu_custom_call", output_to_operand_aliasing={{}: (4, {})} | custom-call | tf_op jit(solution)/shard_map/pallas_call | solution.py:118
  20.9 2.5 %collective-permute-done.4 = bf16[6,2,64,128]{3,2,1,0:T(8,128)(2,1)S(1)} collective-permute-done((bf16[6,2,64,128]{3,2,1,0:T(8,128)(2,1)S(1)}, bf16[6,2,64,128]{3,2,1,0:T(8,128)(2,1)S(1)}, u32[]{:S(2)}, u32[]{:S(2)}) %collective-permute-start.4) | collective-permute-done | bytes 196640 | tf_op jit(solution)/shard_map/ppermute | solution.py:231
  23.4 7.7 %all-to-all-start = ((bf16[32,144,128]{2,1,0:T(8,128)(2,1)}), bf16[32,144,128]{2,1,0:T(8,128)(2,1)S(1)}, u32[]{:S(2)}, u32[]{:S(2)}) async-start(bf16[32,144,128]{2,1,0:T(8,128)(2,1)} %shard_map.65), calls=%async_computation | async-start | bytes 2359296 | tf_op jit(solution)/shard_map/all_to_all | solution.py:254
  31.1 0.1 pad_maximum_fusion.q0_ref
  31.2 11.4 %collective-permute-start.6 = (bf16[6,4,2,64,128]{4,3,2,1,0:T(8,128)(2,1)S(1)}, bf16[6,4,2,64,128]{4,3,2,1,0:T(8,128)(2,1)S(1)}, u32[]{:S(2)}, u32[]{:S(2)}) collective-permute-start(bf16[6,4,2,64,128]{4,3,2,1,0:T(8,128)(2,1)S(1)} %pad_maximum_fusion.q0_ref), channel_id=1, source_target_pairs={{0,3},{1,2},{2,1},{3,0},{4,7},{5,6},{6,5},{7,4},{8,11},{9,10},{10,... | collective-permute-start | bytes 2359304 | tf_op jit(solution)/shard_map/ppermute | solution.py:240
  42.6 1.0 %collective-permute-start.5 = (bf16[6,4,2,64,128]{4,3,2,1,0:T(8,128)(2,1)S(1)}, bf16[6,4,2,64,128]{4,3,2,1,0:T(8,128)(2,1)S(1)}, u32[]{:S(2)}, u32[]{:S(2)}) collective-permute-start(bf16[6,4,2,64,128]{4,3,2,1,0:T(8,128)(2,1)S(1)} %pad_maximum_fusion.q0_ref), channel_id=1, source_target_pairs={{0,1},{1,0},{2,3},{3,2},{4,5},{5,4},{6,7},{7,6},{8,9},{9,8},{10,11... | collective-permute-start | bytes 2359304 | tf_op jit(solution)/shard_map/ppermute | solution.py:240
  43.6 15.1 %collective-permute-done.6.q3_ref = bf16[6,4,2,64,128]{4,3,2,1,0:T(8,128)(2,1)S(1)} collective-permute-done((bf16[6,4,2,64,128]{4,3,2,1,0:T(8,128)(2,1)S(1)}, bf16[6,4,2,64,128]{4,3,2,1,0:T(8,128)(2,1)S(1)}, u32[]{:S(2)}, u32[]{:S(2)}) %collective-permute-start.6) | collective-permute-done | bytes 786464 | tf_op jit(solution)/shard_map/ppermute | solution.py:240
  58.7 0.8 slice.16
  59.5 1.0 %collective-permute-start.7 = (bf16[3,4,2,64,128]{4,3,2,1,0:T(8,128)(2,1)}, bf16[3,4,2,64,128]{4,3,2,1,0:T(8,128)(2,1)}, u32[]{:S(2)}, u32[]{:S(2)}) collective-permute-start(bf16[3,4,2,64,128]{4,3,2,1,0:T(8,128)(2,1)} %slice.16), channel_id=1, source_target_pairs={{0,1},{1,0},{2,3},{3,2},{4,5},{5,4},{6,7},{7,6},{8,9},{9,8},{10,11... | collective-permute-start | bytes 1179656 | tf_op jit(solution)/shard_map/ppermute | solution.py:240
  60.5 0.8 slice.17
  61.3 1.8 %collective-permute-start.8 = (bf16[3,4,2,64,128]{4,3,2,1,0:T(8,128)(2,1)}, bf16[3,4,2,64,128]{4,3,2,1,0:T(8,128)(2,1)}, u32[]{:S(2)}, u32[]{:S(2)}) collective-permute-start(bf16[3,4,2,64,128]{4,3,2,1,0:T(8,128)(2,1)} %slice.17), channel_id=1, source_target_pairs={{0,3},{1,2},{2,1},{3,0},{4,7},{5,6},{6,5},{7,4},{8,11},{9,10},{10,... | collective-permute-start | bytes 1179656 | tf_op jit(solution)/shard_map/ppermute | solution.py:240
  63.1 0.6 stack.159.at_ref
  63.7 4.3 %collective-permute-done.7.q2lo_ref = bf16[3,4,2,64,128]{4,3,2,1,0:T(8,128)(2,1)} collective-permute-done((bf16[3,4,2,64,128]{4,3,2,1,0:T(8,128)(2,1)}, bf16[3,4,2,64,128]{4,3,2,1,0:T(8,128)(2,1)}, u32[]{:S(2)}, u32[]{:S(2)}) %collective-permute-start.7) | collective-permute-done | bytes 393248 | tf_op jit(solution)/shard_map/ppermute | solution.py:240
  68.0 2.7 %collective-permute-done.8.q2hi_ref = bf16[3,4,2,64,128]{4,3,2,1,0:T(8,128)(2,1)} collective-permute-done((bf16[3,4,2,64,128]{4,3,2,1,0:T(8,128)(2,1)}, bf16[3,4,2,64,128]{4,3,2,1,0:T(8,128)(2,1)}, u32[]{:S(2)}, u32[]{:S(2)}) %collective-permute-start.8) | collective-permute-done | bytes 393248 | tf_op jit(solution)/shard_map/ppermute | solution.py:240
  70.7 0.0 all-to-all-done.data_ref
  70.8 0.0 copy-start
  70.8 1.0 %copy-done = bf16[32,144,128]{2,1,0:T(8,128)(2,1)} copy-done((bf16[32,144,128]{2,1,0:T(8,128)(2,1)}, bf16[32,144,128]{2,1,0:T(8,128)(2,1)S(1)}, u32[]{:S(2)}) %copy-start) | copy-done | bytes 1179672
  71.8 6.1 %shard_map.66 = (bf16[4352,128]{1,0:T(8,128)(2,1)}, bf16[4352,128]{1,0:T(8,128)(2,1)}) custom-call(s32[33]{0:T(128)} %stack.159.at_ref, bf16[32,144,128]{2,1,0:T(8,128)(2,1)} %copy-done, bf16[6,4,2,64,128]{4,3,2,1,0:T(8,128)(2,1)} %copy-done.1, bf16[6,4,2,64,128]{4,3,2,1,0:T(8,128)(2,1)} %copy-done.3, ...), custom_call_target="tpu_custom_call" | custom-call | tf_op jit(solution)/shard_map/pallas_call | solution.py:187
  77.9 3.7 %collective-permute-start.9 = (bf16[4352,128]{1,0:T(8,128)(2,1)}, bf16[4352,128]{1,0:T(8,128)(2,1)S(1)}, u32[]{:S(2)}, u32[]{:S(2)}) collective-permute-start(bf16[4352,128]{1,0:T(8,128)(2,1)} %get-tuple-element.22), channel_id=1, source_target_pairs={{0,4},{4,0},{8,12},{12,8},{16,20},{20,16},{24,28},{28,24},{32,36},... | collective-permute-start | bytes 3342344 | tf_op jit(solution)/shard_map/ppermute | solution.py:231
  81.6 0.7 copy.14.eval_ref
  82.3 1.9 %collective-permute-done.9.oth_ref = bf16[4352,128]{1,0:T(8,128)(2,1)S(1)} collective-permute-done((bf16[4352,128]{1,0:T(8,128)(2,1)}, bf16[4352,128]{1,0:T(8,128)(2,1)S(1)}, u32[]{:S(2)}, u32[]{:S(2)}) %collective-permute-start.9) | collective-permute-done | bytes 1114144 | tf_op jit(solution)/shard_map/ppermute | solution.py:231
  84.2 1.0 %copy-done.4 = bf16[4352,128]{1,0:T(8,128)(2,1)} copy-done((bf16[4352,128]{1,0:T(8,128)(2,1)}, bf16[4352,128]{1,0:T(8,128)(2,1)S(1)}, u32[]{:S(2)}) %copy-start.4) | copy-done | bytes 1114136
  85.2 4.4 %shard_map.67 = bf16[128,8192]{1,0:T(8,128)(2,1)} custom-call(s32[33]{0:T(128)} %stack.159.at_ref, bf16[4352,128]{1,0:T(8,128)(2,1)} %get-tuple-element.21.own_ref, bf16[4352,128]{1,0:T(8,128)(2,1)} %copy-done.4, bf16[128,64]{1,0:T(8,128)(2,1)} %copy.14.eval_ref), custom_call_target="tpu_custom_call" | custom-call | tf_op jit(solution)/shard_map/pallas_call | solution.py:216
  (14 shorter events, 0.0 us)
Async XLA Ops:
  1.1 7.3 %collective-permute-start = (bf16[6,64,128]{2,1,0:T(8,128)(2,1)S(1)}, bf16[6,64,128]{2,1,0:T(8,128)(2,1)S(1)}, u32[]{:S(2)}, u32[]{:S(2)}) collective-permute-start(bf16[6,64,128]{2,1,0:T(8,128)(2,1)S(1)} %pad_maximum_fusion.2), channel_id=1, source_target_pairs={{0,0},{1,17},{2,34},{3,51},{4,4},{5,21},{6,38},{7,55},{8,8},{9,25}... | collective-permute-start | bytes 294920 | tf_op jit(solution)/shard_map/ppermute | solution.py:237
  1.7 6.6 %collective-permute-start.1 = (bf16[6,64,128]{2,1,0:T(8,128)(2,1)S(1)}, bf16[6,64,128]{2,1,0:T(8,128)(2,1)S(1)}, u32[]{:S(2)}, u32[]{:S(2)}) collective-permute-start(bf16[6,64,128]{2,1,0:T(8,128)(2,1)S(1)} %pad_maximum_fusion.2), channel_id=1, source_target_pairs={{0,8},{1,25},{2,42},{3,59},{4,12},{5,29},{6,46},{7,63},{8,0},{9,17... | collective-permute-start | bytes 294920 | tf_op jit(solution)/shard_map/ppermute | solution.py:237
  8.4 12.5 %collective-permute-start.2 = (bf16[6,2,64,128]{3,2,1,0:T(8,128)(2,1)S(1)}, bf16[6,2,64,128]{3,2,1,0:T(8,128)(2,1)S(1)}, u32[]{:S(2)}, u32[]{:S(2)}) collective-permute-start(bf16[6,2,64,128]{3,2,1,0:T(8,128)(2,1)S(1)} %pad_maximum_fusion.1), channel_id=1, source_target_pairs={{0,64},{4,68},{8,72},{12,76},{16,80},{20,84},{24,88},{28,92},{32,9... | collective-permute-start | bytes 589832 | tf_op jit(solution)/shard_map/ppermute | solution.py:231
  9.7 11.2 %collective-permute-start.3 = (bf16[6,2,64,128]{3,2,1,0:T(8,128)(2,1)S(1)}, bf16[6,2,64,128]{3,2,1,0:T(8,128)(2,1)S(1)}, u32[]{:S(2)}, u32[]{:S(2)}) collective-permute-start(bf16[6,2,64,128]{3,2,1,0:T(8,128)(2,1)S(1)} %pad_maximum_fusion.1), channel_id=1, source_target_pairs={{0,128},{4,132},{8,136},{12,140},{16,144},{20,148},{24,152},{28,15... | collective-permute-start | bytes 589832 | tf_op jit(solution)/shard_map/ppermute | solution.py:231
  12.2 11.3 %collective-permute-start.4 = (bf16[6,2,64,128]{3,2,1,0:T(8,128)(2,1)S(1)}, bf16[6,2,64,128]{3,2,1,0:T(8,128)(2,1)S(1)}, u32[]{:S(2)}, u32[]{:S(2)}) collective-permute-start(bf16[6,2,64,128]{3,2,1,0:T(8,128)(2,1)S(1)} %pad_maximum_fusion.1), channel_id=1, source_target_pairs={{0,192},{4,196},{8,200},{12,204},{16,208},{20,212},{24,216},{28,22... | collective-permute-start | bytes 589832 | tf_op jit(solution)/shard_map/ppermute | solution.py:231
  23.4 47.3 %all-to-all-start = ((bf16[32,144,128]{2,1,0:T(8,128)(2,1)}), bf16[32,144,128]{2,1,0:T(8,128)(2,1)S(1)}, u32[]{:S(2)}, u32[]{:S(2)}) async-start(bf16[32,144,128]{2,1,0:T(8,128)(2,1)} %shard_map.65), calls=%async_computation | async-start | bytes 2359296 | tf_op jit(solution)/shard_map/all_to_all | solution.py:254
  31.2 39.5 %copy-start.1 = (bf16[6,4,2,64,128]{4,3,2,1,0:T(8,128)(2,1)}, bf16[6,4,2,64,128]{4,3,2,1,0:T(8,128)(2,1)S(1)}, u32[]{:S(2)}) copy-start(bf16[6,4,2,64,128]{4,3,2,1,0:T(8,128)(2,1)S(1)} %pad_maximum_fusion.q0_ref) | copy-start | bytes 2359300
  31.2 27.4 %collective-permute-start.6 = (bf16[6,4,2,64,128]{4,3,2,1,0:T(8,128)(2,1)S(1)}, bf16[6,4,2,64,128]{4,3,2,1,0:T(8,128)(2,1)S(1)}, u32[]{:S(2)}, u32[]{:S(2)}) collective-permute-start(bf16[6,4,2,64,128]{4,3,2,1,0:T(8,128)(2,1)S(1)} %pad_maximum_fusion.q0_ref), channel_id=1, source_target_pairs={{0,3},{1,2},{2,1},{3,0},{4,7},{5,6},{6,5},{7,4},{8,11},{9,10},{10,... | collective-permute-start | bytes 2359304 | tf_op jit(solution)/shard_map/ppermute | solution.py:240
  42.6 17.9 %collective-permute-start.5 = (bf16[6,4,2,64,128]{4,3,2,1,0:T(8,128)(2,1)S(1)}, bf16[6,4,2,64,128]{4,3,2,1,0:T(8,128)(2,1)S(1)}, u32[]{:S(2)}, u32[]{:S(2)}) collective-permute-start(bf16[6,4,2,64,128]{4,3,2,1,0:T(8,128)(2,1)S(1)} %pad_maximum_fusion.q0_ref), channel_id=1, source_target_pairs={{0,1},{1,0},{2,3},{3,2},{4,5},{5,4},{6,7},{7,6},{8,9},{9,8},{10,11... | collective-permute-start | bytes 2359304 | tf_op jit(solution)/shard_map/ppermute | solution.py:240
  58.7 12.1 %copy-start.2 = (bf16[6,4,2,64,128]{4,3,2,1,0:T(8,128)(2,1)}, bf16[6,4,2,64,128]{4,3,2,1,0:T(8,128)(2,1)S(1)}, u32[]{:S(2)}) copy-start(bf16[6,4,2,64,128]{4,3,2,1,0:T(8,128)(2,1)S(1)} %collective-permute-done.6.q3_ref) | copy-start | bytes 2359300
  59.5 8.5 %collective-permute-start.7 = (bf16[3,4,2,64,128]{4,3,2,1,0:T(8,128)(2,1)}, bf16[3,4,2,64,128]{4,3,2,1,0:T(8,128)(2,1)}, u32[]{:S(2)}, u32[]{:S(2)}) collective-permute-start(bf16[3,4,2,64,128]{4,3,2,1,0:T(8,128)(2,1)} %slice.16), channel_id=1, source_target_pairs={{0,1},{1,0},{2,3},{3,2},{4,5},{5,4},{6,7},{7,6},{8,9},{9,8},{10,11... | collective-permute-start | bytes 1179656 | tf_op jit(solution)/shard_map/ppermute | solution.py:240
  60.5 10.3 %copy-start.3 = (bf16[6,4,2,64,128]{4,3,2,1,0:T(8,128)(2,1)}, bf16[6,4,2,64,128]{4,3,2,1,0:T(8,128)(2,1)S(1)}, u32[]{:S(2)}) copy-start(bf16[6,4,2,64,128]{4,3,2,1,0:T(8,128)(2,1)S(1)} %collective-permute-done.5.q1_ref) | copy-start | bytes 2359300
  61.3 9.4 %collective-permute-start.8 = (bf16[3,4,2,64,128]{4,3,2,1,0:T(8,128)(2,1)}, bf16[3,4,2,64,128]{4,3,2,1,0:T(8,128)(2,1)}, u32[]{:S(2)}, u32[]{:S(2)}) collective-permute-start(bf16[3,4,2,64,128]{4,3,2,1,0:T(8,128)(2,1)} %slice.17), channel_id=1, source_target_pairs={{0,3},{1,2},{2,1},{3,0},{4,7},{5,6},{6,5},{7,4},{8,11},{9,10},{10,... | collective-permute-start | bytes 1179656 | tf_op jit(solution)/shard_map/ppermute | solution.py:240
  63.7 17.9 %copy-start.5 = (bf16[128,64]{0,1:T(8,128)(2,1)S(1)}, bf16[128,64]{0,1:T(8,128)(2,1)}, u32[]{:S(2)}) copy-start(bf16[128,64]{0,1:T(8,128)(2,1)} %param.11) | copy-start | bytes 49156
  70.8 1.0 %copy-start = (bf16[32,144,128]{2,1,0:T(8,128)(2,1)}, bf16[32,144,128]{2,1,0:T(8,128)(2,1)S(1)}, u32[]{:S(2)}) copy-start(bf16[32,144,128]{2,1,0:T(8,128)(2,1)S(1)} %all-to-all-done.data_ref) | copy-start | bytes 3538948
  77.9 6.3 %collective-permute-start.9 = (bf16[4352,128]{1,0:T(8,128)(2,1)}, bf16[4352,128]{1,0:T(8,128)(2,1)S(1)}, u32[]{:S(2)}, u32[]{:S(2)}) collective-permute-start(bf16[4352,128]{1,0:T(8,128)(2,1)} %get-tuple-element.22), channel_id=1, source_target_pairs={{0,4},{4,0},{8,12},{12,8},{16,20},{20,16},{24,28},{28,24},{32,36},... | collective-permute-start | bytes 3342344 | tf_op jit(solution)/shard_map/ppermute | solution.py:231
  84.2 1.0 %copy-start.4 = (bf16[4352,128]{1,0:T(8,128)(2,1)}, bf16[4352,128]{1,0:T(8,128)(2,1)S(1)}, u32[]{:S(2)}) copy-start(bf16[4352,128]{1,0:T(8,128)(2,1)S(1)} %collective-permute-done.9.oth_ref) | copy-start | bytes 3342340

commit v3 on v2

--- a/solution.py
+++ b/solution.py
@@ -16,7 +16,19 @@
 BLOCKS = NX * NZ
 ROWS = 2 * R + 16
 PARAMS = pltpu.CompilerParams(vmem_limit_bytes=60 * 2**20)
+SMALL = pltpu.CompilerParams(vmem_limit_bytes=24 * 2**20)
 SLOTS = [(j, t, i) for j in range(NX) for t in range(PLANES) for i in range(2)]
+
+
+def place():
+    box = lax.axis_index("box")
+    return box // (NZ * NC), box // NC % NZ, box % NC, lax.axis_index("src")
+
+
+def block_of(slot):
+    x, z, _, plane = place()
+    j, t, i = slot
+    return (x ^ j) * NZ + (z ^ (((plane ^ t) << 1) | i))
 
 
 def dot(a, b):
@@ -133,30 +145,33 @@
     )(*args)
 
 
-def chip_kernel(at_ref, data_ref, q0_ref, q1_ref, q2lo_ref, q2hi_ref, q3_ref, keep_ref, send_ref, mats_ref, sems):
-    early, late = pl.ds(0, 3), pl.ds(3, 3)
-    pieces = [(t, part, ref.at[part]) for part in (early, late) for t, ref in ((0, q0_ref), (1, q1_ref), (3, q3_ref))]
-    pieces += [(2, early, q2lo_ref), (2, late, q2hi_ref)]
+def chip_kernel(data_ref, *refs):
+    keep_ref, send_ref, mats_ref, sems = refs[-4:]
     copies = [
-        pltpu.make_async_copy(ref, mats_ref.at[t, part], sems.at[n]) for n, (t, part, ref) in enumerate(pieces)
+        [
+            pltpu.make_async_copy(refs[p * PLANES + t], mats_ref.at[t, p], sems.at[p, t])
+            for t in range(PLANES)
+        ]
+        for p in range(2)
     ]
-    for copy in copies:
+    for copy in copies[0] + copies[1]:
         copy.start()
-    low = at_ref[0] == 0
+    low = place()[2] == 0
     x, cs, last = {}, {}, {}
-    for n, slot in enumerate(SLOTS):
-        block = at_ref[1 + n]
+    for slot in SLOTS:
+        block = block_of(slot)
         x[slot] = jnp.concatenate([data_ref[block, :R], data_ref[block, R : 2 * R]], axis=1)
         a = data_ref[block, 2 * R :].astype(F32)
         cs[slot] = cos_sin(jnp.concatenate([a[:8], a[8:]], axis=1))
         last[slot] = (a[:8], a[8:])
-    for copy in copies:
-        copy.wait()
     flips = ((2, 0, 0), (1, 0, 0), (0, 2, 0), (0, 1, 0), (0, 0, 1))
     for level, flip in enumerate(flips):
+        if level % 3 == 0:
+            for copy in copies[level // 3]:
+                copy.wait()
         x = {
             (j, t, i): mix(
-                mats_ref[t, level, j, i],
+                mats_ref[t, level // 3, j, level % 3, i],
                 x[j, t, i],
                 x[j ^ flip[0], t ^ flip[1], i ^ flip[2]],
                 row(cs[j, t, i][0], level),
@@ -177,25 +192,25 @@
         send_ref[at : at + 16] = jnp.where(low, hi, lo).astype(BF)
     for n, (j, t, i) in enumerate(SLOTS):
         at = BLOCKS * (R + 8) + n * R
-        keep_ref[at : at + R] = mats_ref[t, 5, j, i]
-        send_ref[at : at + R] = mats_ref[t, 5, j, i]
-
-
-def chip_levels(at, moved, mats):
+        keep_ref[at : at + R] = mats_ref[t, 1, j, 2, i]
+        send_ref[at : at + R] = mats_ref[t, 1, j, 2, i]
+
+
+def chip_levels(moved, early, late):
     out = jax.ShapeDtypeStruct((BLOCKS * (2 * R + 8), 128), BF)
     vmem = pl.BlockSpec(memory_space=pltpu.VMEM)
     return pl.pallas_call(
         chip_kernel,
-        in_specs=[pl.BlockSpec(memory_space=pltpu.SMEM), vmem] + [pl.BlockSpec(memory_space=pltpu.HBM)] * 5,
+        in_specs=[vmem] + [pl.BlockSpec(memory_space=pl.ANY)] * 8,
         out_specs=[vmem, vmem],
         out_shape=[out, out],
-        scratch_shapes=[pltpu.VMEM((PLANES, 6, NX, 2, R, 2 * R), BF), pltpu.SemaphoreType.DMA((8,))],
-        compiler_params=PARAMS,
-    )(at, moved, *mats)
-
-
-def last_kernel(at_ref, own_ref, oth_ref, eval_ref, out_ref):
-    low = at_ref[0] == 0
+        scratch_shapes=[pltpu.VMEM((PLANES, 2, NX, 3, 2, R, 2 * R), BF), pltpu.SemaphoreType.DMA((2, PLANES))],
+        compiler_params=SMALL,
+    )(moved, *early, *late)
+
+
+def last_kernel(own_ref, oth_ref, eval_ref, out_ref):
+    low = place()[2] == 0
     ev = eval_ref[...]
     for n in range(BLOCKS):
         if n % 2 == 0:
@@ -207,33 +222,31 @@
         y_own = mix(own_ref[m : m + R], own, oth, row(own_c, r), row(own_s, r))
         y_oth = mix(oth_ref[m : m + R], oth, own, row(oth_c, r), row(oth_s, r))
         y = jnp.concatenate([jnp.where(low, y_own, y_oth), jnp.where(low, y_oth, y_own)], axis=1)
-        column = pl.multiple_of(at_ref[1 + n] * TILE, TILE)
-        out_ref[:, pl.ds(column, TILE)] = dot(ev, y).astype(BF)
-
-
-def last_level(at, keep, received, evaluate_mats):
+        column = pl.multiple_of(block_of(SLOTS[n]) * TILE, TILE)
+        out_ref[:, pl.ds(column, TILE)] = lax.dot_general(
+            ev, y, (((0,), (0,)), ((), ())), preferred_element_type=F32
+        ).astype(BF)
+
+
+def last_level(keep, received, evaluate_mats):
     vmem = pl.BlockSpec(memory_space=pltpu.VMEM)
     return pl.pallas_call(
         last_kernel,
-        in_specs=[pl.BlockSpec(memory_space=pltpu.SMEM)] + [vmem] * 3,
+        in_specs=[vmem] * 3,
         out_specs=vmem,
-        out_shape=jax.ShapeDtypeStruct((evaluate_mats.shape[0], 64 * 128), BF),
-        compiler_params=PARAMS,
-    )(at, keep, received, evaluate_mats)
+        out_shape=jax.ShapeDtypeStruct((evaluate_mats.shape[1], 64 * 128), BF),
+        compiler_params=SMALL,
+    )(keep, received, evaluate_mats)
 
 
 def shards(source_field, project_mats, local_mats, cross_mats, angles, evaluate_mats):
-    box, plane = lax.axis_index("box"), lax.axis_index("src")
-    x, z, core = box // (NZ * NC), box // NC % NZ, box % NC
     count = NX * NZ * NC
 
     def swap(values, distance):
         return lax.ppermute(values, "box", [(i, i ^ distance) for i in range(count)])
 
-    def along_z(values, n):
-        pairs = [
-            (i * PLANES + p, (i ^ ((2 * p + n) * NC)) * PLANES + p) for i in range(count) for p in range(PLANES)
-        ]
+    def to_plane(values):
+        pairs = [(i * PLANES + p, (i ^ (2 * p * NC)) * PLANES + p) for i in range(count) for p in range(PLANES)]
         return lax.ppermute(values, ("box", "src"), pairs)
 
     def along_src(values, t):
@@ -245,22 +258,22 @@
     chips = [[xx * NZ * NC + zz * NC + c for xx in range(NX) for zz in range(NZ)] for c in range(NC)]
 
     own = jnp.concatenate([cross_mats[:, 0], cross_mats[:, 1]], axis=-1)
-    pair = [along_z(own, n) for n in (0, 1)]
+    far = to_plane(own)
     first = local_levels(1, 0, None, source_field, angles, project_mats, local_mats)
-    pair = jnp.stack([after(pair[0], first), pair[1]], axis=1)
+    far = after(far, first)
+    pair = jnp.stack([far, swap(far, NC)], axis=1)
     quarter = [pair] + [swap(pair, j * NZ * NC) for j in (1, 2, 3)]
     sent = local_levels(3, 1, after(first, pair), source_field, angles, project_mats, local_mats)
     sent, *quarter = lax.optimization_barrier((sent, *quarter))
     moved = lax.all_to_all(sent, "box", 0, 0, tiled=True, axis_index_groups=chips)
-    quarter = jnp.stack(quarter, axis=1)
-    q1, q3 = along_src(quarter, 1), along_src(quarter, 3)
-    mats = [quarter, q1, along_src(q3[:3], 1), along_src(q1[3:], 3), q3]
-
-    blocks = [(x ^ j) * NZ + (z ^ (((plane ^ t) << 1) | i)) for j, t, i in SLOTS]
-    at = jnp.stack([core] + blocks).astype(jnp.int32)
-    keep, send = chip_levels(at, moved, mats)
+    early, late = (jnp.stack([q[p : p + 3] for q in quarter]) for p in (0, 3))
+    early3, late1 = along_src(early, 3), along_src(late, 1)
+    early1, late3 = along_src(early, 1), along_src(late, 3)
+    early2, late2 = along_src(early3, 1), along_src(late1, 3)
+
+    keep, send = chip_levels(moved, (early, early1, early2, early3), (late, late1, late2, late3))
     received = swap(send, 1)
-    return last_level(at, keep, received, evaluate_mats)
+    return last_level(keep, received, evaluate_mats.T)
 
 
 def solution(mesh):

time: 89.9 us -> 82.6 us (0.919)
  Pallas kernels: 23.1 us -> 19.1 us
  local copies, waits for them, and re-layouts: 5.95 us -> 4.51 us
  waiting for transfers between devices: 26.5 us -> 25.5 us
    ppermute x4 -> x6, starting transfers between devices: 15.1 us -> 10.8 us  [along_src(): return lax.ppermute(values, 'src', [(p, p ^ t) for p in range(PLANES)])]
    pallas_call x2, Pallas kernels: 10.5 us -> 6.56 us  [the longest x1 3.72 us: chip_levels(): pl.pallas_call(chip_kernel, in_specs=[vmem] + [pl.BlockSpec(memory_space=...]
    ppermute x4 -> x5, starting transfers between devices: 7.64 us -> 10.7 us  [swap(): lax.ppermute(values, 'box', [(i, i ^ distance) for i in range(count)])]
    all_to_all x1, starting transfers between devices: 7.69 us -> 10.6 us  [shards(): lax.all_to_all(sent, 'box', 0, 0, tiled=True, axis_index_groups=chips)]
    ppermute x2 -> x1, starting transfers between devices: 3.22 us -> 0.67 us  [to_plane(): return lax.ppermute(values, ('box', 'src'), pairs)]
    slice x2 -> x0, local copies, waits for them, and re-layouts: 1.64 us -> none  [shards(): mats = [quarter, q1, along_src(q3[:3], 1), along_src(q1[3:], 3), q3]]
    ppermute x4 -> x6, waiting for transfers between devices: 22.1 us -> 21.1 us  [along_src(): return lax.ppermute(values, 'src', [(p, p ^ t) for p in range(PLANES)])]
    unnamed x13 -> x10, local copies, waits for them, and re-layouts: 2.71 us -> 3.5 us
  transfers between devices with their start and end apart: 11 -> 13, of which waited for: 5 -> 6; matrix products, arithmetic and copies ran while one was open for 3% -> 0% of each run, Pallas kernels for 14% -> 15%
where the time goes in v3:
time: 82.6 us; the launch traced here: 82.3 us
  starting transfers between devices  32.8 us (40%)
  waiting for transfers between devices  25.5 us (31%)
  Pallas kernels  19.1 us (23%)
  local copies, waits for them, and re-layouts  4.51 us (5%)
    ppermute x6, waiting for transfers between devices, along_src(): return lax.ppermute(values, 'src', [(p, p ^ t) for p in range(PLANES)])  21.1 us
    pallas_call x2, Pallas kernels, local_levels(): pl.pallas_call(functools.partial(local_kernel, start), grid=(steps,), in_...  12.6 us
    ppermute x6, starting transfers between devices, along_src(): return lax.ppermute(values, 'src', [(p, p ^ t) for p in range(PLANES)])  10.8 us
    ppermute x5, starting transfers between devices, swap(): lax.ppermute(values, 'box', [(i, i ^ distance) for i in range(count)])  10.7 us
    all_to_all x1, starting transfers between devices, shards(): lax.all_to_all(sent, 'box', 0, 0, tiled=True, axis_index_groups=chips)  10.6 us
    ppermute x5, waiting for transfers between devices, swap(): lax.ppermute(values, 'box', [(i, i ^ distance) for i in range(count)])  4.4 us
    pallas_call x1, Pallas kernels, chip_levels(): pl.pallas_call(chip_kernel, in_specs=[vmem] + [pl.BlockSpec(memory_space=...  3.72 us
    unnamed x10, local copies, waits for them, and re-layouts  3.5 us
  transfers between devices with their start and end apart: 13, of which 6 were waited for; matrix products, arithmetic and copies ran while one was open for 0% of the time, Pallas kernels for 15%

profile of v3, /device:TPU:1, one launch (start us, length us, event | category | flops | bytes accessed | tf_op | source)
XLA Modules:
  0.0 82.3 jit_solution(17513348779452242029)
XLA Ops:
  0.0 1.0 %slice_bitcast_fusion.9 = (bf16[6,64,64]{2,1,0:T(8,128)(2,1)S(1)}, bf16[6,64,64]{2,1,0:T(8,128)(2,1)S(1)}) fusion(bf16[6,2,64,64]{3,2,1,0:T(8,128)(2,1)} %param.9), kind=kLoop, calls=%fused_computation.13 | loop fusion | bytes 196608 | tf_op jit(solution)/shard_map/squeeze | solution.py:260
  1.0 0.1 pad_maximum_fusion.3
  1.1 0.7 collective-permute-start
  1.7 4.1 %shard_map.64.refs_0_ = bf16[32,144,128]{2,1,0:T(8,128)(2,1)} custom-call(bf16[128,8192]{1,0:T(8,128)(2,1)} %src_any.3, bf16[14,8192]{1,0:T(8,128)(2,1)} %ang_any.3, bf16[64,128]{1,0:T(8,128)(2,1)} %proj_any.3, bf16[8,2,64,64]{3,2,1,0:T(8,128)(2,1)} %mats_any.3), custom_call_target="tpu_custom_call" | custom-call | tf_op jit(solution)/shard_map/pallas_call | solution.py:130
  5.8 2.5 %collective-permute-start.1 = (bf16[6,64,128]{2,1,0:T(8,128)(2,1)S(1)}, bf16[6,64,128]{2,1,0:T(8,128)(2,1)S(1)}, u32[]{:S(2)}, u32[]{:S(2)}) collective-permute-start(bf16[6,64,128]{2,1,0:T(8,128)(2,1)S(1)} %collective-permute-done), channel_id=1, source_target_pairs={{0,8},{4,12},{8,0},{12,4},{16,24},{20,28},{24,16},{28,20},{32,40},... | collective-permute-start | bytes 294920 | tf_op jit(solution)/shard_map/ppermute | solution.py:246
  8.4 2.0 %collective-permute-done.1 = bf16[6,64,128]{2,1,0:T(8,128)(2,1)S(1)} collective-permute-done((bf16[6,64,128]{2,1,0:T(8,128)(2,1)S(1)}, bf16[6,64,128]{2,1,0:T(8,128)(2,1)S(1)}, u32[]{:S(2)}, u32[]{:S(2)}) %collective-permute-start.1) | collective-permute-done | bytes 98336 | tf_op jit(solution)/shard_map/ppermute | solution.py:246
  10.4 3.0 %collective-permute-start.4 = (bf16[6,2,64,128]{3,2,1,0:T(8,128)(2,1)S(1)}, bf16[6,2,64,128]{3,2,1,0:T(8,128)(2,1)S(1)}, u32[]{:S(2)}, u32[]{:S(2)}) collective-permute-start(bf16[6,2,64,128]{3,2,1,0:T(8,128)(2,1)S(1)} %pad_maximum_fusion.2), channel_id=1, source_target_pairs={{0,192},{4,196},{8,200},{12,204},{16,208},{20,212},{24,216},{28,22... | collective-permute-start | bytes 589832 | tf_op jit(solution)/shard_map/ppermute | solution.py:246
  13.4 0.5 collective-permute-start.3
  13.9 0.2 collective-permute-start.2
  14.1 8.5 %shard_map.65 = bf16[32,144,128]{2,1,0:T(8,128)(2,1)} custom-call(bf16[128,8192]{1,0:T(8,128)(2,1)} %src_any.3, bf16[14,8192]{1,0:T(8,128)(2,1)} %ang_any.3, bf16[64,128]{1,0:T(8,128)(2,1)} %proj_any.3, bf16[8,2,64,64]{3,2,1,0:T(8,128)(2,1)} %mats_any.3, bf16[32,144,128]{2,1,0:T(8,128)(2,1)} %shard_map.64.refs_0_), custom_call_target="tpu_custom_call", output_to_operand_aliasing={{}: (4, {})} | custom-call | tf_op jit(solution)/shard_map/pallas_call | solution.py:130
  22.6 0.0 collective-permute-done.4
  22.6 0.0 collective-permute-done.2
  22.6 10.6 %all-to-all-start = ((bf16[32,144,128]{2,1,0:T(8,128)(2,1)}), bf16[32,144,128]{2,1,0:T(8,128)(2,1)S(1)}, u32[]{:S(2)}, u32[]{:S(2)}) async-start(bf16[32,144,128]{2,1,0:T(8,128)(2,1)} %shard_map.65), calls=%async_computation | async-start | bytes 2359296 | tf_op jit(solution)/shard_map/all_to_all | solution.py:268
  33.3 0.1 pad_maximum_fusion.refs_0_
  33.3 7.9 %collective-permute-start.6 = (bf16[4,3,2,64,128]{4,3,2,1,0:T(8,128)(2,1)S(1)}, bf16[4,3,2,64,128]{4,3,2,1,0:T(8,128)(2,1)S(1)}, u32[]{:S(2)}, u32[]{:S(2)}) collective-permute-start(bf16[4,3,2,64,128]{4,3,2,1,0:T(8,128)(2,1)S(1)} %pad_maximum_fusion.refs_0_), channel_id=1, source_target_pairs={{0,3},{1,2},{2,1},{3,0},{4,7},{5,6},{6,5},{7,4},{8,11},{9,10},{10,... | collective-permute-start | bytes 1179656 | tf_op jit(solution)/shard_map/ppermute | solution.py:253
  41.2 0.1 pad_maximum_fusion.1.refs_4_
  41.3 0.7 collective-permute-start.8
  42.0 0.9 %collective-permute-start.5 = (bf16[4,3,2,64,128]{4,3,2,1,0:T(8,128)(2,1)S(1)}, bf16[4,3,2,64,128]{4,3,2,1,0:T(8,128)(2,1)S(1)}, u32[]{:S(2)}, u32[]{:S(2)}) collective-permute-start(bf16[4,3,2,64,128]{4,3,2,1,0:T(8,128)(2,1)S(1)} %pad_maximum_fusion.refs_0_), channel_id=1, source_target_pairs={{0,1},{1,0},{2,3},{3,2},{4,5},{5,4},{6,7},{7,6},{8,9},{9,8},{10,11... | collective-permute-start | bytes 1179656 | tf_op jit(solution)/shard_map/ppermute | solution.py:253
  42.8 0.0 collective-permute-start.10
  42.9 4.6 %collective-permute-done.6.refs_3_ = bf16[4,3,2,64,128]{4,3,2,1,0:T(8,128)(2,1)S(1)} collective-permute-done((bf16[4,3,2,64,128]{4,3,2,1,0:T(8,128)(2,1)S(1)}, bf16[4,3,2,64,128]{4,3,2,1,0:T(8,128)(2,1)S(1)}, u32[]{:S(2)}, u32[]{:S(2)}) %collective-permute-start.6) | collective-permute-done | bytes 393248 | tf_op jit(solution)/shard_map/ppermute | solution.py:253
  47.4 1.0 %collective-permute-done.8.refs_5_ = bf16[4,3,2,64,128]{4,3,2,1,0:T(8,128)(2,1)S(1)} collective-permute-done((bf16[4,3,2,64,128]{4,3,2,1,0:T(8,128)(2,1)S(1)}, bf16[4,3,2,64,128]{4,3,2,1,0:T(8,128)(2,1)S(1)}, u32[]{:S(2)}, u32[]{:S(2)}) %collective-permute-start.8) | collective-permute-done | bytes 393248 | tf_op jit(solution)/shard_map/ppermute | solution.py:253
  48.5 1.4 %collective-permute-start.9 = (bf16[4,3,2,64,128]{4,3,2,1,0:T(8,128)(2,1)S(1)}, bf16[4,3,2,64,128]{4,3,2,1,0:T(8,128)(2,1)S(1)}, u32[]{:S(2)}, u32[]{:S(2)}) collective-permute-start(bf16[4,3,2,64,128]{4,3,2,1,0:T(8,128)(2,1)S(1)} %collective-permute-done.8.refs_5_), channel_id=1, source_target_pairs={{0,3},{1,2},{2,1},{3,0},{4,7},{5,6},{6,5},{7,4},{8,11},{9,10},{10,... | collective-permute-start | bytes 1179656 | tf_op jit(solution)/shard_map/ppermute | solution.py:253
  49.8 7.1 %collective-permute-done.5.refs_1_ = bf16[4,3,2,64,128]{4,3,2,1,0:T(8,128)(2,1)S(1)} collective-permute-done((bf16[4,3,2,64,128]{4,3,2,1,0:T(8,128)(2,1)S(1)}, bf16[4,3,2,64,128]{4,3,2,1,0:T(8,128)(2,1)S(1)}, u32[]{:S(2)}, u32[]{:S(2)}) %collective-permute-start.5) | collective-permute-done | bytes 393248 | tf_op jit(solution)/shard_map/ppermute | solution.py:253
  56.9 8.4 %collective-permute-done.7.refs_2_ = bf16[4,3,2,64,128]{4,3,2,1,0:T(8,128)(2,1)S(1)} collective-permute-done((bf16[4,3,2,64,128]{4,3,2,1,0:T(8,128)(2,1)S(1)}, bf16[4,3,2,64,128]{4,3,2,1,0:T(8,128)(2,1)S(1)}, u32[]{:S(2)}, u32[]{:S(2)}) %collective-permute-start.7) | collective-permute-done | bytes 393248 | tf_op jit(solution)/shard_map/ppermute | solution.py:253
  65.3 0.8 copy-done
  66.1 0.7 copy-done.2
  66.8 1.0 %copy-done.1 = bf16[4,3,2,64,128]{4,3,2,1,0:T(8,128)(2,1)S(1)} copy-done((bf16[4,3,2,64,128]{4,3,2,1,0:T(8,128)(2,1)S(1)}, bf16[4,3,2,64,128]{4,3,2,1,0:T(8,128)(2,1)}, u32[]{:S(2)}) %copy-start.1) | copy-done | bytes 393240
  67.8 1.0 %copy-done.3 = bf16[4,3,2,64,128]{4,3,2,1,0:T(8,128)(2,1)S(1)} copy-done((bf16[4,3,2,64,128]{4,3,2,1,0:T(8,128)(2,1)S(1)}, bf16[4,3,2,64,128]{4,3,2,1,0:T(8,128)(2,1)}, u32[]{:S(2)}) %copy-start.3) | copy-done | bytes 393240
  68.8 3.7 %shard_map.66 = (bf16[4352,128]{1,0:T(8,128)(2,1)S(1)}, bf16[4352,128]{1,0:T(8,128)(2,1)S(1)}) custom-call(bf16[32,144,128]{2,1,0:T(8,128)(2,1)S(1)} %all-to-all-done.data_ref, bf16[4,3,2,64,128]{4,3,2,1,0:T(8,128)(2,1)S(1)} %pad_maximum_fusion.refs_0_, bf16[4,3,2,64,128]{4,3,2,1,0:T(8,128)(2,1)S(1)} %collective-permute-done.5.refs_1_, ...), custom_call_target="tpu_custom_call" | custom-call | tf_op jit(solution)/shard_map/pallas_call | solution.py:202
  72.5 4.5 %collective-permute-start.11 = (bf16[4352,128]{1,0:T(8,128)(2,1)S(1)}, bf16[4352,128]{1,0:T(8,128)(2,1)S(1)}, u32[]{:S(2)}, u32[]{:S(2)}) collective-permute-start(bf16[4352,128]{1,0:T(8,128)(2,1)S(1)} %get-tuple-element.22), channel_id=1, source_target_pairs={{0,4},{4,0},{8,12},{12,8},{16,20},{20,16},{24,28},{28,24},{32,36},... | collective-permute-start | bytes 3342344 | tf_op jit(solution)/shard_map/ppermute | solution.py:246
  77.1 2.4 %collective-permute-done.11.oth_ref = bf16[4352,128]{1,0:T(8,128)(2,1)S(1)} collective-permute-done((bf16[4352,128]{1,0:T(8,128)(2,1)S(1)}, bf16[4352,128]{1,0:T(8,128)(2,1)S(1)}, u32[]{:S(2)}, u32[]{:S(2)}) %collective-permute-start.11) | collective-permute-done | bytes 1114144 | tf_op jit(solution)/shard_map/ppermute | solution.py:246
  79.4 2.8 %shard_map.67 = bf16[128,8192]{1,0:T(8,128)(2,1)} custom-call(bf16[4352,128]{1,0:T(8,128)(2,1)S(1)} %get-tuple-element.21.own_ref, bf16[4352,128]{1,0:T(8,128)(2,1)S(1)} %collective-permute-done.11.oth_ref, bf16[64,128]{1,0:T(8,128)(2,1)S(1)} %bitcast.29), custom_call_target="tpu_custom_call" | custom-call | tf_op jit(solution)/shard_map/pallas_call | solution.py:233
  (15 shorter events, 0.1 us)
Async XLA Ops:
  1.1 4.8 %collective-permute-start = (bf16[6,64,128]{2,1,0:T(8,128)(2,1)S(1)}, bf16[6,64,128]{2,1,0:T(8,128)(2,1)S(1)}, u32[]{:S(2)}, u32[]{:S(2)}) collective-permute-start(bf16[6,64,128]{2,1,0:T(8,128)(2,1)S(1)} %pad_maximum_fusion.3), channel_id=1, source_target_pairs={{0,0},{1,17},{2,34},{3,51},{4,4},{5,21},{6,38},{7,55},{8,8},{9,25}... | collective-permute-start | bytes 294920 | tf_op jit(solution)/shard_map/ppermute | solution.py:250
  5.8 4.6 %collective-permute-start.1 = (bf16[6,64,128]{2,1,0:T(8,128)(2,1)S(1)}, bf16[6,64,128]{2,1,0:T(8,128)(2,1)S(1)}, u32[]{:S(2)}, u32[]{:S(2)}) collective-permute-start(bf16[6,64,128]{2,1,0:T(8,128)(2,1)S(1)} %collective-permute-done), channel_id=1, source_target_pairs={{0,8},{4,12},{8,0},{12,4},{16,24},{20,28},{24,16},{28,20},{32,40},... | collective-permute-start | bytes 294920 | tf_op jit(solution)/shard_map/ppermute | solution.py:246
  10.4 12.2 %collective-permute-start.4 = (bf16[6,2,64,128]{3,2,1,0:T(8,128)(2,1)S(1)}, bf16[6,2,64,128]{3,2,1,0:T(8,128)(2,1)S(1)}, u32[]{:S(2)}, u32[]{:S(2)}) collective-permute-start(bf16[6,2,64,128]{3,2,1,0:T(8,128)(2,1)S(1)} %pad_maximum_fusion.2), channel_id=1, source_target_pairs={{0,192},{4,196},{8,200},{12,204},{16,208},{20,212},{24,216},{28,22... | collective-permute-start | bytes 589832 | tf_op jit(solution)/shard_map/ppermute | solution.py:246
  13.4 9.2 %collective-permute-start.3 = (bf16[6,2,64,128]{3,2,1,0:T(8,128)(2,1)S(1)}, bf16[6,2,64,128]{3,2,1,0:T(8,128)(2,1)S(1)}, u32[]{:S(2)}, u32[]{:S(2)}) collective-permute-start(bf16[6,2,64,128]{3,2,1,0:T(8,128)(2,1)S(1)} %pad_maximum_fusion.2), channel_id=1, source_target_pairs={{0,128},{4,132},{8,136},{12,140},{16,144},{20,148},{24,152},{28,15... | collective-permute-start | bytes 589832 | tf_op jit(solution)/shard_map/ppermute | solution.py:246
  13.9 8.7 %collective-permute-start.2 = (bf16[6,2,64,128]{3,2,1,0:T(8,128)(2,1)S(1)}, bf16[6,2,64,128]{3,2,1,0:T(8,128)(2,1)S(1)}, u32[]{:S(2)}, u32[]{:S(2)}) collective-permute-start(bf16[6,2,64,128]{3,2,1,0:T(8,128)(2,1)S(1)} %pad_maximum_fusion.2), channel_id=1, source_target_pairs={{0,64},{4,68},{8,72},{12,76},{16,80},{20,84},{24,88},{28,92},{32,9... | collective-permute-start | bytes 589832 | tf_op jit(solution)/shard_map/ppermute | solution.py:246
  22.6 44.2 %all-to-all-start = ((bf16[32,144,128]{2,1,0:T(8,128)(2,1)}), bf16[32,144,128]{2,1,0:T(8,128)(2,1)S(1)}, u32[]{:S(2)}, u32[]{:S(2)}) async-start(bf16[32,144,128]{2,1,0:T(8,128)(2,1)} %shard_map.65), calls=%async_computation | async-start | bytes 2359296 | tf_op jit(solution)/shard_map/all_to_all | solution.py:268
  33.3 14.1 %collective-permute-start.6 = (bf16[4,3,2,64,128]{4,3,2,1,0:T(8,128)(2,1)S(1)}, bf16[4,3,2,64,128]{4,3,2,1,0:T(8,128)(2,1)S(1)}, u32[]{:S(2)}, u32[]{:S(2)}) collective-permute-start(bf16[4,3,2,64,128]{4,3,2,1,0:T(8,128)(2,1)S(1)} %pad_maximum_fusion.refs_0_), channel_id=1, source_target_pairs={{0,3},{1,2},{2,1},{3,0},{4,7},{5,6},{6,5},{7,4},{8,11},{9,10},{10,... | collective-permute-start | bytes 1179656 | tf_op jit(solution)/shard_map/ppermute | solution.py:253
  41.2 38.2 %copy-start.4 = (bf16[128,64]{0,1:T(8,128)(2,1)S(1)}, bf16[128,64]{0,1:T(8,128)(2,1)}, u32[]{:S(2)}) copy-start(bf16[128,64]{0,1:T(8,128)(2,1)} %param.11) | copy-start | bytes 49156
  41.3 7.2 %collective-permute-start.8 = (bf16[4,3,2,64,128]{4,3,2,1,0:T(8,128)(2,1)S(1)}, bf16[4,3,2,64,128]{4,3,2,1,0:T(8,128)(2,1)S(1)}, u32[]{:S(2)}, u32[]{:S(2)}) collective-permute-start(bf16[4,3,2,64,128]{4,3,2,1,0:T(8,128)(2,1)S(1)} %pad_maximum_fusion.1.refs_4_), channel_id=1, source_target_pairs={{0,1},{1,0},{2,3},{3,2},{4,5},{5,4},{6,7},{7,6},{8,9},{9,8},{10,11... | collective-permute-start | bytes 1179656 | tf_op jit(solution)/shard_map/ppermute | solution.py:253
  42.0 14.9 %collective-permute-start.5 = (bf16[4,3,2,64,128]{4,3,2,1,0:T(8,128)(2,1)S(1)}, bf16[4,3,2,64,128]{4,3,2,1,0:T(8,128)(2,1)S(1)}, u32[]{:S(2)}, u32[]{:S(2)}) collective-permute-start(bf16[4,3,2,64,128]{4,3,2,1,0:T(8,128)(2,1)S(1)} %pad_maximum_fusion.refs_0_), channel_id=1, source_target_pairs={{0,1},{1,0},{2,3},{3,2},{4,5},{5,4},{6,7},{7,6},{8,9},{9,8},{10,11... | collective-permute-start | bytes 1179656 | tf_op jit(solution)/shard_map/ppermute | solution.py:253
  42.8 14.1 %collective-permute-start.10 = (bf16[4,3,2,64,128]{4,3,2,1,0:T(8,128)(2,1)S(1)}, bf16[4,3,2,64,128]{4,3,2,1,0:T(8,128)(2,1)S(1)}, u32[]{:S(2)}, u32[]{:S(2)}) collective-permute-start(bf16[4,3,2,64,128]{4,3,2,1,0:T(8,128)(2,1)S(1)} %pad_maximum_fusion.1.refs_4_), channel_id=1, source_target_pairs={{0,3},{1,2},{2,1},{3,0},{4,7},{5,6},{6,5},{7,4},{8,11},{9,10},{10,... | collective-permute-start | bytes 1179656 | tf_op jit(solution)/shard_map/ppermute | solution.py:253
  47.4 17.9 %collective-permute-start.7 = (bf16[4,3,2,64,128]{4,3,2,1,0:T(8,128)(2,1)S(1)}, bf16[4,3,2,64,128]{4,3,2,1,0:T(8,128)(2,1)S(1)}, u32[]{:S(2)}, u32[]{:S(2)}) collective-permute-start(bf16[4,3,2,64,128]{4,3,2,1,0:T(8,128)(2,1)S(1)} %collective-permute-done.6.refs_3_), channel_id=1, source_target_pairs={{0,1},{1,0},{2,3},{3,2},{4,5},{5,4},{6,7},{7,6},{8,9},{9,8},{10,11... | collective-permute-start | bytes 1179656 | tf_op jit(solution)/shard_map/ppermute | solution.py:253
  48.5 17.6 %collective-permute-start.9 = (bf16[4,3,2,64,128]{4,3,2,1,0:T(8,128)(2,1)S(1)}, bf16[4,3,2,64,128]{4,3,2,1,0:T(8,128)(2,1)S(1)}, u32[]{:S(2)}, u32[]{:S(2)}) collective-permute-start(bf16[4,3,2,64,128]{4,3,2,1,0:T(8,128)(2,1)S(1)} %collective-permute-done.8.refs_5_), channel_id=1, source_target_pairs={{0,3},{1,2},{2,1},{3,0},{4,7},{5,6},{6,5},{7,4},{8,11},{9,10},{10,... | collective-permute-start | bytes 1179656 | tf_op jit(solution)/shard_map/ppermute | solution.py:253
  65.3 0.8 copy-start
  66.1 0.8 copy-start.2
  66.8 1.0 %copy-start.1 = (bf16[4,3,2,64,128]{4,3,2,1,0:T(8,128)(2,1)S(1)}, bf16[4,3,2,64,128]{4,3,2,1,0:T(8,128)(2,1)}, u32[]{:S(2)}) copy-start(bf16[4,3,2,64,128]{4,3,2,1,0:T(8,128)(2,1)} %copy-done) | copy-start | bytes 1179652
  67.8 1.0 %copy-start.3 = (bf16[4,3,2,64,128]{4,3,2,1,0:T(8,128)(2,1)S(1)}, bf16[4,3,2,64,128]{4,3,2,1,0:T(8,128)(2,1)}, u32[]{:S(2)}) copy-start(bf16[4,3,2,64,128]{4,3,2,1,0:T(8,128)(2,1)} %copy-done.2) | copy-start | bytes 1179652
  72.5 6.9 %collective-permute-start.11 = (bf16[4352,128]{1,0:T(8,128)(2,1)S(1)}, bf16[4352,128]{1,0:T(8,128)(2,1)S(1)}, u32[]{:S(2)}, u32[]{:S(2)}) collective-permute-start(bf16[4352,128]{1,0:T(8,128)(2,1)S(1)} %get-tuple-element.22), channel_id=1, source_target_pairs={{0,4},{4,0},{8,12},{12,8},{16,20},{20,16},{24,28},{28,24},{32,36},... | collective-permute-start | bytes 3342344 | tf_op jit(solution)/shard_map/ppermute | solution.py:246

commit v4 on v3

--- a/solution.py
+++ b/solution.py
@@ -120,9 +120,9 @@
         out_ref[i, 2 * R :] = jnp.concatenate([a[:, lo:mid], a[:, mid:hi]], axis=0).astype(BF)
 
 
-def local_levels(steps, start, before, source_field, angles, project_mats, local_mats):
+def local_levels(steps, parts, start, before, source_field, angles, project_mats, local_mats):
     q, columns = source_field.shape
-    width = columns // 4
+    width = columns // parts
     tiles = width // TILE
     args = [source_field, angles, project_mats, local_mats]
     if before is not None:
@@ -145,33 +145,39 @@
     )(*args)
 
 
-def chip_kernel(data_ref, *refs):
-    keep_ref, send_ref, mats_ref, sems = refs[-4:]
-    copies = [
-        [
-            pltpu.make_async_copy(refs[p * PLANES + t], mats_ref.at[t, p], sems.at[p, t])
-            for t in range(PLANES)
-        ]
-        for p in range(2)
-    ]
-    for copy in copies[0] + copies[1]:
-        copy.start()
+def phases_kernel(ang_ref, cos_ref, sin_ref):
+    cos_ref[...], sin_ref[...] = cos_sin(ang_ref[...].astype(F32))
+
+
+def phases(moved):
+    out = jax.ShapeDtypeStruct((BLOCKS, 16, 128), F32)
+    spec = pl.BlockSpec((BLOCKS, 16, 128), lambda i: (0, 0, 0))
+    return pl.pallas_call(
+        phases_kernel,
+        grid=(1,),
+        in_specs=[pl.BlockSpec((BLOCKS, 16, 128), lambda i: (0, 2 * R // 16, 0))],
+        out_specs=[spec, spec],
+        out_shape=[out, out],
+        compiler_params=SMALL,
+    )(moved)
+
+
+def chip_kernel(data_ref, cos_ref, sin_ref, *refs):
+    keep_ref, send_ref = refs[-2:]
     low = place()[2] == 0
     x, cs, last = {}, {}, {}
     for slot in SLOTS:
         block = block_of(slot)
         x[slot] = jnp.concatenate([data_ref[block, :R], data_ref[block, R : 2 * R]], axis=1)
+        c, s = cos_ref[block], sin_ref[block]
+        cs[slot] = (jnp.concatenate([c[:8], c[8:]], axis=1), jnp.concatenate([s[:8], s[8:]], axis=1))
         a = data_ref[block, 2 * R :].astype(F32)
-        cs[slot] = cos_sin(jnp.concatenate([a[:8], a[8:]], axis=1))
         last[slot] = (a[:8], a[8:])
     flips = ((2, 0, 0), (1, 0, 0), (0, 2, 0), (0, 1, 0), (0, 0, 1))
     for level, flip in enumerate(flips):
-        if level % 3 == 0:
-            for copy in copies[level // 3]:
-                copy.wait()
         x = {
             (j, t, i): mix(
-                mats_ref[t, level // 3, j, level % 3, i],
+                refs[level // 3 * PLANES + t][j, level % 3, i],
                 x[j, t, i],
                 x[j ^ flip[0], t ^ flip[1], i ^ flip[2]],
                 row(cs[j, t, i][0], level),
@@ -192,21 +198,20 @@
         send_ref[at : at + 16] = jnp.where(low, hi, lo).astype(BF)
     for n, (j, t, i) in enumerate(SLOTS):
         at = BLOCKS * (R + 8) + n * R
-        keep_ref[at : at + R] = mats_ref[t, 1, j, 2, i]
-        send_ref[at : at + R] = mats_ref[t, 1, j, 2, i]
-
-
-def chip_levels(moved, early, late):
+        keep_ref[at : at + R] = refs[PLANES + t][j, 2, i]
+        send_ref[at : at + R] = refs[PLANES + t][j, 2, i]
+
+
+def chip_levels(moved, cos, sin, early, late):
     out = jax.ShapeDtypeStruct((BLOCKS * (2 * R + 8), 128), BF)
     vmem = pl.BlockSpec(memory_space=pltpu.VMEM)
     return pl.pallas_call(
         chip_kernel,
-        in_specs=[vmem] + [pl.BlockSpec(memory_space=pl.ANY)] * 8,
+        in_specs=[vmem] * 11,
         out_specs=[vmem, vmem],
         out_shape=[out, out],
-        scratch_shapes=[pltpu.VMEM((PLANES, 2, NX, 3, 2, R, 2 * R), BF), pltpu.SemaphoreType.DMA((2, PLANES))],
         compiler_params=SMALL,
-    )(moved, *early, *late)
+    )(moved, cos, sin, *early, *late)
 
 
 def last_kernel(own_ref, oth_ref, eval_ref, out_ref):
@@ -259,11 +264,11 @@
 
     own = jnp.concatenate([cross_mats[:, 0], cross_mats[:, 1]], axis=-1)
     far = to_plane(own)
-    first = local_levels(1, 0, None, source_field, angles, project_mats, local_mats)
+    first = local_levels(1, 2, 0, None, source_field, angles, project_mats, local_mats)
     far = after(far, first)
     pair = jnp.stack([far, swap(far, NC)], axis=1)
     quarter = [pair] + [swap(pair, j * NZ * NC) for j in (1, 2, 3)]
-    sent = local_levels(3, 1, after(first, pair), source_field, angles, project_mats, local_mats)
+    sent = local_levels(1, 2, 1, after(first, pair), source_field, angles, project_mats, local_mats)
     sent, *quarter = lax.optimization_barrier((sent, *quarter))
     moved = lax.all_to_all(sent, "box", 0, 0, tiled=True, axis_index_groups=chips)
     early, late = (jnp.stack([q[p : p + 3] for q in quarter]) for p in (0, 3))
@@ -271,7 +276,7 @@
     early1, late3 = along_src(early, 1), along_src(late, 3)
     early2, late2 = along_src(early3, 1), along_src(late1, 3)
 
-    keep, send = chip_levels(moved, (early, early1, early2, early3), (late, late1, late2, late3))
+    keep, send = chip_levels(moved, *phases(moved), (early, early1, early2, early3), (late, late1, late2, late3))
     received = swap(send, 1)
     return last_level(keep, received, evaluate_mats.T)
 

time: 82.6 us -> 78.7 us (0.953)
  Pallas kernels: 19.1 us -> 15.6 us
  waiting for transfers between devices: 25.5 us -> 29 us
  local copies, waits for them, and re-layouts: 4.51 us -> 1.02 us
  starting transfers between devices: 32.8 us -> 31.7 us
    all_to_all x1, waiting for transfers between devices: 0.01 us -> 10.2 us  [shards(): lax.all_to_all(sent, 'box', 0, 0, tiled=True, axis_index_groups=chips)]
    ppermute x6, waiting for transfers between devices: 21.1 us -> 11.6 us  [along_src(): return lax.ppermute(values, 'src', [(p, p ^ t) for p in range(PLANES)])]
    unnamed x10 -> x2, local copies, waits for them, and re-layouts: 3.5 us -> 0.01 us
    pallas_call x2, Pallas kernels: 12.6 us -> 9.46 us  [local_levels(): pl.pallas_call(functools.partial(local_kernel, start), grid=(steps,), in_...]
    ppermute x5, waiting for transfers between devices: 4.4 us -> 7.2 us  [swap(): lax.ppermute(values, 'box', [(i, i ^ distance) for i in range(count)])]
    ppermute x5, starting transfers between devices: 10.7 us -> 9.69 us  [swap(): lax.ppermute(values, 'box', [(i, i ^ distance) for i in range(count)])]
    pallas_call x1 -> x2, Pallas kernels: 3.72 us -> 3.29 us  [the longest x1 2.88 us: chip_levels(): pl.pallas_call(chip_kernel, in_specs=[vmem] * 11, out_specs=[vmem, vmem],...]
  transfers between devices with their start and end apart: 13 -> 13, of which waited for: 6 -> 7; matrix products, arithmetic and copies ran while one was open for 0% -> 0% of each run, Pallas kernels for 15% -> 13%
where the time goes in v4:
time: 78.7 us; the launch traced here: 77.7 us
  starting transfers between devices  31.7 us (40%)
  waiting for transfers between devices  29 us (37%)
  Pallas kernels  15.6 us (20%)
  local copies, waits for them, and re-layouts  1.02 us (1%)
    ppermute x6, waiting for transfers between devices, along_src(): return lax.ppermute(values, 'src', [(p, p ^ t) for p in range(PLANES)])  11.6 us
    all_to_all x1, starting transfers between devices, shards(): lax.all_to_all(sent, 'box', 0, 0, tiled=True, axis_index_groups=chips)  11.2 us
    all_to_all x1, waiting for transfers between devices, shards(): lax.all_to_all(sent, 'box', 0, 0, tiled=True, axis_index_groups=chips)  10.2 us
    ppermute x6, starting transfers between devices, along_src(): return lax.ppermute(values, 'src', [(p, p ^ t) for p in range(PLANES)])  10.2 us
    ppermute x5, starting transfers between devices, swap(): lax.ppermute(values, 'box', [(i, i ^ distance) for i in range(count)])  9.69 us
    pallas_call x2, Pallas kernels, local_levels(): pl.pallas_call(functools.partial(local_kernel, start), grid=(steps,), in_...  9.46 us
    ppermute x5, waiting for transfers between devices, swap(): lax.ppermute(values, 'box', [(i, i ^ distance) for i in range(count)])  7.2 us
    pallas_call x1, Pallas kernels, chip_levels(): pl.pallas_call(chip_kernel, in_specs=[vmem] * 11, out_specs=[vmem, vmem],...  2.88 us
  transfers between devices with their start and end apart: 13, of which 7 were waited for; matrix products, arithmetic and copies ran while one was open for 0% of the time, Pallas kernels for 13%

profile of v4, /device:TPU:1, one launch (start us, length us, event | category | flops | bytes accessed | tf_op | source)
XLA Modules:
  0.0 77.7 jit_solution(6136831516989605025)
XLA Ops:
  0.0 1.0 %slice_bitcast_fusion.9 = (bf16[6,64,64]{2,1,0:T(8,128)(2,1)S(1)}, bf16[6,64,64]{2,1,0:T(8,128)(2,1)S(1)}) fusion(bf16[6,2,64,64]{3,2,1,0:T(8,128)(2,1)} %param.9), kind=kLoop, calls=%fused_computation.13 | loop fusion | bytes 196608 | tf_op jit(solution)/shard_map/squeeze | solution.py:265
  1.0 0.1 pad_maximum_fusion.3
  1.1 0.7 collective-permute-start
  1.7 4.7 %shard_map.64.refs_0_ = bf16[32,144,128]{2,1,0:T(8,128)(2,1)} custom-call(bf16[128,8192]{1,0:T(8,128)(2,1)} %src_any.3, bf16[14,8192]{1,0:T(8,128)(2,1)} %ang_any.3, bf16[64,128]{1,0:T(8,128)(2,1)} %proj_any.3, bf16[8,2,64,64]{3,2,1,0:T(8,128)(2,1)} %mats_any.3), custom_call_target="tpu_custom_call" | custom-call | tf_op jit(solution)/shard_map/pallas_call | solution.py:130
  6.5 0.0 collective-permute-done
  6.5 2.6 %collective-permute-start.1 = (bf16[6,64,128]{2,1,0:T(8,128)(2,1)S(1)}, bf16[6,64,128]{2,1,0:T(8,128)(2,1)S(1)}, u32[]{:S(2)}, u32[]{:S(2)}) collective-permute-start(bf16[6,64,128]{2,1,0:T(8,128)(2,1)S(1)} %collective-permute-done), channel_id=1, source_target_pairs={{0,8},{4,12},{8,0},{12,4},{16,24},{20,28},{24,16},{28,20},{32,40},... | collective-permute-start | bytes 294920 | tf_op jit(solution)/shard_map/ppermute | solution.py:251
  9.0 2.0 %collective-permute-done.1 = bf16[6,64,128]{2,1,0:T(8,128)(2,1)S(1)} collective-permute-done((bf16[6,64,128]{2,1,0:T(8,128)(2,1)S(1)}, bf16[6,64,128]{2,1,0:T(8,128)(2,1)S(1)}, u32[]{:S(2)}, u32[]{:S(2)}) %collective-permute-start.1) | collective-permute-done | bytes 98336 | tf_op jit(solution)/shard_map/ppermute | solution.py:251
  11.1 2.9 %collective-permute-start.4 = (bf16[6,2,64,128]{3,2,1,0:T(8,128)(2,1)S(1)}, bf16[6,2,64,128]{3,2,1,0:T(8,128)(2,1)S(1)}, u32[]{:S(2)}, u32[]{:S(2)}) collective-permute-start(bf16[6,2,64,128]{3,2,1,0:T(8,128)(2,1)S(1)} %pad_maximum_fusion.2), channel_id=1, source_target_pairs={{0,192},{4,196},{8,200},{12,204},{16,208},{20,212},{24,216},{28,22... | collective-permute-start | bytes 589832 | tf_op jit(solution)/shard_map/ppermute | solution.py:251
  14.0 0.5 collective-permute-start.3
  14.6 0.1 collective-permute-start.2
  14.7 4.7 %shard_map.65 = bf16[32,144,128]{2,1,0:T(8,128)(2,1)} custom-call(bf16[128,8192]{1,0:T(8,128)(2,1)} %src_any.3, bf16[14,8192]{1,0:T(8,128)(2,1)} %ang_any.3, bf16[64,128]{1,0:T(8,128)(2,1)} %proj_any.3, bf16[8,2,64,64]{3,2,1,0:T(8,128)(2,1)} %mats_any.3, bf16[32,144,128]{2,1,0:T(8,128)(2,1)} %shard_map.64.refs_0_), custom_call_target="tpu_custom_call", output_to_operand_aliasing={{}: (4, {})} | custom-call | tf_op jit(solution)/shard_map/pallas_call | solution.py:130
  19.4 2.8 %collective-permute-done.4 = bf16[6,2,64,128]{3,2,1,0:T(8,128)(2,1)S(1)} collective-permute-done((bf16[6,2,64,128]{3,2,1,0:T(8,128)(2,1)S(1)}, bf16[6,2,64,128]{3,2,1,0:T(8,128)(2,1)S(1)}, u32[]{:S(2)}, u32[]{:S(2)}) %collective-permute-start.4) | collective-permute-done | bytes 196640 | tf_op jit(solution)/shard_map/ppermute | solution.py:251
  22.3 0.0 collective-permute-done.3
  22.3 0.0 collective-permute-done.2
  22.3 11.2 %all-to-all-start = ((bf16[32,144,128]{2,1,0:T(8,128)(2,1)}), bf16[32,144,128]{2,1,0:T(8,128)(2,1)S(1)}, u32[]{:S(2)}, u32[]{:S(2)}) async-start(bf16[32,144,128]{2,1,0:T(8,128)(2,1)} %shard_map.65), calls=%async_computation | async-start | bytes 2359296 | tf_op jit(solution)/shard_map/all_to_all | solution.py:273
  33.5 0.1 pad_maximum_fusion.refs_0_
  33.6 7.2 %collective-permute-start.6 = (bf16[4,3,2,64,128]{4,3,2,1,0:T(8,128)(2,1)S(1)}, bf16[4,3,2,64,128]{4,3,2,1,0:T(8,128)(2,1)S(1)}, u32[]{:S(2)}, u32[]{:S(2)}) collective-permute-start(bf16[4,3,2,64,128]{4,3,2,1,0:T(8,128)(2,1)S(1)} %pad_maximum_fusion.refs_0_), channel_id=1, source_target_pairs={{0,3},{1,2},{2,1},{3,0},{4,7},{5,6},{6,5},{7,4},{8,11},{9,10},{10,... | collective-permute-start | bytes 1179656 | tf_op jit(solution)/shard_map/ppermute | solution.py:258
  40.8 0.1 pad_maximum_fusion.1.refs_4_
  40.9 0.4 collective-permute-start.8
  41.3 1.2 %collective-permute-start.5 = (bf16[4,3,2,64,128]{4,3,2,1,0:T(8,128)(2,1)S(1)}, bf16[4,3,2,64,128]{4,3,2,1,0:T(8,128)(2,1)S(1)}, u32[]{:S(2)}, u32[]{:S(2)}) collective-permute-start(bf16[4,3,2,64,128]{4,3,2,1,0:T(8,128)(2,1)S(1)} %pad_maximum_fusion.refs_0_), channel_id=1, source_target_pairs={{0,1},{1,0},{2,3},{3,2},{4,5},{5,4},{6,7},{7,6},{8,9},{9,8},{10,11... | collective-permute-start | bytes 1179656 | tf_op jit(solution)/shard_map/ppermute | solution.py:258
  42.4 0.0 collective-permute-start.10
  42.5 5.6 %collective-permute-done.6.refs_3_ = bf16[4,3,2,64,128]{4,3,2,1,0:T(8,128)(2,1)S(1)} collective-permute-done((bf16[4,3,2,64,128]{4,3,2,1,0:T(8,128)(2,1)S(1)}, bf16[4,3,2,64,128]{4,3,2,1,0:T(8,128)(2,1)S(1)}, u32[]{:S(2)}, u32[]{:S(2)}) %collective-permute-start.6) | collective-permute-done | bytes 393248 | tf_op jit(solution)/shard_map/ppermute | solution.py:258
  48.0 0.0 collective-permute-start.7
  48.0 1.0 %collective-permute-done.8.refs_5_ = bf16[4,3,2,64,128]{4,3,2,1,0:T(8,128)(2,1)S(1)} collective-permute-done((bf16[4,3,2,64,128]{4,3,2,1,0:T(8,128)(2,1)S(1)}, bf16[4,3,2,64,128]{4,3,2,1,0:T(8,128)(2,1)S(1)}, u32[]{:S(2)}, u32[]{:S(2)}) %collective-permute-start.8) | collective-permute-done | bytes 393248 | tf_op jit(solution)/shard_map/ppermute | solution.py:258
  49.1 1.4 %collective-permute-start.9 = (bf16[4,3,2,64,128]{4,3,2,1,0:T(8,128)(2,1)S(1)}, bf16[4,3,2,64,128]{4,3,2,1,0:T(8,128)(2,1)}, u32[]{:S(2)}, u32[]{:S(2)}) collective-permute-start(bf16[4,3,2,64,128]{4,3,2,1,0:T(8,128)(2,1)S(1)} %collective-permute-done.8.refs_5_), channel_id=1, source_target_pairs={{0,3},{1,2},{2,1},{3,0},{4,7},{5,6},{6,5},{7,4},{8,11},{9,10},{10,... | collective-permute-start | bytes 1179656 | tf_op jit(solution)/shard_map/ppermute | solution.py:258
  50.4 10.2 %all-to-all-done.ang_ref.data_ref = bf16[32,144,128]{2,1,0:T(8,128)(2,1)S(1)} async-done(((bf16[32,144,128]{2,1,0:T(8,128)(2,1)}), bf16[32,144,128]{2,1,0:T(8,128)(2,1)S(1)}, u32[]{:S(2)}, u32[]{:S(2)}) %all-to-all-start) | async-done | bytes 1179680 | tf_op jit(solution)/shard_map/all_to_all | solution.py:273
  60.6 0.4 shard_map.66
  61.1 5.0 %collective-permute-done.7.refs_2_ = bf16[4,3,2,64,128]{4,3,2,1,0:T(8,128)(2,1)} collective-permute-done((bf16[4,3,2,64,128]{4,3,2,1,0:T(8,128)(2,1)S(1)}, bf16[4,3,2,64,128]{4,3,2,1,0:T(8,128)(2,1)}, u32[]{:S(2)}, u32[]{:S(2)}) %collective-permute-start.7) | collective-permute-done | bytes 393248 | tf_op jit(solution)/shard_map/ppermute | solution.py:258
  66.0 2.9 %shard_map.67 = (bf16[4352,128]{1,0:T(8,128)(2,1)S(1)}, bf16[4352,128]{1,0:T(8,128)(2,1)S(1)}) custom-call(bf16[32,144,128]{2,1,0:T(8,128)(2,1)S(1)} %all-to-all-done.ang_ref.data_ref, f32[32,16,128]{2,1,0:T(8,128)S(1)} %get-tuple-element.19.cos_ref, f32[32,16,128]{2,1,0:T(8,128)S(1)} %get-tuple-element.20.sin_ref, ...), custom_call_target="tpu_custom_call" | custom-call | tf_op jit(solution)/shard_map/pallas_call | solution.py:208
  68.9 3.5 %collective-permute-start.11 = (bf16[4352,128]{1,0:T(8,128)(2,1)S(1)}, bf16[4352,128]{1,0:T(8,128)(2,1)S(1)}, u32[]{:S(2)}, u32[]{:S(2)}) collective-permute-start(bf16[4352,128]{1,0:T(8,128)(2,1)S(1)} %get-tuple-element.26), channel_id=1, source_target_pairs={{0,4},{4,0},{8,12},{12,8},{16,20},{20,16},{24,28},{28,24},{32,36},... | collective-permute-start | bytes 3342344 | tf_op jit(solution)/shard_map/ppermute | solution.py:251
  72.4 2.4 %collective-permute-done.11.oth_ref = bf16[4352,128]{1,0:T(8,128)(2,1)S(1)} collective-permute-done((bf16[4352,128]{1,0:T(8,128)(2,1)S(1)}, bf16[4352,128]{1,0:T(8,128)(2,1)S(1)}, u32[]{:S(2)}, u32[]{:S(2)}) %collective-permute-start.11) | collective-permute-done | bytes 1114144 | tf_op jit(solution)/shard_map/ppermute | solution.py:251
  74.8 2.8 %shard_map.68 = bf16[128,8192]{1,0:T(8,128)(2,1)} custom-call(bf16[4352,128]{1,0:T(8,128)(2,1)S(1)} %get-tuple-element.25.own_ref, bf16[4352,128]{1,0:T(8,128)(2,1)S(1)} %collective-permute-done.11.oth_ref, bf16[64,128]{1,0:T(8,128)(2,1)S(1)} %bitcast.29), custom_call_target="tpu_custom_call" | custom-call | tf_op jit(solution)/shard_map/pallas_call | solution.py:238
  (8 shorter events, 0.1 us)
Async XLA Ops:
  1.1 5.4 %collective-permute-start = (bf16[6,64,128]{2,1,0:T(8,128)(2,1)S(1)}, bf16[6,64,128]{2,1,0:T(8,128)(2,1)S(1)}, u32[]{:S(2)}, u32[]{:S(2)}) collective-permute-start(bf16[6,64,128]{2,1,0:T(8,128)(2,1)S(1)} %pad_maximum_fusion.3), channel_id=1, source_target_pairs={{0,0},{1,17},{2,34},{3,51},{4,4},{5,21},{6,38},{7,55},{8,8},{9,25}... | collective-permute-start | bytes 294920 | tf_op jit(solution)/shard_map/ppermute | solution.py:255
  6.5 4.6 %collective-permute-start.1 = (bf16[6,64,128]{2,1,0:T(8,128)(2,1)S(1)}, bf16[6,64,128]{2,1,0:T(8,128)(2,1)S(1)}, u32[]{:S(2)}, u32[]{:S(2)}) collective-permute-start(bf16[6,64,128]{2,1,0:T(8,128)(2,1)S(1)} %collective-permute-done), channel_id=1, source_target_pairs={{0,8},{4,12},{8,0},{12,4},{16,24},{20,28},{24,16},{28,20},{32,40},... | collective-permute-start | bytes 294920 | tf_op jit(solution)/shard_map/ppermute | solution.py:251
  11.1 11.2 %collective-permute-start.4 = (bf16[6,2,64,128]{3,2,1,0:T(8,128)(2,1)S(1)}, bf16[6,2,64,128]{3,2,1,0:T(8,128)(2,1)S(1)}, u32[]{:S(2)}, u32[]{:S(2)}) collective-permute-start(bf16[6,2,64,128]{3,2,1,0:T(8,128)(2,1)S(1)} %pad_maximum_fusion.2), channel_id=1, source_target_pairs={{0,192},{4,196},{8,200},{12,204},{16,208},{20,212},{24,216},{28,22... | collective-permute-start | bytes 589832 | tf_op jit(solution)/shard_map/ppermute | solution.py:251
  14.0 8.2 %collective-permute-start.3 = (bf16[6,2,64,128]{3,2,1,0:T(8,128)(2,1)S(1)}, bf16[6,2,64,128]{3,2,1,0:T(8,128)(2,1)S(1)}, u32[]{:S(2)}, u32[]{:S(2)}) collective-permute-start(bf16[6,2,64,128]{3,2,1,0:T(8,128)(2,1)S(1)} %pad_maximum_fusion.2), channel_id=1, source_target_pairs={{0,128},{4,132},{8,136},{12,140},{16,144},{20,148},{24,152},{28,15... | collective-permute-start | bytes 589832 | tf_op jit(solution)/shard_map/ppermute | solution.py:251
  14.6 7.7 %collective-permute-start.2 = (bf16[6,2,64,128]{3,2,1,0:T(8,128)(2,1)S(1)}, bf16[6,2,64,128]{3,2,1,0:T(8,128)(2,1)S(1)}, u32[]{:S(2)}, u32[]{:S(2)}) collective-permute-start(bf16[6,2,64,128]{3,2,1,0:T(8,128)(2,1)S(1)} %pad_maximum_fusion.2), channel_id=1, source_target_pairs={{0,64},{4,68},{8,72},{12,76},{16,80},{20,84},{24,88},{28,92},{32,9... | collective-permute-start | bytes 589832 | tf_op jit(solution)/shard_map/ppermute | solution.py:251
  22.3 38.4 %all-to-all-start = ((bf16[32,144,128]{2,1,0:T(8,128)(2,1)}), bf16[32,144,128]{2,1,0:T(8,128)(2,1)S(1)}, u32[]{:S(2)}, u32[]{:S(2)}) async-start(bf16[32,144,128]{2,1,0:T(8,128)(2,1)} %shard_map.65), calls=%async_computation | async-start | bytes 2359296 | tf_op jit(solution)/shard_map/all_to_all | solution.py:273
  33.6 14.4 %collective-permute-start.6 = (bf16[4,3,2,64,128]{4,3,2,1,0:T(8,128)(2,1)S(1)}, bf16[4,3,2,64,128]{4,3,2,1,0:T(8,128)(2,1)S(1)}, u32[]{:S(2)}, u32[]{:S(2)}) collective-permute-start(bf16[4,3,2,64,128]{4,3,2,1,0:T(8,128)(2,1)S(1)} %pad_maximum_fusion.refs_0_), channel_id=1, source_target_pairs={{0,3},{1,2},{2,1},{3,0},{4,7},{5,6},{6,5},{7,4},{8,11},{9,10},{10,... | collective-permute-start | bytes 1179656 | tf_op jit(solution)/shard_map/ppermute | solution.py:258
  40.9 8.2 %collective-permute-start.8 = (bf16[4,3,2,64,128]{4,3,2,1,0:T(8,128)(2,1)S(1)}, bf16[4,3,2,64,128]{4,3,2,1,0:T(8,128)(2,1)S(1)}, u32[]{:S(2)}, u32[]{:S(2)}) collective-permute-start(bf16[4,3,2,64,128]{4,3,2,1,0:T(8,128)(2,1)S(1)} %pad_maximum_fusion.1.refs_4_), channel_id=1, source_target_pairs={{0,1},{1,0},{2,3},{3,2},{4,5},{5,4},{6,7},{7,6},{8,9},{9,8},{10,11... | collective-permute-start | bytes 1179656 | tf_op jit(solution)/shard_map/ppermute | solution.py:258
  41.3 19.8 %collective-permute-start.5 = (bf16[4,3,2,64,128]{4,3,2,1,0:T(8,128)(2,1)S(1)}, bf16[4,3,2,64,128]{4,3,2,1,0:T(8,128)(2,1)S(1)}, u32[]{:S(2)}, u32[]{:S(2)}) collective-permute-start(bf16[4,3,2,64,128]{4,3,2,1,0:T(8,128)(2,1)S(1)} %pad_maximum_fusion.refs_0_), channel_id=1, source_target_pairs={{0,1},{1,0},{2,3},{3,2},{4,5},{5,4},{6,7},{7,6},{8,9},{9,8},{10,11... | collective-permute-start | bytes 1179656 | tf_op jit(solution)/shard_map/ppermute | solution.py:258
  42.4 18.6 %collective-permute-start.10 = (bf16[4,3,2,64,128]{4,3,2,1,0:T(8,128)(2,1)S(1)}, bf16[4,3,2,64,128]{4,3,2,1,0:T(8,128)(2,1)S(1)}, u32[]{:S(2)}, u32[]{:S(2)}) collective-permute-start(bf16[4,3,2,64,128]{4,3,2,1,0:T(8,128)(2,1)S(1)} %pad_maximum_fusion.1.refs_4_), channel_id=1, source_target_pairs={{0,3},{1,2},{2,1},{3,0},{4,7},{5,6},{6,5},{7,4},{8,11},{9,10},{10,... | collective-permute-start | bytes 1179656 | tf_op jit(solution)/shard_map/ppermute | solution.py:258
  48.0 18.0 %collective-permute-start.7 = (bf16[4,3,2,64,128]{4,3,2,1,0:T(8,128)(2,1)S(1)}, bf16[4,3,2,64,128]{4,3,2,1,0:T(8,128)(2,1)}, u32[]{:S(2)}, u32[]{:S(2)}) collective-permute-start(bf16[4,3,2,64,128]{4,3,2,1,0:T(8,128)(2,1)S(1)} %collective-permute-done.6.refs_3_), channel_id=1, source_target_pairs={{0,1},{1,0},{2,3},{3,2},{4,5},{5,4},{6,7},{7,6},{8,9},{9,8},{10,11... | collective-permute-start | bytes 1179656 | tf_op jit(solution)/shard_map/ppermute | solution.py:258
  49.1 17.0 %collective-permute-start.9 = (bf16[4,3,2,64,128]{4,3,2,1,0:T(8,128)(2,1)S(1)}, bf16[4,3,2,64,128]{4,3,2,1,0:T(8,128)(2,1)}, u32[]{:S(2)}, u32[]{:S(2)}) collective-permute-start(bf16[4,3,2,64,128]{4,3,2,1,0:T(8,128)(2,1)S(1)} %collective-permute-done.8.refs_5_), channel_id=1, source_target_pairs={{0,3},{1,2},{2,1},{3,0},{4,7},{5,6},{6,5},{7,4},{8,11},{9,10},{10,... | collective-permute-start | bytes 1179656 | tf_op jit(solution)/shard_map/ppermute | solution.py:258
  66.0 8.8 %copy-start = (bf16[128,64]{0,1:T(8,128)(2,1)S(1)}, bf16[128,64]{0,1:T(8,128)(2,1)}, u32[]{:S(2)}) copy-start(bf16[128,64]{0,1:T(8,128)(2,1)} %param.11) | copy-start | bytes 49156
  68.9 5.9 %collective-permute-start.11 = (bf16[4352,128]{1,0:T(8,128)(2,1)S(1)}, bf16[4352,128]{1,0:T(8,128)(2,1)S(1)}, u32[]{:S(2)}, u32[]{:S(2)}) collective-permute-start(bf16[4352,128]{1,0:T(8,128)(2,1)S(1)} %get-tuple-element.26), channel_id=1, source_target_pairs={{0,4},{4,0},{8,12},{12,8},{16,20},{20,16},{24,28},{28,24},{32,36},... | collective-permute-start | bytes 3342344 | tf_op jit(solution)/shard_map/ppermute | solution.py:251

commit v5 on v4

--- a/solution.py
+++ b/solution.py
@@ -266,12 +266,17 @@
     far = to_plane(own)
     first = local_levels(1, 2, 0, None, source_field, angles, project_mats, local_mats)
     far = after(far, first)
-    pair = jnp.stack([far, swap(far, NC)], axis=1)
-    quarter = [pair] + [swap(pair, j * NZ * NC) for j in (1, 2, 3)]
-    sent = local_levels(1, 2, 1, after(first, pair), source_field, angles, project_mats, local_mats)
-    sent, *quarter = lax.optimization_barrier((sent, *quarter))
+    near = swap(far, NC)
+    far_x = [far] + [swap(far, j * NZ * NC) for j in (1, 3, 2)]
+    near, half = lax.optimization_barrier((near, first))
+    near_x = [near] + [swap(near, j * NZ * NC) for j in (1, 3, 2)]
+    sent = local_levels(1, 2, 1, half, source_field, angles, project_mats, local_mats)
+    sent, *pairs = lax.optimization_barrier((sent, *far_x, *near_x))
     moved = lax.all_to_all(sent, "box", 0, 0, tiled=True, axis_index_groups=chips)
-    early, late = (jnp.stack([q[p : p + 3] for q in quarter]) for p in (0, 3))
+    early, late = (
+        jnp.stack([jnp.stack([pairs[j][p : p + 3], pairs[4 + j][p : p + 3]], axis=1) for j in (0, 1, 3, 2)])
+        for p in (0, 3)
+    )
     early3, late1 = along_src(early, 3), along_src(late, 1)
     early1, late3 = along_src(early, 1), along_src(late, 3)
     early2, late2 = along_src(early3, 1), along_src(late1, 3)

time: 78.7 us -> 77.2 us (0.981)
  waiting for transfers between devices: 29 us -> 22.4 us
  starting transfers between devices: 31.7 us -> 37.2 us
    all_to_all x1, waiting for transfers between devices: 10.2 us -> 0.01 us  [shards(): lax.all_to_all(sent, 'box', 0, 0, tiled=True, axis_index_groups=chips)]
    ppermute x6, waiting for transfers between devices: 11.6 us -> 19.8 us  [along_src(): return lax.ppermute(values, 'src', [(p, p ^ t) for p in range(PLANES)])]
    ppermute x5 -> x8, starting transfers between devices: 9.69 us -> 14.4 us  [swap(): lax.ppermute(values, 'box', [(i, i ^ distance) for i in range(count)])]
    ppermute x5 -> x8, waiting for transfers between devices: 7.2 us -> 2.59 us  [swap(): lax.ppermute(values, 'box', [(i, i ^ distance) for i in range(count)])]
    ppermute x6, starting transfers between devices: 10.2 us -> 11.9 us  [along_src(): return lax.ppermute(values, 'src', [(p, p ^ t) for p in range(PLANES)])]
    all_to_all x1, starting transfers between devices: 11.2 us -> 10.2 us  [shards(): lax.all_to_all(sent, 'box', 0, 0, tiled=True, axis_index_groups=chips)]
  transfers between devices with their start and end apart: 13 -> 16, of which waited for: 7 -> 5; matrix products, arithmetic and copies ran while one was open for 0% -> 0% of each run, Pallas kernels for 13% -> 13%
where the time goes in v5:
time: 77.2 us; the launch traced here: 76.9 us
  starting transfers between devices  37.2 us (48%)
  waiting for transfers between devices  22.4 us (29%)
  Pallas kernels  15.6 us (20%)
  local copies, waits for them, and re-layouts  1.13 us (1%)
    ppermute x6, waiting for transfers between devices, along_src(): return lax.ppermute(values, 'src', [(p, p ^ t) for p in range(PLANES)])  19.8 us
    ppermute x8, starting transfers between devices, swap(): lax.ppermute(values, 'box', [(i, i ^ distance) for i in range(count)])  14.4 us
    ppermute x6, starting transfers between devices, along_src(): return lax.ppermute(values, 'src', [(p, p ^ t) for p in range(PLANES)])  11.9 us
    all_to_all x1, starting transfers between devices, shards(): lax.all_to_all(sent, 'box', 0, 0, tiled=True, axis_index_groups=chips)  10.2 us
    pallas_call x2, Pallas kernels, local_levels(): pl.pallas_call(functools.partial(local_kernel, start), grid=(steps,), in_...  9.45 us
    pallas_call x1, Pallas kernels, chip_levels(): pl.pallas_call(chip_kernel, in_specs=[vmem] * 11, out_specs=[vmem, vmem],...  2.86 us
    pallas_call x1, Pallas kernels, last_level(): pl.pallas_call(last_kernel, in_specs=[vmem] * 3, out_specs=vmem, out_shap...  2.84 us
    ppermute x8, waiting for transfers between devices, swap(): lax.ppermute(values, 'box', [(i, i ^ distance) for i in range(count)])  2.59 us
  transfers between devices with their start and end apart: 16, of which 5 were waited for; matrix products, arithmetic and copies ran while one was open for 0% of the time, Pallas kernels for 13%

profile of v5, /device:TPU:1, one launch (start us, length us, event | category | flops | bytes accessed | tf_op | source)
XLA Modules:
  0.0 76.9 jit_solution(15928282776279194420)
XLA Ops:
  0.0 1.0 %slice_bitcast_fusion.1 = (bf16[6,64,64]{2,1,0:T(8,128)(2,1)S(1)}, bf16[6,64,64]{2,1,0:T(8,128)(2,1)S(1)}) fusion(bf16[6,2,64,64]{3,2,1,0:T(8,128)(2,1)} %param.9), kind=kLoop, calls=%fused_computation.12 | loop fusion | bytes 196608 | tf_op jit(solution)/shard_map/squeeze | solution.py:265
  1.0 0.1 pad_maximum_fusion.2
  1.1 0.7 collective-permute-start
  1.7 4.7 %shard_map.64.refs_0_ = bf16[32,144,128]{2,1,0:T(8,128)(2,1)} custom-call(bf16[128,8192]{1,0:T(8,128)(2,1)} %src_any.3, bf16[14,8192]{1,0:T(8,128)(2,1)} %ang_any.3, bf16[64,128]{1,0:T(8,128)(2,1)} %proj_any.3, bf16[8,2,64,64]{3,2,1,0:T(8,128)(2,1)} %mats_any.3), custom_call_target="tpu_custom_call" | custom-call | tf_op jit(solution)/shard_map/pallas_call | solution.py:130
  6.5 2.6 %collective-permute-start.1 = (bf16[6,64,128]{2,1,0:T(8,128)(2,1)S(1)}, bf16[6,64,128]{2,1,0:T(8,128)(2,1)S(1)}, u32[]{:S(2)}, u32[]{:S(2)}) collective-permute-start(bf16[6,64,128]{2,1,0:T(8,128)(2,1)S(1)} %collective-permute-done), channel_id=1, source_target_pairs={{0,8},{4,12},{8,0},{12,4},{16,24},{20,28},{24,16},{28,20},{32,40},... | collective-permute-start | bytes 294920 | tf_op jit(solution)/shard_map/ppermute | solution.py:251
  9.0 2.8 %collective-permute-start.4 = (bf16[6,64,128]{2,1,0:T(8,128)(2,1)S(1)}, bf16[6,64,128]{2,1,0:T(8,128)(2,1)S(1)}, u32[]{:S(2)}, u32[]{:S(2)}) collective-permute-start(bf16[6,64,128]{2,1,0:T(8,128)(2,1)S(1)} %collective-permute-done), channel_id=1, source_target_pairs={{0,128},{4,132},{8,136},{12,140},{16,144},{20,148},{24,152},{28,15... | collective-permute-start | bytes 294920 | tf_op jit(solution)/shard_map/ppermute | solution.py:251
  11.8 0.9 %collective-permute-start.3 = (bf16[6,64,128]{2,1,0:T(8,128)(2,1)S(1)}, bf16[6,64,128]{2,1,0:T(8,128)(2,1)S(1)}, u32[]{:S(2)}, u32[]{:S(2)}) collective-permute-start(bf16[6,64,128]{2,1,0:T(8,128)(2,1)S(1)} %collective-permute-done), channel_id=1, source_target_pairs={{0,192},{4,196},{8,200},{12,204},{16,208},{20,212},{24,216},{28,22... | collective-permute-start | bytes 294920 | tf_op jit(solution)/shard_map/ppermute | solution.py:251
  12.7 3.0 %collective-permute-start.7 = (bf16[6,64,128]{2,1,0:T(8,128)(2,1)S(1)}, bf16[6,64,128]{2,1,0:T(8,128)(2,1)S(1)}, u32[]{:S(2)}, u32[]{:S(2)}) collective-permute-start(bf16[6,64,128]{2,1,0:T(8,128)(2,1)S(1)} %collective-permute-done.1), channel_id=1, source_target_pairs={{0,128},{4,132},{8,136},{12,140},{16,144},{20,148},{24,152},{28,15... | collective-permute-start | bytes 294920 | tf_op jit(solution)/shard_map/ppermute | solution.py:251
  15.7 0.9 %collective-permute-start.6 = (bf16[6,64,128]{2,1,0:T(8,128)(2,1)S(1)}, bf16[6,64,128]{2,1,0:T(8,128)(2,1)S(1)}, u32[]{:S(2)}, u32[]{:S(2)}) collective-permute-start(bf16[6,64,128]{2,1,0:T(8,128)(2,1)S(1)} %collective-permute-done.1), channel_id=1, source_target_pairs={{0,192},{4,196},{8,200},{12,204},{16,208},{20,212},{24,216},{28,22... | collective-permute-start | bytes 294920 | tf_op jit(solution)/shard_map/ppermute | solution.py:251
  16.5 0.0 collective-permute-done.4
  16.5 0.0 collective-permute-start.5
  16.5 4.7 %shard_map.65 = bf16[32,144,128]{2,1,0:T(8,128)(2,1)} custom-call(bf16[128,8192]{1,0:T(8,128)(2,1)} %src_any.3, bf16[14,8192]{1,0:T(8,128)(2,1)} %ang_any.3, bf16[64,128]{1,0:T(8,128)(2,1)} %proj_any.3, bf16[8,2,64,64]{3,2,1,0:T(8,128)(2,1)} %mats_any.3, bf16[32,144,128]{2,1,0:T(8,128)(2,1)} %shard_map.64.refs_0_), custom_call_target="tpu_custom_call", output_to_operand_aliasing={{}: (4, {})} | custom-call | tf_op jit(solution)/shard_map/pallas_call | solution.py:130
  21.3 0.0 collective-permute-done.3
  21.3 0.0 collective-permute-done.7
  21.3 0.2 collective-permute-done.6
  21.5 10.2 %all-to-all-start = ((bf16[32,144,128]{2,1,0:T(8,128)(2,1)}), bf16[32,144,128]{2,1,0:T(8,128)(2,1)S(1)}, u32[]{:S(2)}, u32[]{:S(2)}) async-start(bf16[32,144,128]{2,1,0:T(8,128)(2,1)} %shard_map.65), calls=%async_computation | async-start | bytes 2359296 | tf_op jit(solution)/shard_map/all_to_all | solution.py:275
  31.9 0.1 pad_maximum_fusion
  31.9 7.7 %collective-permute-start.9 = (bf16[4,3,2,64,128]{4,3,1,2,0:T(8,128)(2,1)S(1)}, bf16[4,3,2,64,128]{4,3,1,2,0:T(8,128)(2,1)S(1)}, u32[]{:S(2)}, u32[]{:S(2)}) collective-permute-start(bf16[4,3,2,64,128]{4,3,1,2,0:T(8,128)(2,1)S(1)} %pad_maximum_fusion), channel_id=1, source_target_pairs={{0,3},{1,2},{2,1},{3,0},{4,7},{5,6},{6,5},{7,4},{8,11},{9,10},{10,... | collective-permute-start | bytes 1179656 | tf_op jit(solution)/shard_map/ppermute | solution.py:258
  39.7 0.1 collective-permute-start.11
  39.8 1.5 %collective-permute-start.8 = (bf16[4,3,2,64,128]{4,3,1,2,0:T(8,128)(2,1)S(1)}, bf16[4,3,2,64,128]{4,3,1,2,0:T(8,128)(2,1)S(1)}, u32[]{:S(2)}, u32[]{:S(2)}) collective-permute-start(bf16[4,3,2,64,128]{4,3,1,2,0:T(8,128)(2,1)S(1)} %pad_maximum_fusion), channel_id=1, source_target_pairs={{0,1},{1,0},{2,3},{3,2},{4,5},{5,4},{6,7},{7,6},{8,9},{9,8},{10,11... | collective-permute-start | bytes 1179656 | tf_op jit(solution)/shard_map/ppermute | solution.py:258
  41.3 4.6 %collective-permute-done.9 = bf16[4,3,2,64,128]{4,3,1,2,0:T(8,128)(2,1)S(1)} collective-permute-done((bf16[4,3,2,64,128]{4,3,1,2,0:T(8,128)(2,1)S(1)}, bf16[4,3,2,64,128]{4,3,1,2,0:T(8,128)(2,1)S(1)}, u32[]{:S(2)}, u32[]{:S(2)}) %collective-permute-start.9) | collective-permute-done | bytes 393248 | tf_op jit(solution)/shard_map/ppermute | solution.py:258
  45.8 0.0 collective-permute-start.10
  45.8 2.4 %collective-permute-start.13 = (bf16[4,3,2,64,128]{4,3,2,1,0:T(8,128)(2,1)S(1)}, bf16[4,3,2,64,128]{4,3,2,1,0:T(8,128)(2,1)}, u32[]{:S(2)}, u32[]{:S(2)}) collective-permute-start(bf16[4,3,2,64,128]{4,3,2,1,0:T(8,128)(2,1)S(1)} %pad_maximum_fusion.1.refs_4_), channel_id=1, source_target_pairs={{0,3},{1,2},{2,1},{3,0},{4,7},{5,6},{6,5},{7,4},{8,11},{9,10},{10,... | collective-permute-start | bytes 1179656 | tf_op jit(solution)/shard_map/ppermute | solution.py:258
  48.2 0.3 collective-permute-start.12
  48.6 6.9 %collective-permute-done.8 = bf16[4,3,2,64,128]{4,3,1,2,0:T(8,128)(2,1)S(1)} collective-permute-done((bf16[4,3,2,64,128]{4,3,1,2,0:T(8,128)(2,1)S(1)}, bf16[4,3,2,64,128]{4,3,1,2,0:T(8,128)(2,1)S(1)}, u32[]{:S(2)}, u32[]{:S(2)}) %collective-permute-start.8) | collective-permute-done | bytes 393248 | tf_op jit(solution)/shard_map/ppermute | solution.py:258
  55.5 8.4 %collective-permute-done.10 = bf16[4,3,2,64,128]{4,3,1,2,0:T(8,128)(2,1)S(1)} collective-permute-done((bf16[4,3,2,64,128]{4,3,1,2,0:T(8,128)(2,1)S(1)}, bf16[4,3,2,64,128]{4,3,1,2,0:T(8,128)(2,1)S(1)}, u32[]{:S(2)}, u32[]{:S(2)}) %collective-permute-start.10) | collective-permute-done | bytes 393248 | tf_op jit(solution)/shard_map/ppermute | solution.py:258
  63.9 0.4 shard_map.66
  64.4 0.0 copy-start
  64.4 2.9 %shard_map.67 = (bf16[4352,128]{1,0:T(8,128)(2,1)S(1)}, bf16[4352,128]{1,0:T(8,128)(2,1)S(1)}) custom-call(bf16[32,144,128]{2,1,0:T(8,128)(2,1)S(1)} %all-to-all-done.ang_ref.data_ref, f32[32,16,128]{2,1,0:T(8,128)S(1)} %get-tuple-element.25.cos_ref, f32[32,16,128]{2,1,0:T(8,128)S(1)} %get-tuple-element.26.sin_ref, ...), custom_call_target="tpu_custom_call" | custom-call | tf_op jit(solution)/shard_map/pallas_call | solution.py:208
  67.2 4.4 %collective-permute-start.14 = (bf16[4352,128]{1,0:T(8,128)(2,1)S(1)}, bf16[4352,128]{1,0:T(8,128)(2,1)S(1)}, u32[]{:S(2)}, u32[]{:S(2)}) collective-permute-start(bf16[4352,128]{1,0:T(8,128)(2,1)S(1)} %get-tuple-element.36), channel_id=1, source_target_pairs={{0,4},{4,0},{8,12},{12,8},{16,20},{20,16},{24,28},{28,24},{32,36},... | collective-permute-start | bytes 3342344 | tf_op jit(solution)/shard_map/ppermute | solution.py:251
  71.6 2.4 %collective-permute-done.14.oth_ref = bf16[4352,128]{1,0:T(8,128)(2,1)S(1)} collective-permute-done((bf16[4352,128]{1,0:T(8,128)(2,1)S(1)}, bf16[4352,128]{1,0:T(8,128)(2,1)S(1)}, u32[]{:S(2)}, u32[]{:S(2)}) %collective-permute-start.14) | collective-permute-done | bytes 1114144 | tf_op jit(solution)/shard_map/ppermute | solution.py:251
  74.0 2.8 %shard_map.68 = bf16[128,8192]{1,0:T(8,128)(2,1)} custom-call(bf16[4352,128]{1,0:T(8,128)(2,1)S(1)} %get-tuple-element.35.own_ref, bf16[4352,128]{1,0:T(8,128)(2,1)S(1)} %collective-permute-done.14.oth_ref, bf16[64,128]{1,0:T(8,128)(2,1)S(1)} %bitcast.61), custom_call_target="tpu_custom_call" | custom-call | tf_op jit(solution)/shard_map/pallas_call | solution.py:238
  (26 shorter events, 0.3 us)
Async XLA Ops:
  1.1 5.4 %collective-permute-start = (bf16[6,64,128]{2,1,0:T(8,128)(2,1)S(1)}, bf16[6,64,128]{2,1,0:T(8,128)(2,1)S(1)}, u32[]{:S(2)}, u32[]{:S(2)}) collective-permute-start(bf16[6,64,128]{2,1,0:T(8,128)(2,1)S(1)} %pad_maximum_fusion.2), channel_id=1, source_target_pairs={{0,0},{1,17},{2,34},{3,51},{4,4},{5,21},{6,38},{7,55},{8,8},{9,25}... | collective-permute-start | bytes 294920 | tf_op jit(solution)/shard_map/ppermute | solution.py:255
  6.5 6.2 %collective-permute-start.1 = (bf16[6,64,128]{2,1,0:T(8,128)(2,1)S(1)}, bf16[6,64,128]{2,1,0:T(8,128)(2,1)S(1)}, u32[]{:S(2)}, u32[]{:S(2)}) collective-permute-start(bf16[6,64,128]{2,1,0:T(8,128)(2,1)S(1)} %collective-permute-done), channel_id=1, source_target_pairs={{0,8},{4,12},{8,0},{12,4},{16,24},{20,28},{24,16},{28,20},{32,40},... | collective-permute-start | bytes 294920 | tf_op jit(solution)/shard_map/ppermute | solution.py:251
  9.0 7.5 %collective-permute-start.4 = (bf16[6,64,128]{2,1,0:T(8,128)(2,1)S(1)}, bf16[6,64,128]{2,1,0:T(8,128)(2,1)S(1)}, u32[]{:S(2)}, u32[]{:S(2)}) collective-permute-start(bf16[6,64,128]{2,1,0:T(8,128)(2,1)S(1)} %collective-permute-done), channel_id=1, source_target_pairs={{0,128},{4,132},{8,136},{12,140},{16,144},{20,148},{24,152},{28,15... | collective-permute-start | bytes 294920 | tf_op jit(solution)/shard_map/ppermute | solution.py:251
  11.8 9.5 %collective-permute-start.3 = (bf16[6,64,128]{2,1,0:T(8,128)(2,1)S(1)}, bf16[6,64,128]{2,1,0:T(8,128)(2,1)S(1)}, u32[]{:S(2)}, u32[]{:S(2)}) collective-permute-start(bf16[6,64,128]{2,1,0:T(8,128)(2,1)S(1)} %collective-permute-done), channel_id=1, source_target_pairs={{0,192},{4,196},{8,200},{12,204},{16,208},{20,212},{24,216},{28,22... | collective-permute-start | bytes 294920 | tf_op jit(solution)/shard_map/ppermute | solution.py:251
  12.6 8.6 %collective-permute-start.2 = (bf16[6,64,128]{2,1,0:T(8,128)(2,1)S(1)}, bf16[6,64,128]{2,1,0:T(8,128)(2,1)S(1)}, u32[]{:S(2)}, u32[]{:S(2)}) collective-permute-start(bf16[6,64,128]{2,1,0:T(8,128)(2,1)S(1)} %collective-permute-done), channel_id=1, source_target_pairs={{0,64},{4,68},{8,72},{12,76},{16,80},{20,84},{24,88},{28,92},{32,9... | collective-permute-start | bytes 294920 | tf_op jit(solution)/shard_map/ppermute | solution.py:251
  12.7 8.6 %collective-permute-start.7 = (bf16[6,64,128]{2,1,0:T(8,128)(2,1)S(1)}, bf16[6,64,128]{2,1,0:T(8,128)(2,1)S(1)}, u32[]{:S(2)}, u32[]{:S(2)}) collective-permute-start(bf16[6,64,128]{2,1,0:T(8,128)(2,1)S(1)} %collective-permute-done.1), channel_id=1, source_target_pairs={{0,128},{4,132},{8,136},{12,140},{16,144},{20,148},{24,152},{28,15... | collective-permute-start | bytes 294920 | tf_op jit(solution)/shard_map/ppermute | solution.py:251
  15.7 5.8 %collective-permute-start.6 = (bf16[6,64,128]{2,1,0:T(8,128)(2,1)S(1)}, bf16[6,64,128]{2,1,0:T(8,128)(2,1)S(1)}, u32[]{:S(2)}, u32[]{:S(2)}) collective-permute-start(bf16[6,64,128]{2,1,0:T(8,128)(2,1)S(1)} %collective-permute-done.1), channel_id=1, source_target_pairs={{0,192},{4,196},{8,200},{12,204},{16,208},{20,212},{24,216},{28,22... | collective-permute-start | bytes 294920 | tf_op jit(solution)/shard_map/ppermute | solution.py:251
  16.5 5.0 %collective-permute-start.5 = (bf16[6,64,128]{2,1,0:T(8,128)(2,1)S(1)}, bf16[6,64,128]{2,1,0:T(8,128)(2,1)S(1)}, u32[]{:S(2)}, u32[]{:S(2)}) collective-permute-start(bf16[6,64,128]{2,1,0:T(8,128)(2,1)S(1)} %collective-permute-done.1), channel_id=1, source_target_pairs={{0,64},{4,68},{8,72},{12,76},{16,80},{20,84},{24,88},{28,92},{32,9... | collective-permute-start | bytes 294920 | tf_op jit(solution)/shard_map/ppermute | solution.py:251
  21.5 42.4 %all-to-all-start = ((bf16[32,144,128]{2,1,0:T(8,128)(2,1)}), bf16[32,144,128]{2,1,0:T(8,128)(2,1)S(1)}, u32[]{:S(2)}, u32[]{:S(2)}) async-start(bf16[32,144,128]{2,1,0:T(8,128)(2,1)} %shard_map.65), calls=%async_computation | async-start | bytes 2359296 | tf_op jit(solution)/shard_map/all_to_all | solution.py:275
  31.9 13.9 %collective-permute-start.9 = (bf16[4,3,2,64,128]{4,3,1,2,0:T(8,128)(2,1)S(1)}, bf16[4,3,2,64,128]{4,3,1,2,0:T(8,128)(2,1)S(1)}, u32[]{:S(2)}, u32[]{:S(2)}) collective-permute-start(bf16[4,3,2,64,128]{4,3,1,2,0:T(8,128)(2,1)S(1)} %pad_maximum_fusion), channel_id=1, source_target_pairs={{0,3},{1,2},{2,1},{3,0},{4,7},{5,6},{6,5},{7,4},{8,11},{9,10},{10,... | collective-permute-start | bytes 1179656 | tf_op jit(solution)/shard_map/ppermute | solution.py:258
  39.7 8.5 %collective-permute-start.11 = (bf16[4,3,2,64,128]{4,3,2,1,0:T(8,128)(2,1)S(1)}, bf16[4,3,2,64,128]{4,3,2,1,0:T(8,128)(2,1)S(1)}, u32[]{:S(2)}, u32[]{:S(2)}) collective-permute-start(bf16[4,3,2,64,128]{4,3,2,1,0:T(8,128)(2,1)S(1)} %pad_maximum_fusion.1.refs_4_), channel_id=1, source_target_pairs={{0,1},{1,0},{2,3},{3,2},{4,5},{5,4},{6,7},{7,6},{8,9},{9,8},{10,11... | collective-permute-start | bytes 1179656 | tf_op jit(solution)/shard_map/ppermute | solution.py:258
  39.8 15.6 %collective-permute-start.8 = (bf16[4,3,2,64,128]{4,3,1,2,0:T(8,128)(2,1)S(1)}, bf16[4,3,2,64,128]{4,3,1,2,0:T(8,128)(2,1)S(1)}, u32[]{:S(2)}, u32[]{:S(2)}) collective-permute-start(bf16[4,3,2,64,128]{4,3,1,2,0:T(8,128)(2,1)S(1)} %pad_maximum_fusion), channel_id=1, source_target_pairs={{0,1},{1,0},{2,3},{3,2},{4,5},{5,4},{6,7},{7,6},{8,9},{9,8},{10,11... | collective-permute-start | bytes 1179656 | tf_op jit(solution)/shard_map/ppermute | solution.py:258
  45.8 18.0 %collective-permute-start.10 = (bf16[4,3,2,64,128]{4,3,1,2,0:T(8,128)(2,1)S(1)}, bf16[4,3,2,64,128]{4,3,1,2,0:T(8,128)(2,1)S(1)}, u32[]{:S(2)}, u32[]{:S(2)}) collective-permute-start(bf16[4,3,2,64,128]{4,3,1,2,0:T(8,128)(2,1)S(1)} %collective-permute-done.9), channel_id=1, source_target_pairs={{0,1},{1,0},{2,3},{3,2},{4,5},{5,4},{6,7},{7,6},{8,9},{9,8},{10,11... | collective-permute-start | bytes 1179656 | tf_op jit(solution)/shard_map/ppermute | solution.py:258
  45.8 18.5 %collective-permute-start.13 = (bf16[4,3,2,64,128]{4,3,2,1,0:T(8,128)(2,1)S(1)}, bf16[4,3,2,64,128]{4,3,2,1,0:T(8,128)(2,1)}, u32[]{:S(2)}, u32[]{:S(2)}) collective-permute-start(bf16[4,3,2,64,128]{4,3,2,1,0:T(8,128)(2,1)S(1)} %pad_maximum_fusion.1.refs_4_), channel_id=1, source_target_pairs={{0,3},{1,2},{2,1},{3,0},{4,7},{5,6},{6,5},{7,4},{8,11},{9,10},{10,... | collective-permute-start | bytes 1179656 | tf_op jit(solution)/shard_map/ppermute | solution.py:258
  48.2 16.1 %collective-permute-start.12 = (bf16[4,3,2,64,128]{4,3,2,1,0:T(8,128)(2,1)S(1)}, bf16[4,3,2,64,128]{4,3,2,1,0:T(8,128)(2,1)}, u32[]{:S(2)}, u32[]{:S(2)}) collective-permute-start(bf16[4,3,2,64,128]{4,3,2,1,0:T(8,128)(2,1)S(1)} %collective-permute-done.11.refs_5_), channel_id=1, source_target_pairs={{0,3},{1,2},{2,1},{3,0},{4,7},{5,6},{6,5},{7,4},{8,11},{9,10},{10,... | collective-permute-start | bytes 1179656 | tf_op jit(solution)/shard_map/ppermute | solution.py:258
  64.4 9.7 %copy-start = (bf16[128,64]{0,1:T(8,128)(2,1)S(1)}, bf16[128,64]{0,1:T(8,128)(2,1)}, u32[]{:S(2)}) copy-start(bf16[128,64]{0,1:T(8,128)(2,1)} %param.11) | copy-start | bytes 49156
  67.2 6.8 %collective-permute-start.14 = (bf16[4352,128]{1,0:T(8,128)(2,1)S(1)}, bf16[4352,128]{1,0:T(8,128)(2,1)S(1)}, u32[]{:S(2)}, u32[]{:S(2)}) collective-permute-start(bf16[4352,128]{1,0:T(8,128)(2,1)S(1)} %get-tuple-element.36), channel_id=1, source_target_pairs={{0,4},{4,0},{8,12},{12,8},{16,20},{20,16},{24,28},{28,24},{32,36},... | collective-permute-start | bytes 3342344 | tf_op jit(solution)/shard_map/ppermute | solution.py:251

commit v6 on v5

--- a/solution.py
+++ b/solution.py
@@ -57,45 +57,34 @@
 
 
 def local_kernel(start, src_any, ang_any, proj_any, mats_any, *refs):
-    out_ref, src_all, ang_all, proj_ref, mats_ref, sems = refs[-6:]
-    step, steps, width = pl.program_id(0), src_all.shape[0], src_all.shape[2]
-
-    def loads(n):
-        columns = pl.ds((start + n) * width, width)
-        return (
-            pltpu.make_async_copy(src_any.at[:, columns], src_all.at[n], sems.at[n, 0]),
-            pltpu.make_async_copy(ang_any.at[:, columns], ang_all.at[n], sems.at[n, 1]),
+    out_ref, src_ref, ang_ref, proj_ref, mats_ref, sems = refs[-6:]
+    width = src_ref.shape[1]
+    half = width // 2
+    halves = [
+        pltpu.make_async_copy(
+            src_any.at[:, pl.ds(start * width + n * half, half)], src_ref.at[:, pl.ds(n * half, half)], sems.at[n]
         )
-
-    shared = (
-        pltpu.make_async_copy(proj_any, proj_ref, sems.at[steps, 0]),
-        pltpu.make_async_copy(mats_any, mats_ref, sems.at[steps, 1]),
-    )
-
-    @pl.when(step == 0)
-    def _():
-        for copy in (shared[0], *loads(0), shared[1]):
-            copy.start()
-        for n in range(1, steps):
-            for copy in loads(n):
-                copy.start()
-        for copy in shared:
-            copy.wait()
-
-    for n in range(steps):
-
-        @pl.when(step == n)
-        def _():
-            for copy in loads(n):
-                copy.wait()
-
-    src_ref = src_all.at[step]
+        for n in range(2)
+    ]
+    of_proj = pltpu.make_async_copy(proj_any, proj_ref, sems.at[2])
+    of_ang = pltpu.make_async_copy(ang_any.at[:, pl.ds(start * width, width)], ang_ref, sems.at[3])
+    of_mats = pltpu.make_async_copy(mats_any, mats_ref, sems.at[4])
+    for copy in (of_ang, of_proj, *halves, of_mats):
+        copy.start()
     tiles = width // TILE
     levels = mats_ref.shape[0]
-    ang = ang_all[step].astype(F32)
+    of_ang.wait()
+    ang = ang_ref[...].astype(F32)
     cos, sin = cos_sin(ang[:levels])
+    of_proj.wait()
     proj = proj_ref[...]
-    x = [dot(proj, src_ref[:, i * TILE : (i + 1) * TILE]).astype(BF) for i in range(tiles)]
+    x = []
+    for copy in halves:
+        copy.wait()
+        for _ in range(tiles // 2):
+            i = len(x)
+            x.append(dot(proj, src_ref[:, i * TILE : (i + 1) * TILE]).astype(BF))
+    of_mats.wait()
     to = lax.broadcasted_iota(jnp.int32, (TILE, TILE), 1)
     frm = lax.broadcasted_iota(jnp.int32, (TILE, TILE), 0)
     for level in range(levels):
@@ -120,7 +109,7 @@
         out_ref[i, 2 * R :] = jnp.concatenate([a[:, lo:mid], a[:, mid:hi]], axis=0).astype(BF)
 
 
-def local_levels(steps, parts, start, before, source_field, angles, project_mats, local_mats):
+def local_levels(parts, start, before, source_field, angles, project_mats, local_mats):
     q, columns = source_field.shape
     width = columns // parts
     tiles = width // TILE
@@ -129,16 +118,16 @@
         args.append(before)
     return pl.pallas_call(
         functools.partial(local_kernel, start),
-        grid=(steps,),
+        grid=(1,),
         in_specs=[pl.BlockSpec(memory_space=pltpu.HBM)] * len(args),
         out_specs=pl.BlockSpec((tiles, ROWS, 128), lambda i: (start + i, 0, 0)),
         out_shape=jax.ShapeDtypeStruct((BLOCKS, ROWS, 128), BF),
         scratch_shapes=[
-            pltpu.VMEM((steps, q, width), BF),
-            pltpu.VMEM((steps, angles.shape[0], width), BF),
+            pltpu.VMEM((q, width), BF),
+            pltpu.VMEM((angles.shape[0], width), BF),
             pltpu.VMEM(project_mats.shape, BF),
             pltpu.VMEM(local_mats.shape, BF),
-            pltpu.SemaphoreType.DMA((steps + 1, 2)),
+            pltpu.SemaphoreType.DMA((5,)),
         ],
         input_output_aliases={4: 0} if before is not None else {},
         compiler_params=PARAMS,
@@ -214,9 +203,10 @@
     )(moved, cos, sin, *early, *late)
 
 
-def last_kernel(own_ref, oth_ref, eval_ref, out_ref):
+def last_kernel(own_ref, oth_ref, eval_ref, out_any, out_ref, sems):
     low = place()[2] == 0
     ev = eval_ref[...]
+    copies = []
     for n in range(BLOCKS):
         if n % 2 == 0:
             a = BLOCKS * R + n * 8
@@ -231,6 +221,13 @@
         out_ref[:, pl.ds(column, TILE)] = lax.dot_general(
             ev, y, (((0,), (0,)), ((), ())), preferred_element_type=F32
         ).astype(BF)
+        if n % (BLOCKS // NX) == BLOCKS // NX - 1:
+            done = n // (BLOCKS // NX)
+            columns = pl.ds(pl.multiple_of((place()[0] ^ done) * (NZ * TILE), NZ * TILE), NZ * TILE)
+            copies.append(pltpu.make_async_copy(out_ref.at[:, columns], out_any.at[:, columns], sems.at[done]))
+            copies[-1].start()
+    for copy in copies:
+        copy.wait()
 
 
 def last_level(keep, received, evaluate_mats):
@@ -238,8 +235,9 @@
     return pl.pallas_call(
         last_kernel,
         in_specs=[vmem] * 3,
-        out_specs=vmem,
+        out_specs=pl.BlockSpec(memory_space=pl.ANY),
         out_shape=jax.ShapeDtypeStruct((evaluate_mats.shape[1], 64 * 128), BF),
+        scratch_shapes=[pltpu.VMEM((evaluate_mats.shape[1], 64 * 128), BF), pltpu.SemaphoreType.DMA((NX,))],
         compiler_params=SMALL,
     )(keep, received, evaluate_mats)
 
@@ -264,13 +262,13 @@
 
     own = jnp.concatenate([cross_mats[:, 0], cross_mats[:, 1]], axis=-1)
     far = to_plane(own)
-    first = local_levels(1, 2, 0, None, source_field, angles, project_mats, local_mats)
+    first = local_levels(2, 0, None, source_field, angles, project_mats, local_mats)
     far = after(far, first)
     near = swap(far, NC)
     far_x = [far] + [swap(far, j * NZ * NC) for j in (1, 3, 2)]
     near, half = lax.optimization_barrier((near, first))
     near_x = [near] + [swap(near, j * NZ * NC) for j in (1, 3, 2)]
-    sent = local_levels(1, 2, 1, half, source_field, angles, project_mats, local_mats)
+    sent = local_levels(2, 1, half, source_field, angles, project_mats, local_mats)
     sent, *pairs = lax.optimization_barrier((sent, *far_x, *near_x))
     moved = lax.all_to_all(sent, "box", 0, 0, tiled=True, axis_index_groups=chips)
     early, late = (

time: 77.2 us -> 76.9 us (level)
  no operation moved by 1% of the time
where the time goes in v6:
time: 76.9 us; the launch traced here: 76.6 us
  starting transfers between devices  37.2 us (48%)
  waiting for transfers between devices  22.3 us (29%)
  Pallas kernels  15.3 us (20%)
  local copies, waits for them, and re-layouts  1.13 us (1%)
    ppermute x6, waiting for transfers between devices, along_src(): return lax.ppermute(values, 'src', [(p, p ^ t) for p in range(PLANES)])  19.8 us
    ppermute x8, starting transfers between devices, swap(): lax.ppermute(values, 'box', [(i, i ^ distance) for i in range(count)])  14.4 us
    ppermute x6, starting transfers between devices, along_src(): return lax.ppermute(values, 'src', [(p, p ^ t) for p in range(PLANES)])  11.8 us
    all_to_all x1, starting transfers between devices, shards(): lax.all_to_all(sent, 'box', 0, 0, tiled=True, axis_index_groups=chips)  10.3 us
    pallas_call x2, Pallas kernels, local_levels(): pl.pallas_call(functools.partial(local_kernel, start), grid=(1,), in_spec...  9.64 us
    pallas_call x1, Pallas kernels, chip_levels(): pl.pallas_call(chip_kernel, in_specs=[vmem] * 11, out_specs=[vmem, vmem],...  2.86 us
    ppermute x8, waiting for transfers between devices, swap(): lax.ppermute(values, 'box', [(i, i ^ distance) for i in range(count)])  2.5 us
    pallas_call x1, Pallas kernels, last_level(): pl.pallas_call(last_kernel, in_specs=[vmem] * 3, out_specs=pl.BlockSpec(m...  2.35 us
  transfers between devices with their start and end apart: 16, of which 5 were waited for; matrix products, arithmetic and copies ran while one was open for 0% of the time, Pallas kernels for 13%

profile of v6, /device:TPU:1, one launch (start us, length us, event | category | flops | bytes accessed | tf_op | source)
XLA Modules:
  0.0 76.6 jit_solution(14846479631470540182)
XLA Ops:
  0.0 1.0 %slice_bitcast_fusion.1 = (bf16[6,64,64]{2,1,0:T(8,128)(2,1)S(1)}, bf16[6,64,64]{2,1,0:T(8,128)(2,1)S(1)}) fusion(bf16[6,2,64,64]{3,2,1,0:T(8,128)(2,1)} %param.9), kind=kLoop, calls=%fused_computation.12 | loop fusion | bytes 196608 | tf_op jit(solution)/shard_map/squeeze | solution.py:263
  1.0 0.1 pad_maximum_fusion.2
  1.1 0.7 collective-permute-start
  1.7 4.8 %shard_map.64.refs_0_ = bf16[32,144,128]{2,1,0:T(8,128)(2,1)} custom-call(bf16[128,8192]{1,0:T(8,128)(2,1)} %src_any.3, bf16[14,8192]{1,0:T(8,128)(2,1)} %ang_any.3, bf16[64,128]{1,0:T(8,128)(2,1)} %proj_any.3, bf16[8,2,64,64]{3,2,1,0:T(8,128)(2,1)} %mats_any.3), custom_call_target="tpu_custom_call" | custom-call | tf_op jit(solution)/shard_map/pallas_call | solution.py:119
  6.6 2.6 %collective-permute-start.1 = (bf16[6,64,128]{2,1,0:T(8,128)(2,1)S(1)}, bf16[6,64,128]{2,1,0:T(8,128)(2,1)S(1)}, u32[]{:S(2)}, u32[]{:S(2)}) collective-permute-start(bf16[6,64,128]{2,1,0:T(8,128)(2,1)S(1)} %collective-permute-done), channel_id=1, source_target_pairs={{0,8},{4,12},{8,0},{12,4},{16,24},{20,28},{24,16},{28,20},{32,40},... | collective-permute-start | bytes 294920 | tf_op jit(solution)/shard_map/ppermute | solution.py:249
  9.1 2.7 %collective-permute-start.4 = (bf16[6,64,128]{2,1,0:T(8,128)(2,1)S(1)}, bf16[6,64,128]{2,1,0:T(8,128)(2,1)S(1)}, u32[]{:S(2)}, u32[]{:S(2)}) collective-permute-start(bf16[6,64,128]{2,1,0:T(8,128)(2,1)S(1)} %collective-permute-done), channel_id=1, source_target_pairs={{0,128},{4,132},{8,136},{12,140},{16,144},{20,148},{24,152},{28,15... | collective-permute-start | bytes 294920 | tf_op jit(solution)/shard_map/ppermute | solution.py:249
  11.9 0.9 %collective-permute-start.3 = (bf16[6,64,128]{2,1,0:T(8,128)(2,1)S(1)}, bf16[6,64,128]{2,1,0:T(8,128)(2,1)S(1)}, u32[]{:S(2)}, u32[]{:S(2)}) collective-permute-start(bf16[6,64,128]{2,1,0:T(8,128)(2,1)S(1)} %collective-permute-done), channel_id=1, source_target_pairs={{0,192},{4,196},{8,200},{12,204},{16,208},{20,212},{24,216},{28,22... | collective-permute-start | bytes 294920 | tf_op jit(solution)/shard_map/ppermute | solution.py:249
  12.7 3.0 %collective-permute-start.7 = (bf16[6,64,128]{2,1,0:T(8,128)(2,1)S(1)}, bf16[6,64,128]{2,1,0:T(8,128)(2,1)S(1)}, u32[]{:S(2)}, u32[]{:S(2)}) collective-permute-start(bf16[6,64,128]{2,1,0:T(8,128)(2,1)S(1)} %collective-permute-done.1), channel_id=1, source_target_pairs={{0,128},{4,132},{8,136},{12,140},{16,144},{20,148},{24,152},{28,15... | collective-permute-start | bytes 294920 | tf_op jit(solution)/shard_map/ppermute | solution.py:249
  15.7 0.9 %collective-permute-start.6 = (bf16[6,64,128]{2,1,0:T(8,128)(2,1)S(1)}, bf16[6,64,128]{2,1,0:T(8,128)(2,1)S(1)}, u32[]{:S(2)}, u32[]{:S(2)}) collective-permute-start(bf16[6,64,128]{2,1,0:T(8,128)(2,1)S(1)} %collective-permute-done.1), channel_id=1, source_target_pairs={{0,192},{4,196},{8,200},{12,204},{16,208},{20,212},{24,216},{28,22... | collective-permute-start | bytes 294920 | tf_op jit(solution)/shard_map/ppermute | solution.py:249
  16.6 0.0 collective-permute-done.4
  16.6 4.8 %shard_map.65 = bf16[32,144,128]{2,1,0:T(8,128)(2,1)} custom-call(bf16[128,8192]{1,0:T(8,128)(2,1)} %src_any.3, bf16[14,8192]{1,0:T(8,128)(2,1)} %ang_any.3, bf16[64,128]{1,0:T(8,128)(2,1)} %proj_any.3, bf16[8,2,64,64]{3,2,1,0:T(8,128)(2,1)} %mats_any.3, bf16[32,144,128]{2,1,0:T(8,128)(2,1)} %shard_map.64.refs_0_), custom_call_target="tpu_custom_call", output_to_operand_aliasing={{}: (4, {})} | custom-call | tf_op jit(solution)/shard_map/pallas_call | solution.py:119
  21.5 0.0 collective-permute-done.7
  21.5 0.1 collective-permute-done.6
  21.6 0.0 collective-permute-done.5
  21.6 10.3 %all-to-all-start = ((bf16[32,144,128]{2,1,0:T(8,128)(2,1)}), bf16[32,144,128]{2,1,0:T(8,128)(2,1)S(1)}, u32[]{:S(2)}, u32[]{:S(2)}) async-start(bf16[32,144,128]{2,1,0:T(8,128)(2,1)} %shard_map.65), calls=%async_computation | async-start | bytes 2359296 | tf_op jit(solution)/shard_map/all_to_all | solution.py:273
  32.1 0.1 pad_maximum_fusion
  32.1 7.6 %collective-permute-start.9 = (bf16[4,3,2,64,128]{4,3,1,2,0:T(8,128)(2,1)S(1)}, bf16[4,3,2,64,128]{4,3,1,2,0:T(8,128)(2,1)S(1)}, u32[]{:S(2)}, u32[]{:S(2)}) collective-permute-start(bf16[4,3,2,64,128]{4,3,1,2,0:T(8,128)(2,1)S(1)} %pad_maximum_fusion), channel_id=1, source_target_pairs={{0,3},{1,2},{2,1},{3,0},{4,7},{5,6},{6,5},{7,4},{8,11},{9,10},{10,... | collective-permute-start | bytes 1179656 | tf_op jit(solution)/shard_map/ppermute | solution.py:256
  39.8 0.1 collective-permute-start.11
  39.9 1.5 %collective-permute-start.8 = (bf16[4,3,2,64,128]{4,3,1,2,0:T(8,128)(2,1)S(1)}, bf16[4,3,2,64,128]{4,3,1,2,0:T(8,128)(2,1)S(1)}, u32[]{:S(2)}, u32[]{:S(2)}) collective-permute-start(bf16[4,3,2,64,128]{4,3,1,2,0:T(8,128)(2,1)S(1)} %pad_maximum_fusion), channel_id=1, source_target_pairs={{0,1},{1,0},{2,3},{3,2},{4,5},{5,4},{6,7},{7,6},{8,9},{9,8},{10,11... | collective-permute-start | bytes 1179656 | tf_op jit(solution)/shard_map/ppermute | solution.py:256
  41.4 4.6 %collective-permute-done.9 = bf16[4,3,2,64,128]{4,3,1,2,0:T(8,128)(2,1)S(1)} collective-permute-done((bf16[4,3,2,64,128]{4,3,1,2,0:T(8,128)(2,1)S(1)}, bf16[4,3,2,64,128]{4,3,1,2,0:T(8,128)(2,1)S(1)}, u32[]{:S(2)}, u32[]{:S(2)}) %collective-permute-start.9) | collective-permute-done | bytes 393248 | tf_op jit(solution)/shard_map/ppermute | solution.py:256
  46.0 2.4 %collective-permute-start.13 = (bf16[4,3,2,64,128]{4,3,2,1,0:T(8,128)(2,1)S(1)}, bf16[4,3,2,64,128]{4,3,2,1,0:T(8,128)(2,1)}, u32[]{:S(2)}, u32[]{:S(2)}) collective-permute-start(bf16[4,3,2,64,128]{4,3,2,1,0:T(8,128)(2,1)S(1)} %pad_maximum_fusion.1.refs_4_), channel_id=1, source_target_pairs={{0,3},{1,2},{2,1},{3,0},{4,7},{5,6},{6,5},{7,4},{8,11},{9,10},{10,... | collective-permute-start | bytes 1179656 | tf_op jit(solution)/shard_map/ppermute | solution.py:256
  48.3 0.0 collective-permute-done.11.refs_5_
  48.3 0.3 collective-permute-start.12
  48.7 6.9 %collective-permute-done.8 = bf16[4,3,2,64,128]{4,3,1,2,0:T(8,128)(2,1)S(1)} collective-permute-done((bf16[4,3,2,64,128]{4,3,1,2,0:T(8,128)(2,1)S(1)}, bf16[4,3,2,64,128]{4,3,1,2,0:T(8,128)(2,1)S(1)}, u32[]{:S(2)}, u32[]{:S(2)}) %collective-permute-start.8) | collective-permute-done | bytes 393248 | tf_op jit(solution)/shard_map/ppermute | solution.py:256
  55.6 8.4 %collective-permute-done.10 = bf16[4,3,2,64,128]{4,3,1,2,0:T(8,128)(2,1)S(1)} collective-permute-done((bf16[4,3,2,64,128]{4,3,1,2,0:T(8,128)(2,1)S(1)}, bf16[4,3,2,64,128]{4,3,1,2,0:T(8,128)(2,1)S(1)}, u32[]{:S(2)}, u32[]{:S(2)}) %collective-permute-start.10) | collective-permute-done | bytes 393248 | tf_op jit(solution)/shard_map/ppermute | solution.py:256
  64.0 0.0 all-to-all-done.ang_ref.data_ref
  64.0 0.4 shard_map.66
  64.5 0.0 copy-start
  64.5 2.9 %shard_map.67 = (bf16[4352,128]{1,0:T(8,128)(2,1)S(1)}, bf16[4352,128]{1,0:T(8,128)(2,1)S(1)}) custom-call(bf16[32,144,128]{2,1,0:T(8,128)(2,1)S(1)} %all-to-all-done.ang_ref.data_ref, f32[32,16,128]{2,1,0:T(8,128)S(1)} %get-tuple-element.25.cos_ref, f32[32,16,128]{2,1,0:T(8,128)S(1)} %get-tuple-element.26.sin_ref, ...), custom_call_target="tpu_custom_call" | custom-call | tf_op jit(solution)/shard_map/pallas_call | solution.py:197
  67.4 4.4 %collective-permute-start.14 = (bf16[4352,128]{1,0:T(8,128)(2,1)S(1)}, bf16[4352,128]{1,0:T(8,128)(2,1)S(1)}, u32[]{:S(2)}, u32[]{:S(2)}) collective-permute-start(bf16[4352,128]{1,0:T(8,128)(2,1)S(1)} %get-tuple-element.36), channel_id=1, source_target_pairs={{0,4},{4,0},{8,12},{12,8},{16,20},{20,16},{24,28},{28,24},{32,36},... | collective-permute-start | bytes 3342344 | tf_op jit(solution)/shard_map/ppermute | solution.py:249
  71.7 2.4 %collective-permute-done.14.oth_ref = bf16[4352,128]{1,0:T(8,128)(2,1)S(1)} collective-permute-done((bf16[4352,128]{1,0:T(8,128)(2,1)S(1)}, bf16[4352,128]{1,0:T(8,128)(2,1)S(1)}, u32[]{:S(2)}, u32[]{:S(2)}) %collective-permute-start.14) | collective-permute-done | bytes 1114144 | tf_op jit(solution)/shard_map/ppermute | solution.py:249
  74.1 2.3 %shard_map.68 = bf16[128,8192]{1,0:T(8,128)(2,1)} custom-call(bf16[4352,128]{1,0:T(8,128)(2,1)S(1)} %get-tuple-element.35.own_ref, bf16[4352,128]{1,0:T(8,128)(2,1)S(1)} %collective-permute-done.14.oth_ref, bf16[64,128]{1,0:T(8,128)(2,1)S(1)} %bitcast.61), custom_call_target="tpu_custom_call" | custom-call | tf_op jit(solution)/shard_map/pallas_call | solution.py:235
  (26 shorter events, 0.3 us)
Async XLA Ops:
  1.1 5.5 %collective-permute-start = (bf16[6,64,128]{2,1,0:T(8,128)(2,1)S(1)}, bf16[6,64,128]{2,1,0:T(8,128)(2,1)S(1)}, u32[]{:S(2)}, u32[]{:S(2)}) collective-permute-start(bf16[6,64,128]{2,1,0:T(8,128)(2,1)S(1)} %pad_maximum_fusion.2), channel_id=1, source_target_pairs={{0,0},{1,17},{2,34},{3,51},{4,4},{5,21},{6,38},{7,55},{8,8},{9,25}... | collective-permute-start | bytes 294920 | tf_op jit(solution)/shard_map/ppermute | solution.py:253
  6.6 6.2 %collective-permute-start.1 = (bf16[6,64,128]{2,1,0:T(8,128)(2,1)S(1)}, bf16[6,64,128]{2,1,0:T(8,128)(2,1)S(1)}, u32[]{:S(2)}, u32[]{:S(2)}) collective-permute-start(bf16[6,64,128]{2,1,0:T(8,128)(2,1)S(1)} %collective-permute-done), channel_id=1, source_target_pairs={{0,8},{4,12},{8,0},{12,4},{16,24},{20,28},{24,16},{28,20},{32,40},... | collective-permute-start | bytes 294920 | tf_op jit(solution)/shard_map/ppermute | solution.py:249
  9.1 7.5 %collective-permute-start.4 = (bf16[6,64,128]{2,1,0:T(8,128)(2,1)S(1)}, bf16[6,64,128]{2,1,0:T(8,128)(2,1)S(1)}, u32[]{:S(2)}, u32[]{:S(2)}) collective-permute-start(bf16[6,64,128]{2,1,0:T(8,128)(2,1)S(1)} %collective-permute-done), channel_id=1, source_target_pairs={{0,128},{4,132},{8,136},{12,140},{16,144},{20,148},{24,152},{28,15... | collective-permute-start | bytes 294920 | tf_op jit(solution)/shard_map/ppermute | solution.py:249
  11.9 9.6 %collective-permute-start.3 = (bf16[6,64,128]{2,1,0:T(8,128)(2,1)S(1)}, bf16[6,64,128]{2,1,0:T(8,128)(2,1)S(1)}, u32[]{:S(2)}, u32[]{:S(2)}) collective-permute-start(bf16[6,64,128]{2,1,0:T(8,128)(2,1)S(1)} %collective-permute-done), channel_id=1, source_target_pairs={{0,192},{4,196},{8,200},{12,204},{16,208},{20,212},{24,216},{28,22... | collective-permute-start | bytes 294920 | tf_op jit(solution)/shard_map/ppermute | solution.py:249
  12.7 8.7 %collective-permute-start.2 = (bf16[6,64,128]{2,1,0:T(8,128)(2,1)S(1)}, bf16[6,64,128]{2,1,0:T(8,128)(2,1)S(1)}, u32[]{:S(2)}, u32[]{:S(2)}) collective-permute-start(bf16[6,64,128]{2,1,0:T(8,128)(2,1)S(1)} %collective-permute-done), channel_id=1, source_target_pairs={{0,64},{4,68},{8,72},{12,76},{16,80},{20,84},{24,88},{28,92},{32,9... | collective-permute-start | bytes 294920 | tf_op jit(solution)/shard_map/ppermute | solution.py:249
  12.7 8.7 %collective-permute-start.7 = (bf16[6,64,128]{2,1,0:T(8,128)(2,1)S(1)}, bf16[6,64,128]{2,1,0:T(8,128)(2,1)S(1)}, u32[]{:S(2)}, u32[]{:S(2)}) collective-permute-start(bf16[6,64,128]{2,1,0:T(8,128)(2,1)S(1)} %collective-permute-done.1), channel_id=1, source_target_pairs={{0,128},{4,132},{8,136},{12,140},{16,144},{20,148},{24,152},{28,15... | collective-permute-start | bytes 294920 | tf_op jit(solution)/shard_map/ppermute | solution.py:249
  15.7 5.8 %collective-permute-start.6 = (bf16[6,64,128]{2,1,0:T(8,128)(2,1)S(1)}, bf16[6,64,128]{2,1,0:T(8,128)(2,1)S(1)}, u32[]{:S(2)}, u32[]{:S(2)}) collective-permute-start(bf16[6,64,128]{2,1,0:T(8,128)(2,1)S(1)} %collective-permute-done.1), channel_id=1, source_target_pairs={{0,192},{4,196},{8,200},{12,204},{16,208},{20,212},{24,216},{28,22... | collective-permute-start | bytes 294920 | tf_op jit(solution)/shard_map/ppermute | solution.py:249
  16.6 5.0 %collective-permute-start.5 = (bf16[6,64,128]{2,1,0:T(8,128)(2,1)S(1)}, bf16[6,64,128]{2,1,0:T(8,128)(2,1)S(1)}, u32[]{:S(2)}, u32[]{:S(2)}) collective-permute-start(bf16[6,64,128]{2,1,0:T(8,128)(2,1)S(1)} %collective-permute-done.1), channel_id=1, source_target_pairs={{0,64},{4,68},{8,72},{12,76},{16,80},{20,84},{24,88},{28,92},{32,9... | collective-permute-start | bytes 294920 | tf_op jit(solution)/shard_map/ppermute | solution.py:249
  21.6 42.5 %all-to-all-start = ((bf16[32,144,128]{2,1,0:T(8,128)(2,1)}), bf16[32,144,128]{2,1,0:T(8,128)(2,1)S(1)}, u32[]{:S(2)}, u32[]{:S(2)}) async-start(bf16[32,144,128]{2,1,0:T(8,128)(2,1)} %shard_map.65), calls=%async_computation | async-start | bytes 2359296 | tf_op jit(solution)/shard_map/all_to_all | solution.py:273
  32.1 13.8 %collective-permute-start.9 = (bf16[4,3,2,64,128]{4,3,1,2,0:T(8,128)(2,1)S(1)}, bf16[4,3,2,64,128]{4,3,1,2,0:T(8,128)(2,1)S(1)}, u32[]{:S(2)}, u32[]{:S(2)}) collective-permute-start(bf16[4,3,2,64,128]{4,3,1,2,0:T(8,128)(2,1)S(1)} %pad_maximum_fusion), channel_id=1, source_target_pairs={{0,3},{1,2},{2,1},{3,0},{4,7},{5,6},{6,5},{7,4},{8,11},{9,10},{10,... | collective-permute-start | bytes 1179656 | tf_op jit(solution)/shard_map/ppermute | solution.py:256
  39.8 8.5 %collective-permute-start.11 = (bf16[4,3,2,64,128]{4,3,2,1,0:T(8,128)(2,1)S(1)}, bf16[4,3,2,64,128]{4,3,2,1,0:T(8,128)(2,1)S(1)}, u32[]{:S(2)}, u32[]{:S(2)}) collective-permute-start(bf16[4,3,2,64,128]{4,3,2,1,0:T(8,128)(2,1)S(1)} %pad_maximum_fusion.1.refs_4_), channel_id=1, source_target_pairs={{0,1},{1,0},{2,3},{3,2},{4,5},{5,4},{6,7},{7,6},{8,9},{9,8},{10,11... | collective-permute-start | bytes 1179656 | tf_op jit(solution)/shard_map/ppermute | solution.py:256
  39.9 15.6 %collective-permute-start.8 = (bf16[4,3,2,64,128]{4,3,1,2,0:T(8,128)(2,1)S(1)}, bf16[4,3,2,64,128]{4,3,1,2,0:T(8,128)(2,1)S(1)}, u32[]{:S(2)}, u32[]{:S(2)}) collective-permute-start(bf16[4,3,2,64,128]{4,3,1,2,0:T(8,128)(2,1)S(1)} %pad_maximum_fusion), channel_id=1, source_target_pairs={{0,1},{1,0},{2,3},{3,2},{4,5},{5,4},{6,7},{7,6},{8,9},{9,8},{10,11... | collective-permute-start | bytes 1179656 | tf_op jit(solution)/shard_map/ppermute | solution.py:256
  45.9 18.0 %collective-permute-start.10 = (bf16[4,3,2,64,128]{4,3,1,2,0:T(8,128)(2,1)S(1)}, bf16[4,3,2,64,128]{4,3,1,2,0:T(8,128)(2,1)S(1)}, u32[]{:S(2)}, u32[]{:S(2)}) collective-permute-start(bf16[4,3,2,64,128]{4,3,1,2,0:T(8,128)(2,1)S(1)} %collective-permute-done.9), channel_id=1, source_target_pairs={{0,1},{1,0},{2,3},{3,2},{4,5},{5,4},{6,7},{7,6},{8,9},{9,8},{10,11... | collective-permute-start | bytes 1179656 | tf_op jit(solution)/shard_map/ppermute | solution.py:256
  46.0 18.5 %collective-permute-start.13 = (bf16[4,3,2,64,128]{4,3,2,1,0:T(8,128)(2,1)S(1)}, bf16[4,3,2,64,128]{4,3,2,1,0:T(8,128)(2,1)}, u32[]{:S(2)}, u32[]{:S(2)}) collective-permute-start(bf16[4,3,2,64,128]{4,3,2,1,0:T(8,128)(2,1)S(1)} %pad_maximum_fusion.1.refs_4_), channel_id=1, source_target_pairs={{0,3},{1,2},{2,1},{3,0},{4,7},{5,6},{6,5},{7,4},{8,11},{9,10},{10,... | collective-permute-start | bytes 1179656 | tf_op jit(solution)/shard_map/ppermute | solution.py:256
  48.3 16.1 %collective-permute-start.12 = (bf16[4,3,2,64,128]{4,3,2,1,0:T(8,128)(2,1)S(1)}, bf16[4,3,2,64,128]{4,3,2,1,0:T(8,128)(2,1)}, u32[]{:S(2)}, u32[]{:S(2)}) collective-permute-start(bf16[4,3,2,64,128]{4,3,2,1,0:T(8,128)(2,1)S(1)} %collective-permute-done.11.refs_5_), channel_id=1, source_target_pairs={{0,3},{1,2},{2,1},{3,0},{4,7},{5,6},{6,5},{7,4},{8,11},{9,10},{10,... | collective-permute-start | bytes 1179656 | tf_op jit(solution)/shard_map/ppermute | solution.py:256
  64.5 9.6 %copy-start = (bf16[128,64]{0,1:T(8,128)(2,1)S(1)}, bf16[128,64]{0,1:T(8,128)(2,1)}, u32[]{:S(2)}) copy-start(bf16[128,64]{0,1:T(8,128)(2,1)} %param.11) | copy-start | bytes 49156
  67.4 6.8 %collective-permute-start.14 = (bf16[4352,128]{1,0:T(8,128)(2,1)S(1)}, bf16[4352,128]{1,0:T(8,128)(2,1)S(1)}, u32[]{:S(2)}, u32[]{:S(2)}) collective-permute-start(bf16[4352,128]{1,0:T(8,128)(2,1)S(1)} %get-tuple-element.36), channel_id=1, source_target_pairs={{0,4},{4,0},{8,12},{12,8},{16,20},{20,16},{24,28},{28,24},{32,36},... | collective-permute-start | bytes 3342344 | tf_op jit(solution)/shard_map/ppermute | solution.py:249

commit v7 on v6

--- a/solution.py
+++ b/solution.py
@@ -54,6 +54,13 @@
 
 def row(values, i):
     return values[i : i + 1].astype(BF)
+
+
+def swapped(values, span):
+    if span == 64:
+        return pltpu.roll(values, 64, 1)
+    upper = (lax.broadcasted_iota(jnp.int32, values.shape, 1) & span) != 0
+    return jnp.where(upper, pltpu.roll(values, span, 1), pltpu.roll(values, 128 - span, 1))
 
 
 def local_kernel(start, src_any, ang_any, proj_any, mats_any, *refs):
@@ -93,8 +100,10 @@
             xp = [jnp.concatenate([v[:, 128:], v[:, :128]], axis=1) for v in x]
         else:
             perm = jnp.where(frm == (to ^ span), 1.0, 0.0).astype(BF)
-            every = dot(jnp.concatenate(x, axis=0), perm).astype(BF)
-            xp = [every[i * R : (i + 1) * R] for i in range(tiles)]
+            product = tiles - tiles // 3
+            every = dot(jnp.concatenate(x[:product], axis=0), perm).astype(BF)
+            xp = [every[i * R : (i + 1) * R] for i in range(product)]
+            xp += [jnp.concatenate([swapped(v[:, :128], span), swapped(v[:, 128:], span)], axis=1) for v in x[product:]]
         mat = jnp.concatenate([mats_ref[level, 0], mats_ref[level, 1]], axis=1)
         c, s = row(cos, level), row(sin, level)
         x = [

time: 76.9 us -> 76.7 us (level)
  no operation moved by 1% of the time
where the time goes in v7:
time: 76.7 us; the launch traced here: 76.4 us
  starting transfers between devices  37.2 us (49%)
  waiting for transfers between devices  22.5 us (29%)
  Pallas kernels  14.9 us (19%)
  local copies, waits for them, and re-layouts  1.13 us (1%)
    ppermute x6, waiting for transfers between devices, along_src(): return lax.ppermute(values, 'src', [(p, p ^ t) for p in range(PLANES)])  19.8 us
    ppermute x8, starting transfers between devices, swap(): lax.ppermute(values, 'box', [(i, i ^ distance) for i in range(count)])  14.4 us
    ppermute x6, starting transfers between devices, along_src(): return lax.ppermute(values, 'src', [(p, p ^ t) for p in range(PLANES)])  12 us
    all_to_all x1, starting transfers between devices, shards(): lax.all_to_all(sent, 'box', 0, 0, tiled=True, axis_index_groups=chips)  10.1 us
    pallas_call x2, Pallas kernels, local_levels(): pl.pallas_call(functools.partial(local_kernel, start), grid=(1,), in_spec...  9.28 us
    pallas_call x1, Pallas kernels, chip_levels(): pl.pallas_call(chip_kernel, in_specs=[vmem] * 11, out_specs=[vmem, vmem],...  2.86 us
    ppermute x8, waiting for transfers between devices, swap(): lax.ppermute(values, 'box', [(i, i ^ distance) for i in range(count)])  2.66 us
    pallas_call x1, Pallas kernels, last_level(): pl.pallas_call(last_kernel, in_specs=[vmem] * 3, out_specs=pl.BlockSpec(m...  2.35 us
  transfers between devices with their start and end apart: 16, of which 5 were waited for; matrix products, arithmetic and copies ran while one was open for 0% of the time, Pallas kernels for 13%

profile of v7, /device:TPU:1, one launch (start us, length us, event | category | flops | bytes accessed | tf_op | source)
XLA Modules:
  0.0 76.4 jit_solution(13963662506744404980)
XLA Ops:
  0.0 1.0 %slice_bitcast_fusion.1 = (bf16[6,64,64]{2,1,0:T(8,128)(2,1)S(1)}, bf16[6,64,64]{2,1,0:T(8,128)(2,1)S(1)}) fusion(bf16[6,2,64,64]{3,2,1,0:T(8,128)(2,1)} %param.9), kind=kLoop, calls=%fused_computation.12 | loop fusion | bytes 196608 | tf_op jit(solution)/shard_map/squeeze | solution.py:272
  1.0 0.1 pad_maximum_fusion.2
  1.1 0.7 collective-permute-start
  1.7 4.6 %shard_map.64.refs_0_ = bf16[32,144,128]{2,1,0:T(8,128)(2,1)} custom-call(bf16[128,8192]{1,0:T(8,128)(2,1)} %src_any.3, bf16[14,8192]{1,0:T(8,128)(2,1)} %ang_any.3, bf16[64,128]{1,0:T(8,128)(2,1)} %proj_any.3, bf16[8,2,64,64]{3,2,1,0:T(8,128)(2,1)} %mats_any.3), custom_call_target="tpu_custom_call" | custom-call | tf_op jit(solution)/shard_map/pallas_call | solution.py:128
  6.4 2.6 %collective-permute-start.1 = (bf16[6,64,128]{2,1,0:T(8,128)(2,1)S(1)}, bf16[6,64,128]{2,1,0:T(8,128)(2,1)S(1)}, u32[]{:S(2)}, u32[]{:S(2)}) collective-permute-start(bf16[6,64,128]{2,1,0:T(8,128)(2,1)S(1)} %collective-permute-done), channel_id=1, source_target_pairs={{0,8},{4,12},{8,0},{12,4},{16,24},{20,28},{24,16},{28,20},{32,40},... | collective-permute-start | bytes 294920 | tf_op jit(solution)/shard_map/ppermute | solution.py:258
  9.0 2.7 %collective-permute-start.4 = (bf16[6,64,128]{2,1,0:T(8,128)(2,1)S(1)}, bf16[6,64,128]{2,1,0:T(8,128)(2,1)S(1)}, u32[]{:S(2)}, u32[]{:S(2)}) collective-permute-start(bf16[6,64,128]{2,1,0:T(8,128)(2,1)S(1)} %collective-permute-done), channel_id=1, source_target_pairs={{0,128},{4,132},{8,136},{12,140},{16,144},{20,148},{24,152},{28,15... | collective-permute-start | bytes 294920 | tf_op jit(solution)/shard_map/ppermute | solution.py:258
  11.7 0.9 %collective-permute-start.3 = (bf16[6,64,128]{2,1,0:T(8,128)(2,1)S(1)}, bf16[6,64,128]{2,1,0:T(8,128)(2,1)S(1)}, u32[]{:S(2)}, u32[]{:S(2)}) collective-permute-start(bf16[6,64,128]{2,1,0:T(8,128)(2,1)S(1)} %collective-permute-done), channel_id=1, source_target_pairs={{0,192},{4,196},{8,200},{12,204},{16,208},{20,212},{24,216},{28,22... | collective-permute-start | bytes 294920 | tf_op jit(solution)/shard_map/ppermute | solution.py:258
  12.6 0.0 collective-permute-start.2
  12.6 3.0 %collective-permute-start.7 = (bf16[6,64,128]{2,1,0:T(8,128)(2,1)S(1)}, bf16[6,64,128]{2,1,0:T(8,128)(2,1)S(1)}, u32[]{:S(2)}, u32[]{:S(2)}) collective-permute-start(bf16[6,64,128]{2,1,0:T(8,128)(2,1)S(1)} %collective-permute-done.1), channel_id=1, source_target_pairs={{0,128},{4,132},{8,136},{12,140},{16,144},{20,148},{24,152},{28,15... | collective-permute-start | bytes 294920 | tf_op jit(solution)/shard_map/ppermute | solution.py:258
  15.6 0.9 %collective-permute-start.6 = (bf16[6,64,128]{2,1,0:T(8,128)(2,1)S(1)}, bf16[6,64,128]{2,1,0:T(8,128)(2,1)S(1)}, u32[]{:S(2)}, u32[]{:S(2)}) collective-permute-start(bf16[6,64,128]{2,1,0:T(8,128)(2,1)S(1)} %collective-permute-done.1), channel_id=1, source_target_pairs={{0,192},{4,196},{8,200},{12,204},{16,208},{20,212},{24,216},{28,22... | collective-permute-start | bytes 294920 | tf_op jit(solution)/shard_map/ppermute | solution.py:258
  16.4 0.0 collective-permute-done.4
  16.4 0.0 collective-permute-start.5
  16.4 4.6 %shard_map.65 = bf16[32,144,128]{2,1,0:T(8,128)(2,1)} custom-call(bf16[128,8192]{1,0:T(8,128)(2,1)} %src_any.3, bf16[14,8192]{1,0:T(8,128)(2,1)} %ang_any.3, bf16[64,128]{1,0:T(8,128)(2,1)} %proj_any.3, bf16[8,2,64,64]{3,2,1,0:T(8,128)(2,1)} %mats_any.3, bf16[32,144,128]{2,1,0:T(8,128)(2,1)} %shard_map.64.refs_0_), custom_call_target="tpu_custom_call", output_to_operand_aliasing={{}: (4, {})} | custom-call | tf_op jit(solution)/shard_map/pallas_call | solution.py:128
  21.1 0.0 collective-permute-done.3
  21.1 0.3 collective-permute-done.6
  21.4 10.1 %all-to-all-start = ((bf16[32,144,128]{2,1,0:T(8,128)(2,1)}), bf16[32,144,128]{2,1,0:T(8,128)(2,1)S(1)}, u32[]{:S(2)}, u32[]{:S(2)}) async-start(bf16[32,144,128]{2,1,0:T(8,128)(2,1)} %shard_map.65), calls=%async_computation | async-start | bytes 2359296 | tf_op jit(solution)/shard_map/all_to_all | solution.py:282
  31.7 0.1 pad_maximum_fusion
  31.8 7.8 %collective-permute-start.9 = (bf16[4,3,2,64,128]{4,3,1,2,0:T(8,128)(2,1)S(1)}, bf16[4,3,2,64,128]{4,3,1,2,0:T(8,128)(2,1)S(1)}, u32[]{:S(2)}, u32[]{:S(2)}) collective-permute-start(bf16[4,3,2,64,128]{4,3,1,2,0:T(8,128)(2,1)S(1)} %pad_maximum_fusion), channel_id=1, source_target_pairs={{0,3},{1,2},{2,1},{3,0},{4,7},{5,6},{6,5},{7,4},{8,11},{9,10},{10,... | collective-permute-start | bytes 1179656 | tf_op jit(solution)/shard_map/ppermute | solution.py:265
  39.6 0.1 collective-permute-start.11
  39.7 1.5 %collective-permute-start.8 = (bf16[4,3,2,64,128]{4,3,1,2,0:T(8,128)(2,1)S(1)}, bf16[4,3,2,64,128]{4,3,1,2,0:T(8,128)(2,1)S(1)}, u32[]{:S(2)}, u32[]{:S(2)}) collective-permute-start(bf16[4,3,2,64,128]{4,3,1,2,0:T(8,128)(2,1)S(1)} %pad_maximum_fusion), channel_id=1, source_target_pairs={{0,1},{1,0},{2,3},{3,2},{4,5},{5,4},{6,7},{7,6},{8,9},{9,8},{10,11... | collective-permute-start | bytes 1179656 | tf_op jit(solution)/shard_map/ppermute | solution.py:265
  41.2 4.6 %collective-permute-done.9 = bf16[4,3,2,64,128]{4,3,1,2,0:T(8,128)(2,1)S(1)} collective-permute-done((bf16[4,3,2,64,128]{4,3,1,2,0:T(8,128)(2,1)S(1)}, bf16[4,3,2,64,128]{4,3,1,2,0:T(8,128)(2,1)S(1)}, u32[]{:S(2)}, u32[]{:S(2)}) %collective-permute-start.9) | collective-permute-done | bytes 393248 | tf_op jit(solution)/shard_map/ppermute | solution.py:265
  45.8 0.0 collective-permute-start.10
  45.8 2.4 %collective-permute-start.13 = (bf16[4,3,2,64,128]{4,3,2,1,0:T(8,128)(2,1)S(1)}, bf16[4,3,2,64,128]{4,3,2,1,0:T(8,128)(2,1)}, u32[]{:S(2)}, u32[]{:S(2)}) collective-permute-start(bf16[4,3,2,64,128]{4,3,2,1,0:T(8,128)(2,1)S(1)} %pad_maximum_fusion.1.refs_4_), channel_id=1, source_target_pairs={{0,3},{1,2},{2,1},{3,0},{4,7},{5,6},{6,5},{7,4},{8,11},{9,10},{10,... | collective-permute-start | bytes 1179656 | tf_op jit(solution)/shard_map/ppermute | solution.py:265
  48.2 0.3 collective-permute-start.12
  48.5 6.9 %collective-permute-done.8 = bf16[4,3,2,64,128]{4,3,1,2,0:T(8,128)(2,1)S(1)} collective-permute-done((bf16[4,3,2,64,128]{4,3,1,2,0:T(8,128)(2,1)S(1)}, bf16[4,3,2,64,128]{4,3,1,2,0:T(8,128)(2,1)S(1)}, u32[]{:S(2)}, u32[]{:S(2)}) %collective-permute-start.8) | collective-permute-done | bytes 393248 | tf_op jit(solution)/shard_map/ppermute | solution.py:265
  55.4 8.4 %collective-permute-done.10 = bf16[4,3,2,64,128]{4,3,1,2,0:T(8,128)(2,1)S(1)} collective-permute-done((bf16[4,3,2,64,128]{4,3,1,2,0:T(8,128)(2,1)S(1)}, bf16[4,3,2,64,128]{4,3,1,2,0:T(8,128)(2,1)S(1)}, u32[]{:S(2)}, u32[]{:S(2)}) %collective-permute-start.10) | collective-permute-done | bytes 393248 | tf_op jit(solution)/shard_map/ppermute | solution.py:265
  63.9 0.4 shard_map.66
  64.3 0.0 copy-start
  64.3 2.9 %shard_map.67 = (bf16[4352,128]{1,0:T(8,128)(2,1)S(1)}, bf16[4352,128]{1,0:T(8,128)(2,1)S(1)}) custom-call(bf16[32,144,128]{2,1,0:T(8,128)(2,1)S(1)} %all-to-all-done.ang_ref.data_ref, f32[32,16,128]{2,1,0:T(8,128)S(1)} %get-tuple-element.25.cos_ref, f32[32,16,128]{2,1,0:T(8,128)S(1)} %get-tuple-element.26.sin_ref, ...), custom_call_target="tpu_custom_call" | custom-call | tf_op jit(solution)/shard_map/pallas_call | solution.py:206
  67.2 4.4 %collective-permute-start.14 = (bf16[4352,128]{1,0:T(8,128)(2,1)S(1)}, bf16[4352,128]{1,0:T(8,128)(2,1)S(1)}, u32[]{:S(2)}, u32[]{:S(2)}) collective-permute-start(bf16[4352,128]{1,0:T(8,128)(2,1)S(1)} %get-tuple-element.36), channel_id=1, source_target_pairs={{0,4},{4,0},{8,12},{12,8},{16,20},{20,16},{24,28},{28,24},{32,36},... | collective-permute-start | bytes 3342344 | tf_op jit(solution)/shard_map/ppermute | solution.py:258
  71.6 2.4 %collective-permute-done.14.oth_ref = bf16[4352,128]{1,0:T(8,128)(2,1)S(1)} collective-permute-done((bf16[4352,128]{1,0:T(8,128)(2,1)S(1)}, bf16[4352,128]{1,0:T(8,128)(2,1)S(1)}, u32[]{:S(2)}, u32[]{:S(2)}) %collective-permute-start.14) | collective-permute-done | bytes 1114144 | tf_op jit(solution)/shard_map/ppermute | solution.py:258
  73.9 2.3 %shard_map.68 = bf16[128,8192]{1,0:T(8,128)(2,1)} custom-call(bf16[4352,128]{1,0:T(8,128)(2,1)S(1)} %get-tuple-element.35.own_ref, bf16[4352,128]{1,0:T(8,128)(2,1)S(1)} %collective-permute-done.14.oth_ref, bf16[64,128]{1,0:T(8,128)(2,1)S(1)} %bitcast.61), custom_call_target="tpu_custom_call" | custom-call | tf_op jit(solution)/shard_map/pallas_call | solution.py:244
  (26 shorter events, 0.3 us)
Async XLA Ops:
  1.1 5.3 %collective-permute-start = (bf16[6,64,128]{2,1,0:T(8,128)(2,1)S(1)}, bf16[6,64,128]{2,1,0:T(8,128)(2,1)S(1)}, u32[]{:S(2)}, u32[]{:S(2)}) collective-permute-start(bf16[6,64,128]{2,1,0:T(8,128)(2,1)S(1)} %pad_maximum_fusion.2), channel_id=1, source_target_pairs={{0,0},{1,17},{2,34},{3,51},{4,4},{5,21},{6,38},{7,55},{8,8},{9,25}... | collective-permute-start | bytes 294920 | tf_op jit(solution)/shard_map/ppermute | solution.py:262
  6.4 6.2 %collective-permute-start.1 = (bf16[6,64,128]{2,1,0:T(8,128)(2,1)S(1)}, bf16[6,64,128]{2,1,0:T(8,128)(2,1)S(1)}, u32[]{:S(2)}, u32[]{:S(2)}) collective-permute-start(bf16[6,64,128]{2,1,0:T(8,128)(2,1)S(1)} %collective-permute-done), channel_id=1, source_target_pairs={{0,8},{4,12},{8,0},{12,4},{16,24},{20,28},{24,16},{28,20},{32,40},... | collective-permute-start | bytes 294920 | tf_op jit(solution)/shard_map/ppermute | solution.py:258
  9.0 7.5 %collective-permute-start.4 = (bf16[6,64,128]{2,1,0:T(8,128)(2,1)S(1)}, bf16[6,64,128]{2,1,0:T(8,128)(2,1)S(1)}, u32[]{:S(2)}, u32[]{:S(2)}) collective-permute-start(bf16[6,64,128]{2,1,0:T(8,128)(2,1)S(1)} %collective-permute-done), channel_id=1, source_target_pairs={{0,128},{4,132},{8,136},{12,140},{16,144},{20,148},{24,152},{28,15... | collective-permute-start | bytes 294920 | tf_op jit(solution)/shard_map/ppermute | solution.py:258
  11.7 9.4 %collective-permute-start.3 = (bf16[6,64,128]{2,1,0:T(8,128)(2,1)S(1)}, bf16[6,64,128]{2,1,0:T(8,128)(2,1)S(1)}, u32[]{:S(2)}, u32[]{:S(2)}) collective-permute-start(bf16[6,64,128]{2,1,0:T(8,128)(2,1)S(1)} %collective-permute-done), channel_id=1, source_target_pairs={{0,192},{4,196},{8,200},{12,204},{16,208},{20,212},{24,216},{28,22... | collective-permute-start | bytes 294920 | tf_op jit(solution)/shard_map/ppermute | solution.py:258
  12.6 8.5 %collective-permute-start.2 = (bf16[6,64,128]{2,1,0:T(8,128)(2,1)S(1)}, bf16[6,64,128]{2,1,0:T(8,128)(2,1)S(1)}, u32[]{:S(2)}, u32[]{:S(2)}) collective-permute-start(bf16[6,64,128]{2,1,0:T(8,128)(2,1)S(1)} %collective-permute-done), channel_id=1, source_target_pairs={{0,64},{4,68},{8,72},{12,76},{16,80},{20,84},{24,88},{28,92},{32,9... | collective-permute-start | bytes 294920 | tf_op jit(solution)/shard_map/ppermute | solution.py:258
  12.6 8.5 %collective-permute-start.7 = (bf16[6,64,128]{2,1,0:T(8,128)(2,1)S(1)}, bf16[6,64,128]{2,1,0:T(8,128)(2,1)S(1)}, u32[]{:S(2)}, u32[]{:S(2)}) collective-permute-start(bf16[6,64,128]{2,1,0:T(8,128)(2,1)S(1)} %collective-permute-done.1), channel_id=1, source_target_pairs={{0,128},{4,132},{8,136},{12,140},{16,144},{20,148},{24,152},{28,15... | collective-permute-start | bytes 294920 | tf_op jit(solution)/shard_map/ppermute | solution.py:258
  15.6 5.8 %collective-permute-start.6 = (bf16[6,64,128]{2,1,0:T(8,128)(2,1)S(1)}, bf16[6,64,128]{2,1,0:T(8,128)(2,1)S(1)}, u32[]{:S(2)}, u32[]{:S(2)}) collective-permute-start(bf16[6,64,128]{2,1,0:T(8,128)(2,1)S(1)} %collective-permute-done.1), channel_id=1, source_target_pairs={{0,192},{4,196},{8,200},{12,204},{16,208},{20,212},{24,216},{28,22... | collective-permute-start | bytes 294920 | tf_op jit(solution)/shard_map/ppermute | solution.py:258
  16.4 5.0 %collective-permute-start.5 = (bf16[6,64,128]{2,1,0:T(8,128)(2,1)S(1)}, bf16[6,64,128]{2,1,0:T(8,128)(2,1)S(1)}, u32[]{:S(2)}, u32[]{:S(2)}) collective-permute-start(bf16[6,64,128]{2,1,0:T(8,128)(2,1)S(1)} %collective-permute-done.1), channel_id=1, source_target_pairs={{0,64},{4,68},{8,72},{12,76},{16,80},{20,84},{24,88},{28,92},{32,9... | collective-permute-start | bytes 294920 | tf_op jit(solution)/shard_map/ppermute | solution.py:258
  21.4 42.5 %all-to-all-start = ((bf16[32,144,128]{2,1,0:T(8,128)(2,1)}), bf16[32,144,128]{2,1,0:T(8,128)(2,1)S(1)}, u32[]{:S(2)}, u32[]{:S(2)}) async-start(bf16[32,144,128]{2,1,0:T(8,128)(2,1)} %shard_map.65), calls=%async_computation | async-start | bytes 2359296 | tf_op jit(solution)/shard_map/all_to_all | solution.py:282
  31.8 14.0 %collective-permute-start.9 = (bf16[4,3,2,64,128]{4,3,1,2,0:T(8,128)(2,1)S(1)}, bf16[4,3,2,64,128]{4,3,1,2,0:T(8,128)(2,1)S(1)}, u32[]{:S(2)}, u32[]{:S(2)}) collective-permute-start(bf16[4,3,2,64,128]{4,3,1,2,0:T(8,128)(2,1)S(1)} %pad_maximum_fusion), channel_id=1, source_target_pairs={{0,3},{1,2},{2,1},{3,0},{4,7},{5,6},{6,5},{7,4},{8,11},{9,10},{10,... | collective-permute-start | bytes 1179656 | tf_op jit(solution)/shard_map/ppermute | solution.py:265
  39.6 8.5 %collective-permute-start.11 = (bf16[4,3,2,64,128]{4,3,2,1,0:T(8,128)(2,1)S(1)}, bf16[4,3,2,64,128]{4,3,2,1,0:T(8,128)(2,1)S(1)}, u32[]{:S(2)}, u32[]{:S(2)}) collective-permute-start(bf16[4,3,2,64,128]{4,3,2,1,0:T(8,128)(2,1)S(1)} %pad_maximum_fusion.1.refs_4_), channel_id=1, source_target_pairs={{0,1},{1,0},{2,3},{3,2},{4,5},{5,4},{6,7},{7,6},{8,9},{9,8},{10,11... | collective-permute-start | bytes 1179656 | tf_op jit(solution)/shard_map/ppermute | solution.py:265
  39.7 15.7 %collective-permute-start.8 = (bf16[4,3,2,64,128]{4,3,1,2,0:T(8,128)(2,1)S(1)}, bf16[4,3,2,64,128]{4,3,1,2,0:T(8,128)(2,1)S(1)}, u32[]{:S(2)}, u32[]{:S(2)}) collective-permute-start(bf16[4,3,2,64,128]{4,3,1,2,0:T(8,128)(2,1)S(1)} %pad_maximum_fusion), channel_id=1, source_target_pairs={{0,1},{1,0},{2,3},{3,2},{4,5},{5,4},{6,7},{7,6},{8,9},{9,8},{10,11... | collective-permute-start | bytes 1179656 | tf_op jit(solution)/shard_map/ppermute | solution.py:265
  45.8 18.0 %collective-permute-start.10 = (bf16[4,3,2,64,128]{4,3,1,2,0:T(8,128)(2,1)S(1)}, bf16[4,3,2,64,128]{4,3,1,2,0:T(8,128)(2,1)S(1)}, u32[]{:S(2)}, u32[]{:S(2)}) collective-permute-start(bf16[4,3,2,64,128]{4,3,1,2,0:T(8,128)(2,1)S(1)} %collective-permute-done.9), channel_id=1, source_target_pairs={{0,1},{1,0},{2,3},{3,2},{4,5},{5,4},{6,7},{7,6},{8,9},{9,8},{10,11... | collective-permute-start | bytes 1179656 | tf_op jit(solution)/shard_map/ppermute | solution.py:265
  45.8 18.5 %collective-permute-start.13 = (bf16[4,3,2,64,128]{4,3,2,1,0:T(8,128)(2,1)S(1)}, bf16[4,3,2,64,128]{4,3,2,1,0:T(8,128)(2,1)}, u32[]{:S(2)}, u32[]{:S(2)}) collective-permute-start(bf16[4,3,2,64,128]{4,3,2,1,0:T(8,128)(2,1)S(1)} %pad_maximum_fusion.1.refs_4_), channel_id=1, source_target_pairs={{0,3},{1,2},{2,1},{3,0},{4,7},{5,6},{6,5},{7,4},{8,11},{9,10},{10,... | collective-permute-start | bytes 1179656 | tf_op jit(solution)/shard_map/ppermute | solution.py:265
  48.2 16.1 %collective-permute-start.12 = (bf16[4,3,2,64,128]{4,3,2,1,0:T(8,128)(2,1)S(1)}, bf16[4,3,2,64,128]{4,3,2,1,0:T(8,128)(2,1)}, u32[]{:S(2)}, u32[]{:S(2)}) collective-permute-start(bf16[4,3,2,64,128]{4,3,2,1,0:T(8,128)(2,1)S(1)} %collective-permute-done.11.refs_5_), channel_id=1, source_target_pairs={{0,3},{1,2},{2,1},{3,0},{4,7},{5,6},{6,5},{7,4},{8,11},{9,10},{10,... | collective-permute-start | bytes 1179656 | tf_op jit(solution)/shard_map/ppermute | solution.py:265
  64.3 9.6 %copy-start = (bf16[128,64]{0,1:T(8,128)(2,1)S(1)}, bf16[128,64]{0,1:T(8,128)(2,1)}, u32[]{:S(2)}) copy-start(bf16[128,64]{0,1:T(8,128)(2,1)} %param.11) | copy-start | bytes 49156
  67.2 6.8 %collective-permute-start.14 = (bf16[4352,128]{1,0:T(8,128)(2,1)S(1)}, bf16[4352,128]{1,0:T(8,128)(2,1)S(1)}, u32[]{:S(2)}, u32[]{:S(2)}) collective-permute-start(bf16[4352,128]{1,0:T(8,128)(2,1)S(1)} %get-tuple-element.36), channel_id=1, source_target_pairs={{0,4},{4,0},{8,12},{12,8},{16,20},{20,16},{24,28},{28,24},{32,36},... | collective-permute-start | bytes 3342344 | tf_op jit(solution)/shard_map/ppermute | solution.py:258
